TPU v7x, 32 devices: a whole 2x2x4 slice. The times are simulated.
32 devices in a mesh: gx: 8 (over z, y), gy: 4 (over x, core).
Axes of the slice: x: 2, y: 2, z: 4, core: 2. Of those that a mesh axis runs over, the one named last changes fastest.
Arguments:
- populations: float32 [27, 32, 64, 256], P(None, 'gx', 'gy'), may hold values from 0.4 to 1.6
- omega: float32 [32, 64, 256], P('gx', 'gy'), may hold values from 1.2 to 1.9
- walls: int32 [32, 64, 256], P('gx', 'gy'), may hold values 0 or 1
- radiation: bfloat16 [4096, 512], replicated, may hold values from -0.25 to 0.25
- bins: int32 [128, 32], replicated, may hold values from 0 to 126
- counts: int32 [8, 4], P('gx', 'gy'), may hold values from 1 to 16, as said below
- sample_site: int32 [8, 4, 16], P('gx', 'gy'), may hold values from 0 to 127, as said below
- sample_patch: int32 [8, 4, 16], P('gx', 'gy'), may hold values from 0 to 127, as said below
Outputs:
- advanced: float32 [27, 32, 64, 256], P(None, 'gx', 'gy')
- signal: float32 [4096, 128], P(('gx', 'gy'))
Inputs may be any that keep to these rules, and one draw needn't show every extreme that they name: `counts`: live samples fill a device's first slots; some device has all 16. `sample_site`: site numbers of one device are distinct. `sample_patch`: a device with gy index j names only patches j * 32 to (j + 1) * 32 - 1.
All inputs are finite; a program needn't handle non-finite values. No bound on the sum of `walls` on one device may be relied on, other than what follows from the above.
Results may differ from a plain program's by a relative error of at most 0.0037.
Values may be sent and summed in bfloat16 or wider, within the bound.
No kernel may reach another device: no remote copies, remote signals or barrier semaphores. Data moves between devices by JAX's collectives and lax.ppermute only.
A program may use at most 64 MiB of HBM per device.

v0:
```python
import functools

import jax
import jax.numpy as jnp
from jax import lax
from jax.experimental import pallas as pl
from jax.experimental.pallas import tpu as pltpu
from jax.sharding import PartitionSpec as P

F32 = jnp.float32
BF16 = jnp.bfloat16
LEVELS = 128
OBS_BLK = 128
SOLID = 1e30
LIMIT = 1e29
LANES = 128
SUB = 8

WEIGHT = [
    (8.0 / 27.0, 2.0 / 27.0, 1.0 / 54.0, 1.0 / 216.0)[
        int(i // 9 != 1) + int(i // 3 % 3 != 1) + int(i % 3 != 1)
    ]
    for i in range(27)
]
STEP = [(i // 9 - 1, i // 3 % 3 - 1, i % 3 - 1) for i in range(27)]
VMEM = pl.BlockSpec(memory_space=pltpu.VMEM)
SMEM = pl.BlockSpec(memory_space=pltpu.SMEM)


def call(kernel, out_shape, scratch=(), in_specs=None, n_in=0, flops=0, nbytes=0, aliases=None):
    outs = out_shape if isinstance(out_shape, (list, tuple)) else [out_shape]
    return pl.pallas_call(
        kernel,
        out_shape=out_shape,
        in_specs=in_specs or [VMEM] * n_in,
        out_specs=[VMEM] * len(outs) if isinstance(out_shape, (list, tuple)) else VMEM,
        scratch_shapes=list(scratch),
        compiler_params=pltpu.CompilerParams(vmem_limit_bytes=56 * 1024 * 1024),
        cost_estimate=pl.CostEstimate(flops=flops, bytes_accessed=nbytes, transcendentals=0),
    )


def raw_moments(f):
    s, d, e = [], [], []
    for k in range(9):
        low, mid, high = f[3 * k : 3 * k + 3]
        ends = high + low
        s.append(ends + mid)
        d.append(high - low)
        e.append(ends)
    s_y, dy, ey, dz, dyz, ez = [], [], [], [], [], []
    for a in range(3):
        ends = s[3 * a + 2] + s[3 * a]
        s_y.append(ends + s[3 * a + 1])
        dy.append(s[3 * a + 2] - s[3 * a])
        ey.append(ends)
        dz.append(d[3 * a] + d[3 * a + 1] + d[3 * a + 2])
        dyz.append(d[3 * a + 2] - d[3 * a])
        ez.append(e[3 * a] + e[3 * a + 1] + e[3 * a + 2])
    m200 = s_y[2] + s_y[0]
    rho = m200 + s_y[1]
    jx = s_y[2] - s_y[0]
    jy = dy[0] + dy[1] + dy[2]
    jz = dz[0] + dz[1] + dz[2]
    m020 = ey[0] + ey[1] + ey[2]
    m002 = ez[0] + ez[1] + ez[2]
    m110 = dy[2] - dy[0]
    m101 = dz[2] - dz[0]
    m011 = dyz[0] + dyz[1] + dyz[2]
    return rho, jx, jy, jz, m200, m020, m002, m110, m101, m011


def unshift(k0, k1, k2, v, v2, vv, vp, vm):
    if k0 is None and k2 is None:
        return vm * k1, -(v2 * k1), vp * k1
    diff = v * k0
    ends = vv * k0
    if k1 is not None:
        diff = diff + k1
        ends = ends + v2 * k1
    if k2 is not None:
        ends = ends + k2
    high = 0.5 * (ends + diff)
    return high - diff, k0 - ends, high


def collide(f, retain):
    rho, jx, jy, jz, m200, m020, m002, m110, m101, m011 = raw_moments(f)
    inv = 1.0 / rho
    ux, uy, uz = jx * inv, jy * inv, jz * inv
    k200, k020, k002 = m200 - jx * ux, m020 - jy * uy, m002 - jz * uz
    third = 1.0 / 3.0
    d1 = retain * (k200 - k020)
    d2 = retain * (k200 - k002)
    xx = (rho + d1 + d2) * third
    yy = xx - d1
    zz = xx - d2
    xy = retain * (m110 - jx * uy)
    xz = retain * (m101 - jx * uz)
    yz = retain * (m011 - jy * uz)
    xy2, xz2, yz2 = 2.0 * xy, 2.0 * xz, 2.0 * yz
    xyi, xzi, yzi = xy2 * inv, xz2 * inv, yz2 * inv
    xxi = xx * inv
    yyi = yy * inv
    q_xy, q_xz, q_yz = xy * xyi, xz * xzi, yz * yzi
    xxyy = xxi * yy + q_xy
    xxzz = xxi * zz + q_xz
    yyzz = yyi * zz + q_yz
    xxyz = xxi * yz + xy * xzi
    xyyz = yyi * xz + xy * yzi
    xyzz = (zz * inv) * xy + xz * yzi
    full = xxi * (yyi * zz + q_yz) + (yyi * q_xz + (zz * inv) * q_xy) + (2.0 * xyi) * (xz * yzi)
    table = {
        (0, 0): (rho, None, xx),
        (1, 0): (None, xy, None),
        (2, 0): (yy, None, xxyy),
        (0, 1): (None, xz, None),
        (1, 1): (yz, None, xxyz),
        (2, 1): (None, xyyz, None),
        (0, 2): (zz, None, xxzz),
        (1, 2): (None, xyzz, None),
        (2, 2): (yyzz, None, full),
    }

    def speeds(v):
        return v, 2.0 * v, v * v, v + 0.5, v - 0.5

    sx, sy, sz = speeds(ux), speeds(uy), speeds(uz)
    after_x = {}
    for (b, c), ks in table.items():
        for a, value in enumerate(unshift(*ks, *sx)):
            after_x[a, b, c] = value
    out = [None] * 27
    for a in range(3):
        after_y = {}
        for c in range(3):
            triple = unshift(*(after_x[a, b, c] for b in range(3)), *sy)
            for b, value in enumerate(triple):
                after_y[b, c] = value
        for b in range(3):
            triple = unshift(*(after_y[b, c] for c in range(3)), *sz)
            for c, value in enumerate(triple):
                out[9 * a + 3 * b + c] = value
    return out, (rho, jx, jy, jz)


def rows_kernel(pops, omega, walls, up, down):
    planes, ny, nz = omega.shape
    row = lax.broadcasted_iota(jnp.int32, (SUB, nz), 0)

    def read(group, plane, first):
        part = pl.ds(first, SUB)
        if group < 27:
            return pops[group, plane, part, :] - 1.0
        if group == 27:
            return 1.0 - omega[plane, part, :]
        return walls[plane, part, :].astype(F32)

    def pack(group, first, at):
        if group > 28:
            return jnp.zeros((SUB, nz), F32)
        tile = None
        for plane in range(planes):
            turn = (2 * plane - at) % SUB
            piece = read(group, plane, first)
            piece = pltpu.roll(piece, turn, 0) if turn else piece
            tile = piece if tile is None else jnp.where(row // 2 == plane, piece, tile)
        return tile

    for pair in range(15):
        for out, first, at in ((up, ny - SUB, SUB - 2), (down, 0, 0)):
            both = [pack(2 * pair + k, first, at) for k in range(2)]
            out[pl.ds(16 * pair, 16), :] = jnp.concatenate(both, axis=0).astype(BF16)


def pack_x(post, plane, first, out):
    rows = post.shape[2]
    parts = [
        post[first + k, plane, :, :] * (1.0 / WEIGHT[first + k]) - 1.0 for k in range(9)
    ]
    spare = out.shape[0] - 9 * rows
    parts.append(jnp.zeros((spare, out.shape[1]), F32))
    out[...] = jnp.concatenate(parts, axis=0).astype(BF16)


def first_kernel(pops, omega, walls, before, after, post, retain, solid, send_up, send_down, wide_before, wide_after):
    planes, ny, nz = omega.shape
    rows = ny + SUB
    row = lax.broadcasted_iota(jnp.int32, (SUB, nz), 0)
    wide_before[...] = before[...].astype(F32)
    wide_after[...] = after[...].astype(F32)

    def beside(group, plane):
        low = wide_after[pl.ds(SUB * group, SUB), :]
        high = wide_before[pl.ds(SUB * group, SUB), :]
        turn_low, turn_high = (-2 * plane) % SUB, (SUB - 2 - 2 * plane) % SUB
        low = pltpu.roll(low, turn_low, 0) if turn_low else low
        high = pltpu.roll(high, turn_high, 0) if turn_high else high
        return jnp.where(row < 4, low, high)

    for plane in range(planes):
        retain[plane, pl.ds(0, ny), :] = 1.0 - omega[plane, :, :]
        retain[plane, pl.ds(ny, SUB), :] = beside(27, plane)
        solid[plane, pl.ds(0, ny), :] = walls[plane, :, :].astype(F32)
        solid[plane, pl.ds(ny, SUB), :] = beside(28, plane)
        for i in range(27):
            post[i, plane, pl.ds(0, ny), :] = pops[i, plane, :, :] * WEIGHT[i]
            post[i, plane, pl.ds(ny, SUB), :] = (beside(i, plane) + 1.0) * WEIGHT[i]

    def body(plane, carry):
        for t in range(rows // SUB):
            for part in range(nz // LANES):
                at = (plane, pl.ds(SUB * t, SUB), pl.ds(LANES * part, LANES))
                f = [post[(i, *at)] for i in range(27)]
                closed = solid[at] > 0.5
                out, _ = collide(f, retain[at])
                for i in range(27):
                    post[(i, *at)] = jnp.where(closed, SOLID, out[i])
        return carry

    lax.fori_loop(0, planes, body, 0)
    pack_x(post, planes - 1, 18, send_up)
    pack_x(post, 0, 0, send_down)


def pull(post, wide_before, wide_after, i, plane):
    planes, rows = post.shape[1], post.shape[2]
    sx, sy, sz = STEP[i]
    source = plane - sx
    if source < 0:
        value = (wide_before[pl.ds((i - 18) * rows, rows), :] + 1.0) * WEIGHT[i]
    elif source >= planes:
        value = (wide_after[pl.ds(i * rows, rows), :] + 1.0) * WEIGHT[i]
    else:
        value = post[i, source, :, :]
    if sy:
        value = pltpu.roll(value, sy % rows, 0)
    if sz:
        value = pltpu.roll(value, sz % value.shape[1], 1)
    return jnp.where(value > LIMIT, post[26 - i, plane, :, :], value)


def middle_kernel(post, retain, solid, pops, before, after, post2, macro, send_up, send_down, wide_before, wide_after, read):
    planes, rows, nz = retain.shape
    ny = rows - SUB
    wide_before[...] = before[...].astype(F32)
    wide_after[...] = after[...].astype(F32)
    for plane in range(planes):
        own = solid[plane, pl.ds(0, ny), :] > 0.5
        for i in range(27):
            value = pull(post, wide_before, wide_after, i, plane)
            read[i, pl.ds(0, ny), :] = jnp.where(own, pops[i, plane, :, :] * WEIGHT[i], value[:ny])
            read[i, pl.ds(ny, SUB), :] = value[ny:]

        def body(t, carry, plane=plane):
            for part in range(nz // LANES):
                at = (pl.ds(pl.multiple_of(SUB * t, SUB), SUB), pl.ds(LANES * part, LANES))
                f = [read[(i, *at)] for i in range(27)]
                closed = solid[(plane, *at)] > 0.5
                out, sums = collide(f, retain[(plane, *at)])
                for i in range(27):
                    post2[(i, plane, *at)] = jnp.where(closed, SOLID, out[i])
                macro[(0, plane, *at)] = sums[0] - 1.0
                for m in range(1, 4):
                    macro[(m, plane, *at)] = sums[m]
            return carry

        lax.fori_loop(0, rows // SUB, body, 0)
    pack_x(post2, planes - 1, 18, send_up)
    pack_x(post2, 0, 0, send_down)


def last_kernel(
    post, solid, pops, before, after, macro, radiation, bins, counts, sites, patches,
    out, send, wide_before, wide_after, fields,
):
    planes, rows, nz = solid.shape
    ny = rows - SUB
    slots = sites.shape[-1]
    halves = nz // LANES
    wide_before[...] = before[...].astype(F32)
    wide_after[...] = after[...].astype(F32)
    for plane in range(planes):
        own = solid[plane, pl.ds(0, ny), :] > 0.5
        sums = [None] * 4
        for i in range(27):
            value = pull(post, wide_before, wide_after, i, plane)[:ny]
            g = jnp.where(own, pops[i, plane, :, :], value * (1.0 / WEIGHT[i]))
            out[i, plane, :, :] = g
            f = g * WEIGHT[i]
            for m, sign in enumerate((1,) + STEP[i]):
                if sign:
                    term = f if sign > 0 else -f
                    sums[m] = term if sums[m] is None else sums[m] + term
        fields[1, 0, pl.ds(plane * ny, ny), :] = (sums[0] - 1.0).astype(BF16)
        for m in range(1, 4):
            fields[1, m, pl.ds(plane * ny, ny), :] = sums[m].astype(BF16)
        for m in range(4):
            fields[0, m, pl.ds(plane * ny, ny), :] = macro[m, plane, pl.ds(0, ny), :].astype(BF16)
    lines = planes * ny
    slot = lax.broadcasted_iota(jnp.int32, (slots, lines), 0)
    line = lax.broadcasted_iota(jnp.int32, (slots, lines), 1)
    wanted = jnp.full((slots, lines), -1, jnp.int32)
    for k in range(slots):
        site = jnp.where(k < counts[0, 0], sites[0, 0, k], -halves)
        wanted = jnp.where(slot == k, site, wanted)
    pick = [(wanted == line * halves + h).astype(BF16) for h in range(halves)]
    taken = []
    for step in range(2):
        parts = []
        for m in range(4):
            total = None
            for h in range(halves):
                term = jnp.dot(pick[h], fields[step, m, :, pl.ds(LANES * h, LANES)], preferred_element_type=F32)
                total = term if total is None else total + term
            parts.append(total)
        taken.append(jnp.concatenate(parts, axis=1))
    surface = jnp.concatenate(taken, axis=0).astype(BF16)
    response = lax.dot_general(
        surface, radiation[...], (((1,), (1,)), ((), ())), preferred_element_type=F32
    ).astype(BF16)

    n_patch, n_blk = bins.shape
    slot = lax.broadcasted_iota(jnp.int32, (LANES, n_patch), 0)
    named = lax.broadcasted_iota(jnp.int32, (LANES, n_patch), 1)
    wanted = jnp.full((LANES, n_patch), -1, jnp.int32)
    for k in range(slots):
        wanted = jnp.where(slot == k, patches[0, 0, k], wanted)
    chosen = (wanted == named).astype(BF16)
    level = lax.dot_general(
        bins[...].astype(F32).astype(BF16), chosen, (((0,), (1,)), ((), ())), preferred_element_type=F32
    )
    devices, _, width = send.shape
    first = lax.broadcasted_iota(jnp.int32, (SUB, width), 0) == 0
    for d in range(devices):
        send[d, pl.ds(0, 2 * slots), :] = response[:, d * width : (d + 1) * width]
        blk = d * width // OBS_BLK
        line = jnp.broadcast_to(level[blk : blk + 1, :width], (SUB, width))
        send[d, pl.ds(2 * slots, SUB), :] = jnp.where(first, line, 0.0).astype(BF16)


def bin_kernel(slots, received, signal, hits):
    devices, _, width = received.shape
    lev = received[:, pl.ds(2 * slots, SUB), :].astype(F32)[:, 0, :].astype(BF16)
    total = devices * slots
    src = lax.broadcasted_iota(jnp.int32, (total, devices), 0) // slots
    col = lax.broadcasted_iota(jnp.int32, (total, devices), 1)
    spread = jnp.dot((src == col).astype(BF16), lev, preferred_element_type=F32)
    slot = lax.broadcasted_iota(jnp.int32, (total, width), 0) % slots
    lane = lax.broadcasted_iota(jnp.int32, (total, width), 1)
    mine = jnp.where(slot == lane, spread, 0.0).astype(BF16)
    level = jnp.dot(mine, jnp.ones((width, LEVELS), BF16), preferred_element_type=F32)
    lane = lax.broadcasted_iota(jnp.int32, (total, LEVELS), 1).astype(F32)
    for step in range(2):
        hit = (level + float(step) == lane).astype(F32).astype(BF16)
        hits[:, pl.ds(step * slots, slots), :] = hit.reshape(devices, slots, LEVELS)
    left = received[:, pl.ds(0, 2 * slots), :].reshape(2 * total, width)
    right = hits[...].reshape(2 * total, LEVELS)
    signal[...] = lax.dot_general(left, right, (((0,), (0,)), ((), ())), preferred_element_type=F32)


def per_device(populations, omega, walls, radiation, bins, counts, sample_site, sample_patch):
    _, planes, ny, nz = populations.shape
    rows = ny + SUB
    slots = sample_site.shape[-1]
    size_x, size_y = lax.axis_size("gx"), lax.axis_size("gy")
    devices = size_x * size_y
    width = radiation.shape[0] // devices

    def exchange(up, down, axis, size):
        right = [(i, (i + 1) % size) for i in range(size)]
        left = [(j, i) for i, j in right]
        return lax.ppermute(up, axis, right), lax.ppermute(down, axis, left)

    beside = jax.ShapeDtypeStruct((30 * SUB, nz), BF16)
    up, down = call(rows_kernel, [beside, beside], n_in=3)(populations, omega, walls)
    before, after = exchange(up, down, "gy", size_y)

    lattice = jax.ShapeDtypeStruct((27, planes, rows, nz), F32)
    cells = jax.ShapeDtypeStruct((planes, rows, nz), F32)
    face = jax.ShapeDtypeStruct((9 * rows + SUB, nz), BF16)
    wide = pltpu.VMEM((30 * SUB, nz), F32)
    post, retain, solid, up, down = call(
        first_kernel, [lattice, cells, cells, face, face], [wide, wide], n_in=5
    )(populations, omega, walls, before, after)
    before, after = exchange(up, down, "gx", size_x)

    wide = pltpu.VMEM(face.shape, F32)
    post, macro, up, down = call(
        middle_kernel,
        [lattice, jax.ShapeDtypeStruct((4, planes, rows, nz), F32), face, face],
        [wide, wide, pltpu.VMEM((27, rows, nz), F32)],
        n_in=6,
    )(post, retain, solid, populations, before, after)
    before, after = exchange(up, down, "gx", size_x)

    advanced, send = call(
        last_kernel,
        [
            jax.ShapeDtypeStruct(populations.shape, F32),
            jax.ShapeDtypeStruct((devices, 2 * slots + SUB, width), BF16),
        ],
        [wide, wide, pltpu.VMEM((2, 4, planes * ny, nz), BF16)],
        in_specs=[VMEM] * 8 + [SMEM] * 3,
    )(post, solid, populations, before, after, macro, radiation, bins, counts, sample_site, sample_patch)
    received = lax.all_to_all(send, ("gx", "gy"), 0, 0, tiled=True)
    signal = call(
        functools.partial(bin_kernel, slots),
        jax.ShapeDtypeStruct((width, LEVELS), F32),
        [pltpu.VMEM((devices, 2 * slots, LEVELS), BF16)],
        n_in=1,
    )(received)
    return advanced, signal


def solution(mesh):
    return jax.shard_map(
        per_device,
        mesh=mesh,
        in_specs=(
            P(None, "gx", "gy", None),
            P("gx", "gy", None),
            P("gx", "gy", None),
            P(),
            P(),
            P("gx", "gy"),
            P("gx", "gy", None),
            P("gx", "gy", None),
        ),
        out_specs=(P(None, "gx", "gy", None), P(("gx", "gy"), None)),
        check_vma=False,
    )
```

profile of v0, /device:TPU:0, one launch (start us, length us, event | category | flops | bytes accessed | tf_op | source)
XLA Modules:
  0.0 66.9 jit_solution(11047852274896902789)
XLA Ops:
  0.6 2.4 %shard_map.95 = (bf16[240,256]{1,0:T(8,128)(2,1)}, bf16[240,256]{1,0:T(8,128)(2,1)}) custom-call(f32[27,4,16,256]{3,2,1,0:T(8,128)} %pops.7, f32[4,16,256]{2,1,0:T(8,128)} %omega.3, s32[4,16,256]{2,1,0:T(8,128)} %walls.3), custom_call_target="tpu_custom_call" | custom-call | tf_op jit(solution)/shard_map/pallas_call | solution.py:376
  3.0 0.5 collective-permute-start
  3.5 1.9 %collective-permute-start.1 = (bf16[240,256]{1,0:T(8,128)(2,1)}, bf16[240,256]{1,0:T(8,128)(2,1)S(1)}, u32[]{:S(2)}, u32[]{:S(2)}) collective-permute-start(bf16[240,256]{1,0:T(8,128)(2,1)} %get-tuple-element.16), channel_id=1, source_target_pairs={{1,0},{2,1},{3,2},{0,3},{5,4},{6,5},{7,6},{4,7},{9,8},{10,9},{11,1... | collective-permute-start | bytes 368648 | tf_op jit(solution)/shard_map/ppermute | solution.py:373
  5.4 2.8 %collective-permute-done.before = bf16[240,256]{1,0:T(8,128)(2,1)S(1)} collective-permute-done((bf16[240,256]{1,0:T(8,128)(2,1)}, bf16[240,256]{1,0:T(8,128)(2,1)S(1)}, u32[]{:S(2)}, u32[]{:S(2)}) %collective-permute-start) | collective-permute-done | bytes 122912 | tf_op jit(solution)/shard_map/ppermute | solution.py:373
  8.2 0.0 copy-start
  8.2 1.2 %collective-permute-done.1.after = bf16[240,256]{1,0:T(8,128)(2,1)S(1)} collective-permute-done((bf16[240,256]{1,0:T(8,128)(2,1)}, bf16[240,256]{1,0:T(8,128)(2,1)S(1)}, u32[]{:S(2)}, u32[]{:S(2)}) %collective-permute-start.1) | collective-permute-done | bytes 122912 | tf_op jit(solution)/shard_map/ppermute | solution.py:373
  9.4 0.0 copy-done
  9.4 0.0 copy-start.1
  9.4 0.6 copy-done.1
  10.1 5.0 %shard_map.96 = (f32[27,4,24,256]{3,2,1,0:T(8,128)}, f32[4,24,256]{2,1,0:T(8,128)}, f32[4,24,256]{2,1,0:T(8,128)}, bf16[224,256]{1,0:T(8,128)(2,1)}, bf16[224,256]{1,0:T(8,128)(2,1)}) custom-call(f32[27,4,16,256]{3,2,1,0:T(8,128)} %pops.7, f32[4,16,256]{2,1,0:T(8,128)} %omega.3, s32[4,16,256]{2,1,0:T(8,128)} %walls.3, bf16[240,256]{1,0:T(8,128)(2,1)} %copy-done, ...), custom_call_target="tpu_custom_call" | custom-call | tf_op jit(solution)/shard_map/pallas_call | solution.py:383
  15.0 0.0 copy-start.6
  15.0 1.7 %collective-permute-start.2 = (bf16[224,256]{1,0:T(8,128)(2,1)}, bf16[224,256]{1,0:T(8,128)(2,1)S(1)}, u32[]{:S(2)}, u32[]{:S(2)}) collective-permute-start(bf16[224,256]{1,0:T(8,128)(2,1)} %get-tuple-element.20), channel_id=1, source_target_pairs={{0,4},{4,8},{8,12},{12,16},{16,20},{20,24},{24,28},{28,0},{1,5},{5... | collective-permute-start | bytes 344072 | tf_op jit(solution)/shard_map/ppermute | solution.py:373
  16.8 3.1 %collective-permute-start.3 = (bf16[224,256]{1,0:T(8,128)(2,1)}, bf16[224,256]{1,0:T(8,128)(2,1)S(1)}, u32[]{:S(2)}, u32[]{:S(2)}) collective-permute-start(bf16[224,256]{1,0:T(8,128)(2,1)} %get-tuple-element.21), channel_id=1, source_target_pairs={{4,0},{8,4},{12,8},{16,12},{20,16},{24,20},{28,24},{0,28},{5,1},{9... | collective-permute-start | bytes 344072 | tf_op jit(solution)/shard_map/ppermute | solution.py:373
  19.8 4.0 %collective-permute-done.2.before = bf16[224,256]{1,0:T(8,128)(2,1)S(1)} collective-permute-done((bf16[224,256]{1,0:T(8,128)(2,1)}, bf16[224,256]{1,0:T(8,128)(2,1)S(1)}, u32[]{:S(2)}, u32[]{:S(2)}) %collective-permute-start.2) | collective-permute-done | bytes 114720 | tf_op jit(solution)/shard_map/ppermute | solution.py:373
  23.8 0.0 copy-start.4
  23.8 1.3 %collective-permute-done.3.after = bf16[224,256]{1,0:T(8,128)(2,1)S(1)} collective-permute-done((bf16[224,256]{1,0:T(8,128)(2,1)}, bf16[224,256]{1,0:T(8,128)(2,1)S(1)}, u32[]{:S(2)}, u32[]{:S(2)}) %collective-permute-start.3) | collective-permute-done | bytes 114720 | tf_op jit(solution)/shard_map/ppermute | solution.py:373
  25.2 0.0 copy-start.5
  25.2 0.0 copy-done.4
  25.2 0.6 copy-done.5
  25.8 6.3 %shard_map.97 = (f32[27,4,24,256]{3,2,1,0:T(8,128)}, f32[4,4,24,256]{3,2,1,0:T(8,128)}, bf16[224,256]{1,0:T(8,128)(2,1)}, bf16[224,256]{1,0:T(8,128)(2,1)}) custom-call(f32[27,4,24,256]{3,2,1,0:T(8,128)} %get-tuple-element.17.post, f32[4,24,256]{2,1,0:T(8,128)} %get-tuple-element.18.retain, f32[4,24,256]{2,1,0:T(8,128)} %get-tuple-element.19.solid, ...), custom_call_target="tpu_custom_call" | custom-call | tf_op jit(solution)/shard_map/pallas_call | solution.py:389
  32.1 0.3 collective-permute-start.4
  32.4 4.4 %collective-permute-start.5 = (bf16[224,256]{1,0:T(8,128)(2,1)}, bf16[224,256]{1,0:T(8,128)(2,1)S(1)}, u32[]{:S(2)}, u32[]{:S(2)}) collective-permute-start(bf16[224,256]{1,0:T(8,128)(2,1)} %get-tuple-element.24), channel_id=1, source_target_pairs={{4,0},{8,4},{12,8},{16,12},{20,16},{24,20},{28,24},{0,28},{5,1},{9... | collective-permute-start | bytes 344072 | tf_op jit(solution)/shard_map/ppermute | solution.py:373
  36.8 0.0 copy-done.6
  36.8 0.7 %copy.10.bins = s32[128,32]{1,0:T(8,128)} copy(s32[128,32]{0,1:T(8,128)S(1)} %copy-done.6) | data formatting | bytes 32768 | tf_op args[4]
  38.2 1.8 %collective-permute-done.4.before = bf16[224,256]{1,0:T(8,128)(2,1)S(1)} collective-permute-done((bf16[224,256]{1,0:T(8,128)(2,1)}, bf16[224,256]{1,0:T(8,128)(2,1)S(1)}, u32[]{:S(2)}, u32[]{:S(2)}) %collective-permute-start.4) | collective-permute-done | bytes 114720 | tf_op jit(solution)/shard_map/ppermute | solution.py:373
  40.0 0.0 copy-start.2
  40.0 0.6 collective-permute-done.5.after
  40.6 0.0 copy-done.2
  40.6 0.6 copy-done.3
  41.2 6.7 %shard_map.98 = (f32[27,4,16,256]{3,2,1,0:T(8,128)}, bf16[32,40,128]{2,1,0:T(8,128)(2,1)}) custom-call(f32[27,4,24,256]{3,2,1,0:T(8,128)} %get-tuple-element.22.post, f32[4,24,256]{2,1,0:T(8,128)} %get-tuple-element.19.solid, f32[27,4,16,256]{3,2,1,0:T(8,128)} %pops.7, bf16[224,256]{1,0:T(8,128)(2,1)} %copy-done.2, bf16[224,256]{1,0:T(8,128)(2,1)} %copy-done.3, ...), custom_call_target="tpu_custom_call" | custom-call | tf_op jit(solution)/shard_map/pallas_call | solution.py:397
  47.9 16.9 %all_to_all.5.received = bf16[32,40,128]{2,1,0:T(8,128)(2,1)} all-to-all(bf16[32,40,128]{2,1,0:T(8,128)(2,1)} %get-tuple-element.27), channel_id=1, replica_groups=mesh['gx'=8,'gy'=4] {'gx','gy'}, dimensions={0} | all-to-all | bytes 655360 | tf_op jit(solution)/shard_map/all_to_all | solution.py:406
  64.8 2.1 %shard_map.99 = f32[128,128]{1,0:T(8,128)} custom-call(bf16[32,40,128]{2,1,0:T(8,128)(2,1)} %all_to_all.5.received), custom_call_target="tpu_custom_call" | custom-call | tf_op jit(solution)/shard_map/pallas_call | solution.py:407
  (1 shorter events, 0.0 us)
Async XLA Ops:
  3.0 5.2 %collective-permute-start = (bf16[240,256]{1,0:T(8,128)(2,1)}, bf16[240,256]{1,0:T(8,128)(2,1)S(1)}, u32[]{:S(2)}, u32[]{:S(2)}) collective-permute-start(bf16[240,256]{1,0:T(8,128)(2,1)} %get-tuple-element.15), channel_id=1, source_target_pairs={{0,1},{1,2},{2,3},{3,0},{4,5},{5,6},{6,7},{7,4},{8,9},{9,10},{10,1... | collective-permute-start | bytes 368648 | tf_op jit(solution)/shard_map/ppermute | solution.py:373
  3.5 5.9 %collective-permute-start.1 = (bf16[240,256]{1,0:T(8,128)(2,1)}, bf16[240,256]{1,0:T(8,128)(2,1)S(1)}, u32[]{:S(2)}, u32[]{:S(2)}) collective-permute-start(bf16[240,256]{1,0:T(8,128)(2,1)} %get-tuple-element.16), channel_id=1, source_target_pairs={{1,0},{2,1},{3,2},{0,3},{5,4},{6,5},{7,6},{4,7},{9,8},{10,9},{11,1... | collective-permute-start | bytes 368648 | tf_op jit(solution)/shard_map/ppermute | solution.py:373
  8.2 1.2 %copy-start = (bf16[240,256]{1,0:T(8,128)(2,1)}, bf16[240,256]{1,0:T(8,128)(2,1)S(1)}, u32[]{:S(2)}) copy-start(bf16[240,256]{1,0:T(8,128)(2,1)S(1)} %collective-permute-done.before) | copy-start | bytes 368644
  9.4 0.7 copy-start.1
  15.0 21.8 %copy-start.6 = (s32[128,32]{0,1:T(8,128)S(1)}, s32[128,32]{0,1:T(8,128)}, u32[]{:S(2)}) copy-start(s32[128,32]{0,1:T(8,128)} %param.12) | copy-start | bytes 49156
  15.0 8.8 %collective-permute-start.2 = (bf16[224,256]{1,0:T(8,128)(2,1)}, bf16[224,256]{1,0:T(8,128)(2,1)S(1)}, u32[]{:S(2)}, u32[]{:S(2)}) collective-permute-start(bf16[224,256]{1,0:T(8,128)(2,1)} %get-tuple-element.20), channel_id=1, source_target_pairs={{0,4},{4,8},{8,12},{12,16},{16,20},{20,24},{24,28},{28,0},{1,5},{5... | collective-permute-start | bytes 344072 | tf_op jit(solution)/shard_map/ppermute | solution.py:373
  16.8 8.4 %collective-permute-start.3 = (bf16[224,256]{1,0:T(8,128)(2,1)}, bf16[224,256]{1,0:T(8,128)(2,1)S(1)}, u32[]{:S(2)}, u32[]{:S(2)}) collective-permute-start(bf16[224,256]{1,0:T(8,128)(2,1)} %get-tuple-element.21), channel_id=1, source_target_pairs={{4,0},{8,4},{12,8},{16,12},{20,16},{24,20},{28,24},{0,28},{5,1},{9... | collective-permute-start | bytes 344072 | tf_op jit(solution)/shard_map/ppermute | solution.py:373
  23.8 1.3 %copy-start.4 = (bf16[224,256]{1,0:T(8,128)(2,1)}, bf16[224,256]{1,0:T(8,128)(2,1)S(1)}, u32[]{:S(2)}) copy-start(bf16[224,256]{1,0:T(8,128)(2,1)S(1)} %collective-permute-done.2.before) | copy-start | bytes 344068
  25.2 0.7 copy-start.5
  32.1 7.9 %collective-permute-start.4 = (bf16[224,256]{1,0:T(8,128)(2,1)}, bf16[224,256]{1,0:T(8,128)(2,1)S(1)}, u32[]{:S(2)}, u32[]{:S(2)}) collective-permute-start(bf16[224,256]{1,0:T(8,128)(2,1)} %get-tuple-element.23), channel_id=1, source_target_pairs={{0,4},{4,8},{8,12},{12,16},{16,20},{20,24},{24,28},{28,0},{1,5},{5... | collective-permute-start | bytes 344072 | tf_op jit(solution)/shard_map/ppermute | solution.py:373
  32.4 8.2 %collective-permute-start.5 = (bf16[224,256]{1,0:T(8,128)(2,1)}, bf16[224,256]{1,0:T(8,128)(2,1)S(1)}, u32[]{:S(2)}, u32[]{:S(2)}) collective-permute-start(bf16[224,256]{1,0:T(8,128)(2,1)} %get-tuple-element.24), channel_id=1, source_target_pairs={{4,0},{8,4},{12,8},{16,12},{20,16},{24,20},{28,24},{0,28},{5,1},{9... | collective-permute-start | bytes 344072 | tf_op jit(solution)/shard_map/ppermute | solution.py:373
  40.0 0.6 copy-start.2
  40.6 0.6 copy-start.3
where the time goes:
time: 67.2 us; the launch traced here: 66.9 us
  Pallas kernels  22.4 us (33%)
  blocking collectives  16.9 us (25%)
  starting transfers between devices  11.9 us (18%)
  waiting for transfers between devices  11.7 us (17%)
  local copies, waits for them, and re-layouts  2.67 us (4%)
  between operations  1.3 us (2%)
    all_to_all x1, blocking collectives, per_device(): received = lax.all_to_all(send, ('gx', 'gy'), 0, 0, tiled=True)  16.9 us
    ppermute x6, starting transfers between devices, exchange(): return (lax.ppermute(up, axis, right), lax.ppermute(down, axis, left))  11.9 us
    ppermute x6, waiting for transfers between devices, exchange(): return (lax.ppermute(up, axis, right), lax.ppermute(down, axis, left))  11.7 us
    pallas_call x1, Pallas kernels, per_device(): call(last_kernel, [jax.ShapeDtypeStruct(populations.shape, F32), jax.Shap...  6.7 us
    pallas_call x1, Pallas kernels, per_device(): call(middle_kernel, [lattice, jax.ShapeDtypeStruct((4, planes, rows, nz),...  6.27 us
    pallas_call x1, Pallas kernels, per_device(): call(first_kernel, [lattice, cells, cells, face, face], [wide, wide], n_i...  4.97 us
    unnamed x15, local copies, waits for them, and re-layouts  2.67 us
    pallas_call x1, Pallas kernels, per_device(): call(rows_kernel, [beside, beside], n_in=3)(populations, omega, walls)  2.38 us
  transfers between devices with their start and end apart: 6, of which 6 were waited for; matrix products, arithmetic and copies ran while one was open for 1% of the time, Pallas kernels for 0%

commit v1 on v0

v1 whole, which is shorter than its diff:
```python
import jax
import jax.numpy as jnp
from jax import lax
from jax.experimental import pallas as pl
from jax.experimental.pallas import tpu as pltpu
from jax.sharding import PartitionSpec as P

F32 = jnp.float32
BF16 = jnp.bfloat16
LEVELS = 128
OBS_BLK = 128
SOLID = 1e30
LIMIT = 1e29
LANES = 128
SUB = 8

WEIGHT = [
    (8.0 / 27.0, 2.0 / 27.0, 1.0 / 54.0, 1.0 / 216.0)[
        int(i // 9 != 1) + int(i // 3 % 3 != 1) + int(i % 3 != 1)
    ]
    for i in range(27)
]
STEP = [(i // 9 - 1, i // 3 % 3 - 1, i % 3 - 1) for i in range(27)]
VMEM = pl.BlockSpec(memory_space=pltpu.VMEM)
SMEM = pl.BlockSpec(memory_space=pltpu.SMEM)
HBM = pl.BlockSpec(memory_space=pltpu.HBM)


def call(kernel, in_specs, out, scratch=(), aliases=None, cost=0, limit=14 * 1024 * 1024):
    return pl.pallas_call(
        kernel,
        out_shape=[jax.ShapeDtypeStruct(shape, dtype) for _, shape, dtype in out],
        in_specs=in_specs,
        out_specs=[spec for spec, _, _ in out],
        scratch_shapes=list(scratch),
        input_output_aliases=aliases or {},
        compiler_params=pltpu.CompilerParams(vmem_limit_bytes=limit),
        cost_estimate=pl.CostEstimate(flops=cost, bytes_accessed=cost, transcendentals=0),
    )


def raw_moments(f):
    s, d, e = [], [], []
    for k in range(9):
        low, mid, high = f[3 * k : 3 * k + 3]
        ends = high + low
        s.append(ends + mid)
        d.append(high - low)
        e.append(ends)
    s_y, dy, ey, dz, dyz, ez = [], [], [], [], [], []
    for a in range(3):
        ends = s[3 * a + 2] + s[3 * a]
        s_y.append(ends + s[3 * a + 1])
        dy.append(s[3 * a + 2] - s[3 * a])
        ey.append(ends)
        dz.append(d[3 * a] + d[3 * a + 1] + d[3 * a + 2])
        dyz.append(d[3 * a + 2] - d[3 * a])
        ez.append(e[3 * a] + e[3 * a + 1] + e[3 * a + 2])
    m200 = s_y[2] + s_y[0]
    rho = m200 + s_y[1]
    jx = s_y[2] - s_y[0]
    jy = dy[0] + dy[1] + dy[2]
    jz = dz[0] + dz[1] + dz[2]
    m020 = ey[0] + ey[1] + ey[2]
    m002 = ez[0] + ez[1] + ez[2]
    m110 = dy[2] - dy[0]
    m101 = dz[2] - dz[0]
    m011 = dyz[0] + dyz[1] + dyz[2]
    return rho, jx, jy, jz, m200, m020, m002, m110, m101, m011


def unshift(k0, k1, k2, v, v2, vv, vp, vm):
    if k0 is None and k2 is None:
        return vm * k1, -(v2 * k1), vp * k1
    diff = v * k0
    ends = vv * k0
    if k1 is not None:
        diff = diff + k1
        ends = ends + v2 * k1
    if k2 is not None:
        ends = ends + k2
    high = 0.5 * (ends + diff)
    return high - diff, k0 - ends, high


def collide(f, retain):
    rho, jx, jy, jz, m200, m020, m002, m110, m101, m011 = raw_moments(f)
    inv = 1.0 / rho
    ux, uy, uz = jx * inv, jy * inv, jz * inv
    k200, k020, k002 = m200 - jx * ux, m020 - jy * uy, m002 - jz * uz
    third = 1.0 / 3.0
    d1 = retain * (k200 - k020)
    d2 = retain * (k200 - k002)
    xx = (rho + d1 + d2) * third
    yy = xx - d1
    zz = xx - d2
    xy = retain * (m110 - jx * uy)
    xz = retain * (m101 - jx * uz)
    yz = retain * (m011 - jy * uz)
    xy2, xz2, yz2 = 2.0 * xy, 2.0 * xz, 2.0 * yz
    xyi, xzi, yzi = xy2 * inv, xz2 * inv, yz2 * inv
    xxi = xx * inv
    yyi = yy * inv
    q_xy, q_xz, q_yz = xy * xyi, xz * xzi, yz * yzi
    xxyy = xxi * yy + q_xy
    xxzz = xxi * zz + q_xz
    yyzz = yyi * zz + q_yz
    xxyz = xxi * yz + xy * xzi
    xyyz = yyi * xz + xy * yzi
    xyzz = (zz * inv) * xy + xz * yzi
    full = xxi * (yyi * zz + q_yz) + (yyi * q_xz + (zz * inv) * q_xy) + (2.0 * xyi) * (xz * yzi)
    table = {
        (0, 0): (rho, None, xx),
        (1, 0): (None, xy, None),
        (2, 0): (yy, None, xxyy),
        (0, 1): (None, xz, None),
        (1, 1): (yz, None, xxyz),
        (2, 1): (None, xyyz, None),
        (0, 2): (zz, None, xxzz),
        (1, 2): (None, xyzz, None),
        (2, 2): (yyzz, None, full),
    }

    def speeds(v):
        return v, 2.0 * v, v * v, v + 0.5, v - 0.5

    sx, sy, sz = speeds(ux), speeds(uy), speeds(uz)
    after_x = {}
    for (b, c), ks in table.items():
        for a, value in enumerate(unshift(*ks, *sx)):
            after_x[a, b, c] = value
    out = [None] * 27
    for a in range(3):
        after_y = {}
        for c in range(3):
            triple = unshift(*(after_x[a, b, c] for b in range(3)), *sy)
            for b, value in enumerate(triple):
                after_y[b, c] = value
        for b in range(3):
            triple = unshift(*(after_y[b, c] for c in range(3)), *sz)
            for c, value in enumerate(triple):
                out[9 * a + 3 * b + c] = value
    return out, (rho, jx, jy, jz)


def start_all(copies):
    for copy in copies:
        copy.start()
    return copies


def rows_kernel(pops_in, omega_in, walls_in, up, down, pops, omega, walls, sems):
    planes, ny, nz = omega.shape
    row = lax.broadcasted_iota(jnp.int32, (SUB, nz), 0)
    chunk = 4
    spans = [pl.ds(i, min(chunk, 27 - i)) for i in range(0, 27, chunk)]
    cells = [
        pltpu.make_async_copy(omega_in, omega, sems.at[len(spans)]),
        pltpu.make_async_copy(walls_in, walls, sems.at[len(spans) + 1]),
    ]
    copies = [pltpu.make_async_copy(pops_in.at[span], pops.at[span], sems.at[k]) for k, span in enumerate(spans)]
    start_all(cells + copies)

    def read(group, plane, first):
        part = pl.ds(first, SUB)
        if group < 27:
            return pops[group, plane, part, :] - 1.0
        if group == 27:
            return 1.0 - omega[plane, part, :]
        return walls[plane, part, :].astype(F32)

    def pack(group, first, at):
        if group > 28:
            return jnp.zeros((SUB, nz), F32)
        tile = None
        for plane in range(planes):
            turn = (2 * plane - at) % SUB
            piece = read(group, plane, first)
            piece = pltpu.roll(piece, turn, 0) if turn else piece
            tile = piece if tile is None else jnp.where(row // 2 == plane, piece, tile)
        return tile

    for pair in range(15):
        if pair % 2 == 0 and pair < 14:
            copies[pair // 2].wait()
        if pair == 13:
            for copy in cells:
                copy.wait()
        for out, first, at in ((up, ny - SUB, SUB - 2), (down, 0, 0)):
            both = [pack(2 * pair + k, first, at) for k in range(2)]
            out[pl.ds(16 * pair, 16), :] = jnp.concatenate(both, axis=0).astype(BF16)


def first_main_kernel(pops, omega, walls, post):
    planes, ny, nz = omega.shape

    def body(plane, carry):
        for t in range(ny // SUB):
            for part in range(nz // LANES):
                at = (plane, pl.ds(SUB * t, SUB), pl.ds(LANES * part, LANES))
                f = [pops[(i, *at)] * WEIGHT[i] for i in range(27)]
                closed = walls[at] == 1
                out, _ = collide(f, 1.0 - omega[at])
                for i in range(27):
                    post[(i, *at)] = jnp.where(closed, SOLID, out[i])
        return carry

    lax.fori_loop(0, planes, body, 0)


def fold(tiles):
    if len(tiles) == 1:
        return tiles[0]
    row = lax.broadcasted_iota(jnp.int32, tiles[0].shape, 0)
    return jnp.where((row < 2) | (row > 5), tiles[0], pltpu.roll(tiles[1], 4, 0))


def pack_x(main, halo, plane, first, out):
    ny, nz = main.shape[2:]
    scaled = lambda ref, i: ref[i, plane, :, :] * (1.0 / WEIGHT[i]) - 1.0
    for k in range(9):
        out[pl.ds(ny * k, ny), :] = scaled(main, first + k).astype(BF16)
    tiles = [fold([scaled(halo, first + k + j) for j in range(2) if k + j < 9]) for k in range(0, 9, 2)]
    tiles.append(jnp.zeros((SUB, nz), F32))
    out[pl.ds(9 * ny, SUB * len(tiles)), :] = jnp.concatenate(tiles, axis=0).astype(BF16)


def first_halo_kernel(before, after, main, halo, retain, solid, send_up, send_down, wide_before, wide_after):
    _, planes, _, nz = halo.shape
    row = lax.broadcasted_iota(jnp.int32, (SUB, nz), 0)
    wide_before[...] = before[...].astype(F32)
    wide_after[...] = after[...].astype(F32)

    def beside(group, plane):
        low = wide_after[pl.ds(SUB * group, SUB), :]
        high = wide_before[pl.ds(SUB * group, SUB), :]
        turn_low, turn_high = (-2 * plane) % SUB, (SUB - 2 - 2 * plane) % SUB
        low = pltpu.roll(low, turn_low, 0) if turn_low else low
        high = pltpu.roll(high, turn_high, 0) if turn_high else high
        return jnp.where(row < 4, low, high)

    for plane in range(planes):
        retain[plane, :, :] = beside(27, plane)
        solid[plane, :, :] = beside(28, plane)
        for i in range(27):
            halo[i, plane, :, :] = (beside(i, plane) + 1.0) * WEIGHT[i]

    def body(plane, carry):
        for part in range(nz // LANES):
            at = (plane, slice(None), pl.ds(LANES * part, LANES))
            closed = solid[at] > 0.5
            out, _ = collide([halo[(i, *at)] for i in range(27)], retain[at])
            for i in range(27):
                halo[(i, *at)] = jnp.where(closed, SOLID, out[i])
        return carry

    lax.fori_loop(0, planes, body, 0)
    pack_x(main, halo, planes - 1, 18, send_up)
    pack_x(main, halo, 0, 0, send_down)


def turned(value, i):
    _, sy, sz = STEP[i]
    if sy:
        value = pltpu.roll(value, sy % value.shape[0], 0)
    if sz:
        value = pltpu.roll(value, sz % value.shape[1], 1)
    return value


def pull(load, i, plane):
    value = turned(load(i, plane - STEP[i][0]), i)
    return jnp.where(value > LIMIT, load(26 - i, plane), value)


def widen(face, wide):
    wide[...] = face[...].astype(F32)


def loader(planes, ny, places, before=None, after=None):
    def load(i, plane):
        if 0 <= plane < planes:
            main, halo, at = places[plane]
            return jnp.concatenate([main[i, at, :, :], halo[i, at, :, :]], axis=0)
        wide, k = (before, i - 18) if plane < 0 else (after, i)
        halo = wide[pl.ds(9 * ny + SUB * (k // 2), SUB), :]
        if k % 2:
            halo = pltpu.roll(halo, 4, 0)
        both = jnp.concatenate([wide[pl.ds(ny * k, ny), :], halo], axis=0)
        return (both + 1.0) * WEIGHT[i]

    return load


def middle(mine, load, pops, omega, walls, retain, solid, main2, halo2, macro, read):
    planes, ny, nz = omega.shape
    for at, plane in enumerate(mine):
        own = walls[plane, :, :] == 1
        for i in range(27):
            value = pull(load, i, plane)
            read[i, pl.ds(0, ny), :] = jnp.where(own, pops[i, plane, :, :] * WEIGHT[i], value[:ny])
            read[i, pl.ds(ny, SUB), :] = value[ny:]
        for t in range(ny // SUB + 1):
            for part in range(nz // LANES):
                rows, cols = pl.ds(SUB * t, SUB), pl.ds(LANES * part, LANES)
                inner = SUB * t < ny
                if inner:
                    closed = walls[plane, rows, cols] == 1
                    keep = 1.0 - omega[plane, rows, cols]
                else:
                    closed = solid[plane, :, cols] > 0.5
                    keep = retain[plane, :, cols]
                out, sums = collide([read[i, rows, cols] for i in range(27)], keep)
                for i in range(27):
                    value = jnp.where(closed, SOLID, out[i])
                    if inner:
                        main2[i, at, rows, cols] = value
                    else:
                        halo2[i, at, :, cols] = value
                if inner:
                    macro[0, at, rows, cols] = sums[0] - 1.0
                    for m in range(1, 4):
                        macro[m, at, rows, cols] = sums[m]


def middle_inner_kernel(main, halo, pops, omega, walls, retain, solid, main2, halo2, macro, read):
    planes, ny, _ = omega.shape
    load = loader(planes, ny, [(main, halo, p) for p in range(planes)])
    middle(range(1, planes - 1), load, pops, omega, walls, retain, solid, main2, halo2, macro, read)


def middle_outer_kernel(
    main, halo, pops, omega, walls, retain, solid, before, after, _,
    main2, halo2, macro, send_up, send_down, read, wide_before, wide_after,
):
    planes, ny, _ = omega.shape
    widen(before, wide_before)
    widen(after, wide_after)
    load = loader(planes, ny, [(main, halo, p) for p in range(planes)], wide_before, wide_after)
    middle((0, planes - 1), load, pops, omega, walls, retain, solid, main2, halo2, macro, read)
    pack_x(main2, halo2, 1, 18, send_up)
    pack_x(main2, halo2, 0, 0, send_down)


def add_moments(sums, i, f):
    for m, sign in enumerate((1,) + STEP[i]):
        if sign:
            term = f if sign > 0 else -f
            sums[m] = term if sums[m] is None else sums[m] + term


def respond(planes, radiation, pick, fields):
    for p, rows in enumerate(planes):
        ny = rows[0].shape[0]
        for m in range(4):
            fields[m, pl.ds(p * ny, ny), :] = rows[m].astype(BF16)
    parts = []
    for m in range(4):
        total = None
        for h in range(pick.shape[0]):
            term = jnp.dot(pick[h, :, :], fields[m, :, pl.ds(LANES * h, LANES)], preferred_element_type=F32)
            total = term if total is None else total + term
        parts.append(total)
    surface = jnp.concatenate(parts, axis=1).astype(BF16)
    response = lax.dot_general(
        surface, radiation[...], (((1,), (1,)), ((), ())), preferred_element_type=F32
    )
    return response.astype(BF16)


def slots_kernel(bins, counts, sites, patches, pick, level):
    halves, slots, lines = pick.shape
    slot = lax.broadcasted_iota(jnp.int32, (slots, lines), 0)
    line = lax.broadcasted_iota(jnp.int32, (slots, lines), 1)
    wanted = jnp.full((slots, lines), -1, jnp.int32)
    for k in range(slots):
        site = jnp.where(k < counts[0, 0], sites[0, 0, k], -halves)
        wanted = jnp.where(slot == k, site, wanted)
    for h in range(halves):
        pick[h, :, :] = (wanted == line * halves + h).astype(BF16)

    n_patch = bins.shape[1]
    slot = lax.broadcasted_iota(jnp.int32, (LANES, n_patch), 0)
    named = lax.broadcasted_iota(jnp.int32, (LANES, n_patch), 1)
    wanted = jnp.full((LANES, n_patch), -1, jnp.int32)
    for k in range(slots):
        wanted = jnp.where(slot == k, patches[0, 0, k], wanted)
    chosen = (wanted == named).astype(BF16)
    per_block = lax.dot_general(
        bins[...].astype(F32).astype(BF16), chosen, (((1,), (1,)), ((), ())), preferred_element_type=F32
    )
    devices, _, width = level.shape
    first = lax.broadcasted_iota(jnp.int32, (SUB, width), 0) == 0
    for d in range(devices):
        blk = d * width // OBS_BLK
        line = jnp.broadcast_to(per_block[blk : blk + 1, :width], (SUB, width))
        level[d, :, :] = jnp.where(first, line, 0.0).astype(BF16)


def last_early_kernel(
    main_in, halo_in, main_out, halo_out, pops, walls, macro_in, macro_out, radiation, pick,
    out, spare, part, inner, send, g_out, fields, sems,
):
    planes, ny, _ = walls.shape
    last = planes - 1
    places = [(main_out, halo_out, 0)]
    places += [(main_in, halo_in, p) for p in range(planes - 2)]
    places += [(main_out, halo_out, 1)]
    load = loader(planes, ny, places)
    copies = []
    for plane in (0, last, *range(1, last)):
        own = walls[plane, :, :] == 1
        edge = {0: 0, last: 1}.get(plane)
        sums = [None] * 4
        for i in range(27):
            if 0 <= plane - STEP[i][0] <= last:
                value = pull(load, i, plane)[:ny]
                g = jnp.where(own, pops[i, plane, :, :], value * (1.0 / WEIGHT[i]))
                g_out[i, plane, :, :] = g
                add_moments(sums, i, g * WEIGHT[i])
            else:
                bounced = load(26 - i, plane)[:ny]
                spare[edge, i % 9, :, :] = jnp.where(own, pops[i, plane, :, :] * WEIGHT[i], bounced)
        for m in range(4):
            if edge is None:
                inner[m, plane - 1, :, :] = sums[m] - 1.0 if m == 0 else sums[m]
            else:
                part[m, edge, :, :] = sums[m]
        span = pl.ds((0, 9)[edge], 18) if edge is not None else pl.ds(0, 27)
        copies += start_all(
            [pltpu.make_async_copy(g_out.at[span, plane], out.at[span, plane], sems.at[len(copies)])]
        )
    rows = [[macro_out[m, 0, :, :] for m in range(4)]]
    rows += [[macro_in[m, p, :, :] for m in range(4)] for p in range(planes - 2)]
    rows += [[macro_out[m, 1, :, :] for m in range(4)]]
    response = respond(rows, radiation, pick, fields)
    devices, _, width = send.shape
    for d in range(devices):
        send[d, :, :] = response[:, d * width : (d + 1) * width]
    for copy in copies:
        copy.wait()


def last_kernel(
    before, after, walls, spare, part, inner, radiation, pick, early, level, started,
    out, send, g_out, fields, wide_before, wide_after, sems,
):
    planes, ny, _ = walls.shape
    last = planes - 1
    widen(before, wide_before)
    widen(after, wide_after)
    load = loader(planes, ny, None, wide_before, wide_after)
    rows, copies = {}, []
    for edge, (plane, first) in enumerate(((0, 18), (last, 0))):
        own = walls[plane, :, :] == 1
        sums = [part[m, edge, :, :] for m in range(4)]
        for k in range(9):
            i = first + k
            value = turned(load(i, plane - STEP[i][0]), i)[:ny]
            f = jnp.where(own | (value > LIMIT), spare[edge, k, :, :], value)
            g_out[k, edge, :, :] = f * (1.0 / WEIGHT[i])
            add_moments(sums, i, f)
        rows[plane] = [sums[0] - 1.0, *sums[1:]]
        copies += start_all(
            [pltpu.make_async_copy(g_out.at[:, edge], out.at[pl.ds(first, 9), plane], sems.at[edge])]
        )
    for p in range(planes - 2):
        rows[p + 1] = [inner[m, p, :, :] for m in range(4)]
    response = respond([rows[p] for p in range(planes)], radiation, pick, fields)
    devices, _, width = send.shape
    slots = early.shape[1]
    for d in range(devices):
        send[d, pl.ds(0, slots), :] = early[d, :, :]
        send[d, pl.ds(slots, slots), :] = response[:, d * width : (d + 1) * width]
        send[d, pl.ds(2 * slots, SUB), :] = level[d, :, :]
    for copy in copies:
        copy.wait()


def bin_kernel(received, signal, hits):
    devices, rows, width = received.shape
    slots = (rows - SUB) // 2
    lev = received[:, pl.ds(2 * slots, SUB), :].astype(F32)[:, 0, :].astype(BF16)
    total = devices * slots
    src = lax.broadcasted_iota(jnp.int32, (total, devices), 0) // slots
    col = lax.broadcasted_iota(jnp.int32, (total, devices), 1)
    spread = jnp.dot((src == col).astype(BF16), lev, preferred_element_type=F32)
    slot = lax.broadcasted_iota(jnp.int32, (total, width), 0) % slots
    lane = lax.broadcasted_iota(jnp.int32, (total, width), 1)
    mine = jnp.where(slot == lane, spread, 0.0).astype(BF16)
    level = jnp.dot(mine, jnp.ones((width, LEVELS), BF16), preferred_element_type=F32)
    lane = lax.broadcasted_iota(jnp.int32, (total, LEVELS), 1).astype(F32)
    for step in range(2):
        hit = (level + float(step) == lane).astype(F32).astype(BF16)
        hits[:, pl.ds(step * slots, slots), :] = hit.reshape(devices, slots, LEVELS)
    left = received[:, pl.ds(0, 2 * slots), :].reshape(2 * total, width)
    right = hits[...].reshape(2 * total, LEVELS)
    signal[...] = lax.dot_general(left, right, (((0,), (0,)), ((), ())), preferred_element_type=F32)


def per_device(populations, omega, walls, radiation, bins, counts, sample_site, sample_patch):
    _, planes, ny, nz = populations.shape
    slots = sample_site.shape[-1]
    size_x, size_y = lax.axis_size("gx"), lax.axis_size("gy")
    devices = size_x * size_y
    width = radiation.shape[0] // devices

    def exchange(up, down, axis, size):
        right = [(i, (i + 1) % size) for i in range(size)]
        left = [(j, i) for i, j in right]
        return lax.ppermute(up, axis, right), lax.ppermute(down, axis, left)

    dma = pltpu.SemaphoreType.DMA
    block, cells = populations.shape, (planes, ny, nz)
    beside = (30 * SUB, nz)
    up, down = call(
        rows_kernel,
        [HBM] * 3,
        [(VMEM, beside, BF16)] * 2,
        [pltpu.VMEM(block, F32), pltpu.VMEM(cells, F32), pltpu.VMEM(cells, walls.dtype), dma((9,))],
        cost=1 << 20,
        limit=64800000,
    )(populations, omega, walls)
    before, after = exchange(up, down, "gy", size_y)
    pick, level = call(
        slots_kernel,
        [VMEM] + [SMEM] * 3,
        [(VMEM, (nz // LANES, slots, planes * ny), BF16), (VMEM, (devices, SUB, width), BF16)],
        cost=1 << 18,
    )(bins.T, counts, sample_site, sample_patch)
    (main,) = call(first_main_kernel, [VMEM] * 3, [(VMEM, block, F32)], cost=1 << 22)(populations, omega, walls)

    edge = (planes, SUB, nz)
    face = (9 * ny + 6 * SUB, nz)
    faces = [(VMEM, face, BF16)] * 2
    halo, retain, solid, up, down = call(
        first_halo_kernel,
        [VMEM] * 3,
        [(VMEM, (27, *edge), F32), (VMEM, edge, F32), (VMEM, edge, F32), *faces],
        [pltpu.VMEM(beside, F32)] * 2,
        cost=1 << 20,
    )(before, after, main)
    before, after = exchange(up, down, "gx", size_x)

    def relaxed(n):
        return [(VMEM, (27, n, ny, nz), F32), (VMEM, (27, n, SUB, nz), F32), (VMEM, (4, n, ny, nz), F32)]

    read = pltpu.VMEM((27, ny + SUB, nz), F32)
    wide = [pltpu.VMEM(face, F32)] * 2
    args = (main, halo, populations, omega, walls, retain, solid)
    main_in, halo_in, macro_in = call(
        middle_inner_kernel, [VMEM] * 7, relaxed(planes - 2), [read], cost=1 << 22
    )(*args)
    main_out, halo_out, macro_out, up, down = call(
        middle_outer_kernel, [VMEM] * 10, relaxed(2) + faces, [read, *wide], cost=1 << 22
    )(*args, before, after, macro_in)
    before, after = exchange(up, down, "gx", size_x)

    fields = pltpu.VMEM((4, planes * ny, nz), BF16)
    inner = (4, planes - 2, ny, nz)
    started, spare, part, inner, early = call(
        last_early_kernel,
        [VMEM] * 10,
        [
            (HBM, block, F32),
            (VMEM, (2, 9, ny, nz), F32),
            (VMEM, (4, 2, ny, nz), F32),
            (VMEM, inner, F32),
            (VMEM, (devices, slots, width), BF16),
        ],
        [pltpu.VMEM(block, F32), fields, dma((planes,))],
        cost=1 << 22,
    )(main_in, halo_in, main_out, halo_out, populations, walls, macro_in, macro_out, radiation, pick)
    advanced, send = call(
        last_kernel,
        [VMEM] * 10 + [HBM],
        [(HBM, block, F32), (VMEM, (devices, 2 * slots + SUB, width), BF16)],
        [pltpu.VMEM((9, 2, ny, nz), F32), fields, *wide, dma((2,))],
        aliases={10: 0},
        cost=1 << 22,
    )(before, after, walls, spare, part, inner, radiation, pick, early, level, started)
    received = lax.all_to_all(send, ("gx", "gy"), 0, 0, tiled=True)
    (signal,) = call(
        bin_kernel, [VMEM], [(VMEM, (width, LEVELS), F32)], [pltpu.VMEM((devices, 2 * slots, LEVELS), BF16)], cost=1 << 20
    )(received)
    return advanced, signal


def solution(mesh):
    return jax.shard_map(
        per_device,
        mesh=mesh,
        in_specs=(
            P(None, "gx", "gy", None),
            P("gx", "gy", None),
            P("gx", "gy", None),
            P(),
            P(),
            P("gx", "gy"),
            P("gx", "gy", None),
            P("gx", "gy", None),
        ),
        out_specs=(P(None, "gx", "gy", None), P(("gx", "gy"), None)),
        check_vma=False,
    )
```

time: 67.2 us -> 48.1 us (0.72)
  Pallas kernels: 22.4 us -> 11.9 us
  waiting for transfers between devices: 11.7 us -> 6.32 us
  local copies, waits for them, and re-layouts: 2.67 us -> 0.03 us
  blocking collectives: 16.9 us -> 16.2 us
    pallas_call x5 -> x9, Pallas kernels: 22.4 us -> 11.9 us  [the longest x1 2.4 us: per_device(): call(rows_kernel, [HBM] * 3, [(VMEM, beside, BF16)] * 2, [pltpu.VMEM(bloc...]
    ppermute x6, waiting for transfers between devices: 11.7 us -> 6.32 us  [exchange(): return (lax.ppermute(up, axis, right), lax.ppermute(down, axis, left))]
    unnamed x15 -> x14, local copies, waits for them, and re-layouts: 2.67 us -> 0.03 us
    all_to_all x1, blocking collectives: 16.9 us -> 16.2 us  [per_device(): received = lax.all_to_all(send, ('gx', 'gy'), 0, 0, tiled=True)]
  transfers between devices with their start and end apart: 6 -> 6, of which waited for: 6 -> 4; matrix products, arithmetic and copies ran while one was open for 1% -> 0% of each run, Pallas kernels for 0% -> 11%
where the time goes in v1:
time: 48.1 us; the launch traced here: 48 us
  blocking collectives  16.2 us (34%)
  starting transfers between devices  12 us (25%)
  Pallas kernels  11.9 us (25%)
  waiting for transfers between devices  6.32 us (13%)
  between operations  1.43 us (3%)
    all_to_all x1, blocking collectives, per_device(): received = lax.all_to_all(send, ('gx', 'gy'), 0, 0, tiled=True)  16.2 us
    ppermute x6, starting transfers between devices, exchange(): return (lax.ppermute(up, axis, right), lax.ppermute(down, axis, left))  12 us
    ppermute x6, waiting for transfers between devices, exchange(): return (lax.ppermute(up, axis, right), lax.ppermute(down, axis, left))  6.32 us
    pallas_call x1, Pallas kernels, per_device(): call(rows_kernel, [HBM] * 3, [(VMEM, beside, BF16)] * 2, [pltpu.VMEM(bloc...  2.4 us
    pallas_call x1, Pallas kernels, per_device(): call(last_early_kernel, [VMEM] * 10, [(HBM, block, F32), (VMEM, (2, 9, ny...  2.31 us
    pallas_call x1, Pallas kernels, per_device(): call(last_kernel, [VMEM] * 10 + [HBM], [(HBM, block, F32), (VMEM, (device...  1.46 us
    pallas_call x1, Pallas kernels, per_device(): call(middle_outer_kernel, [VMEM] * 10, relaxed(2) + faces, [read, *wide],...  1.13 us
    pallas_call x1, Pallas kernels, per_device(): call(bin_kernel, [VMEM], [(VMEM, (width, LEVELS), F32)], [pltpu.VMEM((dev...  1.12 us
  transfers between devices with their start and end apart: 6, of which 4 were waited for; matrix products, arithmetic and copies ran while one was open for 0% of the time, Pallas kernels for 11%

profile of v1, /device:TPU:0, one launch (start us, length us, event | category | flops | bytes accessed | tf_op | source)
XLA Modules:
  0.0 48.0 jit_solution(12785826994268874319)
XLA Ops:
  0.6 0.0 copy-start.2
  0.6 0.0 copy-start
  0.6 0.0 copy-start.3
  0.7 2.4 %shard_map.96 = (bf16[240,256]{1,0:T(8,128)(2,1)}, bf16[240,256]{1,0:T(8,128)(2,1)}) custom-call(f32[27,4,16,256]{3,2,1,0:T(8,128)} %pops.7, f32[4,16,256]{2,1,0:T(8,128)} %omega.5, s32[4,16,256]{2,1,0:T(8,128)} %walls.9), custom_call_target="tpu_custom_call" | custom-call | flops 1048576 | bytes 1048576 | tf_op jit(solution)/shard_map/pallas_call | solution.py:516
  3.1 0.5 %collective-permute-start = (bf16[240,256]{1,0:T(8,128)(2,1)}, bf16[240,256]{1,0:T(8,128)(2,1)S(1)}, u32[]{:S(2)}, u32[]{:S(2)}) collective-permute-start(bf16[240,256]{1,0:T(8,128)(2,1)} %get-tuple-element.26), channel_id=1, source_target_pairs={{0,1},{1,2},{2,3},{3,0},{4,5},{5,6},{6,7},{7,4},{8,9},{9,10},{10,1... | collective-permute-start | bytes 368648 | tf_op jit(solution)/shard_map/ppermute | solution.py:511
  3.6 2.0 %collective-permute-start.1 = (bf16[240,256]{1,0:T(8,128)(2,1)}, bf16[240,256]{1,0:T(8,128)(2,1)S(1)}, u32[]{:S(2)}, u32[]{:S(2)}) collective-permute-start(bf16[240,256]{1,0:T(8,128)(2,1)} %get-tuple-element.27), channel_id=1, source_target_pairs={{1,0},{2,1},{3,2},{0,3},{5,4},{6,5},{7,6},{4,7},{9,8},{10,9},{11,1... | collective-permute-start | bytes 368648 | tf_op jit(solution)/shard_map/ppermute | solution.py:511
  5.6 0.0 copy-done.2
  5.6 0.0 copy-done
  5.6 0.0 copy-done.3
  5.6 1.1 %shard_map.95.main = f32[27,4,16,256]{3,2,1,0:T(8,128)S(1)} custom-call(f32[27,4,16,256]{3,2,1,0:T(8,128)S(1)} %copy-done, f32[4,16,256]{2,1,0:T(8,128)S(1)} %copy-done.3, s32[4,16,256]{2,1,0:T(8,128)S(1)} %copy-done.2), custom_call_target="tpu_custom_call" | custom-call | flops 4194304 | bytes 4194304 | tf_op jit(solution)/shard_map/pallas_call | solution.py:531
  6.6 1.6 %collective-permute-done.before = bf16[240,256]{1,0:T(8,128)(2,1)S(1)} collective-permute-done((bf16[240,256]{1,0:T(8,128)(2,1)}, bf16[240,256]{1,0:T(8,128)(2,1)S(1)}, u32[]{:S(2)}, u32[]{:S(2)}) %collective-permute-start) | collective-permute-done | bytes 122912 | tf_op jit(solution)/shard_map/ppermute | solution.py:511
  8.3 1.2 %collective-permute-done.1.after = bf16[240,256]{1,0:T(8,128)(2,1)S(1)} collective-permute-done((bf16[240,256]{1,0:T(8,128)(2,1)}, bf16[240,256]{1,0:T(8,128)(2,1)S(1)}, u32[]{:S(2)}, u32[]{:S(2)}) %collective-permute-start.1) | collective-permute-done | bytes 122912 | tf_op jit(solution)/shard_map/ppermute | solution.py:511
  9.5 0.7 %shard_map.97 = (f32[27,4,8,256]{3,2,1,0:T(8,128)S(1)}, f32[4,8,256]{2,1,0:T(8,128)S(1)}, f32[4,8,256]{2,1,0:T(8,128)S(1)}, bf16[192,256]{1,0:T(8,128)(2,1)S(1)}, bf16[192,256]{1,0:T(8,128)(2,1)S(1)}) custom-call(bf16[240,256]{1,0:T(8,128)(2,1)S(1)} %collective-permute-done.before, bf16[240,256]{1,0:T(8,128)(2,1)S(1)} %collective-permute-done.1.after, ...), custom_call_target="tpu_custom_call" | custom-call | flops 1048576 | bytes 1048576 | tf_op jit(solution)/shard_map/pallas_call | solution.py:536
  10.2 1.6 %collective-permute-start.2 = (bf16[192,256]{1,0:T(8,128)(2,1)S(1)}, bf16[192,256]{1,0:T(8,128)(2,1)S(1)}, u32[]{:S(2)}, u32[]{:S(2)}) collective-permute-start(bf16[192,256]{1,0:T(8,128)(2,1)S(1)} %get-tuple-element.31), channel_id=1, source_target_pairs={{0,4},{4,8},{8,12},{12,16},{16,20},{20,24},{24,28},{28,0},{1,5},{5... | collective-permute-start | bytes 294920 | tf_op jit(solution)/shard_map/ppermute | solution.py:511
  11.8 3.2 %collective-permute-start.3 = (bf16[192,256]{1,0:T(8,128)(2,1)S(1)}, bf16[192,256]{1,0:T(8,128)(2,1)S(1)}, u32[]{:S(2)}, u32[]{:S(2)}) collective-permute-start(bf16[192,256]{1,0:T(8,128)(2,1)S(1)} %get-tuple-element.32), channel_id=1, source_target_pairs={{4,0},{8,4},{12,8},{16,12},{20,16},{24,20},{28,24},{0,28},{5,1},{9... | collective-permute-start | bytes 294920 | tf_op jit(solution)/shard_map/ppermute | solution.py:511
  15.0 1.1 %shard_map.98 = (f32[27,2,16,256]{3,2,1,0:T(8,128)S(1)}, f32[27,2,8,256]{3,2,1,0:T(8,128)S(1)}, f32[4,2,16,256]{3,2,1,0:T(8,128)S(1)}) custom-call(f32[27,4,16,256]{3,2,1,0:T(8,128)S(1)} %shard_map.95.main, f32[27,4,8,256]{3,2,1,0:T(8,128)S(1)} %get-tuple-element.28.halo, f32[27,4,16,256]{3,2,1,0:T(8,128)S(1)} %copy-done, f32[4,16,256]{2,1,0:T(8,128)S(1)} %copy-done.3, ...), custom_call_target="tpu_custom_call" | custom-call | flops 4194304 | bytes 4194304 | tf_op jit(solution)/shard_map/pallas_call | solution.py:551
  16.1 2.3 %collective-permute-done.2.before = bf16[192,256]{1,0:T(8,128)(2,1)S(1)} collective-permute-done((bf16[192,256]{1,0:T(8,128)(2,1)S(1)}, bf16[192,256]{1,0:T(8,128)(2,1)S(1)}, u32[]{:S(2)}, u32[]{:S(2)}) %collective-permute-start.2) | collective-permute-done | bytes 98336 | tf_op jit(solution)/shard_map/ppermute | solution.py:511
  18.4 1.1 %collective-permute-done.3.after = bf16[192,256]{1,0:T(8,128)(2,1)S(1)} collective-permute-done((bf16[192,256]{1,0:T(8,128)(2,1)S(1)}, bf16[192,256]{1,0:T(8,128)(2,1)S(1)}, u32[]{:S(2)}, u32[]{:S(2)}) %collective-permute-start.3) | collective-permute-done | bytes 98336 | tf_op jit(solution)/shard_map/ppermute | solution.py:511
  19.5 1.1 %shard_map.99 = (f32[27,2,16,256]{3,2,1,0:T(8,128)S(1)}, f32[27,2,8,256]{3,2,1,0:T(8,128)S(1)}, f32[4,2,16,256]{3,2,1,0:T(8,128)S(1)}, bf16[192,256]{1,0:T(8,128)(2,1)S(1)}, bf16[192,256]{1,0:T(8,128)(2,1)S(1)}) custom-call(f32[27,4,16,256]{3,2,1,0:T(8,128)S(1)} %shard_map.95.main, f32[27,4,8,256]{3,2,1,0:T(8,128)S(1)} %get-tuple-element.28.halo, ...), custom_call_target="tpu_custom_call" | custom-call | flops 4194304 | bytes 4194304 | tf_op jit(solution)/shard_map/pallas_call | solution.py:554
  20.6 0.4 collective-permute-start.4
  21.0 4.4 %collective-permute-start.5 = (bf16[192,256]{1,0:T(8,128)(2,1)S(1)}, bf16[192,256]{1,0:T(8,128)(2,1)S(1)}, u32[]{:S(2)}, u32[]{:S(2)}) collective-permute-start(bf16[192,256]{1,0:T(8,128)(2,1)S(1)} %get-tuple-element.35), channel_id=1, source_target_pairs={{4,0},{8,4},{12,8},{16,12},{20,16},{24,20},{28,24},{0,28},{5,1},{9... | collective-permute-start | bytes 294920 | tf_op jit(solution)/shard_map/ppermute | solution.py:511
  26.1 0.0 copy-done.4
  26.1 0.0 copy-done.5
  26.1 0.0 copy-done.6
  26.1 0.7 %shard_map.100 = (bf16[2,16,64]{2,1,0:T(8,128)(2,1)S(1)}, bf16[32,8,128]{2,1,0:T(8,128)(2,1)S(1)}) custom-call(s32[32,128]{1,0:T(8,128)S(1)} %bitcast.1, s32[1,1]{1,0:T(1,128)S(6)} %copy.12.counts, s32[1,1,16]{2,1,0:T(1,128)S(1)} %copy-done.5, s32[1,1,16]{2,1,0:T(1,128)S(1)} %copy-done.6), custom_call_target="tpu_custom_call" | custom-call | flops 262144 | bytes 262144 | tf_op jit(solution)/shard_map/pallas_call | solution.py:525
  26.8 0.0 copy-done.1
  26.8 2.3 %shard_map.101 = (f32[27,4,16,256]{3,2,1,0:T(8,128)}, f32[2,9,16,256]{3,2,1,0:T(8,128)S(1)}, f32[4,2,16,256]{3,2,1,0:T(8,128)S(1)}, f32[4,2,16,256]{3,2,1,0:T(8,128)S(1)}, bf16[32,16,128]{2,1,0:T(8,128)(2,1)S(1)}) custom-call(f32[27,2,16,256]{3,2,1,0:T(8,128)S(1)} %get-tuple-element.36.main_in, f32[27,2,8,256]{3,2,1,0:T(8,128)S(1)} %get-tuple-element.37.halo_in, ...), custom_call_target="tpu_custom_call" | custom-call | flops 4194304 | bytes 4194304 | tf_op jit(solution)/shard_map/pallas_call | solution.py:561
  29.1 0.0 collective-permute-done.4.before
  29.1 0.0 collective-permute-done.5.after
  29.2 1.5 %shard_map.102 = (f32[27,4,16,256]{3,2,1,0:T(8,128)}, bf16[32,40,128]{2,1,0:T(8,128)(2,1)S(1)}) custom-call(bf16[192,256]{1,0:T(8,128)(2,1)S(1)} %collective-permute-done.4.before, bf16[192,256]{1,0:T(8,128)(2,1)S(1)} %collective-permute-done.5.after, s32[4,16,256]{2,1,0:T(8,128)S(1)} %copy-done.2, ...), custom_call_target="tpu_custom_call", output_to_operand_aliasing={{0}: (10, {})} | custom-call | flops 4194304 | bytes 4194304 | tf_op jit(solution)/shard_map/pallas_call | solution.py:574
  30.6 16.2 %all_to_all.5.received = bf16[32,40,128]{2,1,0:T(8,128)(2,1)S(1)} all-to-all(bf16[32,40,128]{2,1,0:T(8,128)(2,1)S(1)} %get-tuple-element.49), channel_id=1, replica_groups=mesh['gx'=8,'gy'=4] {'gx','gy'}, dimensions={0} | all-to-all | bytes 655360 | tf_op jit(solution)/shard_map/all_to_all | solution.py:582
  46.8 1.1 %shard_map.103 = f32[128,128]{1,0:T(8,128)} custom-call(bf16[32,40,128]{2,1,0:T(8,128)(2,1)S(1)} %all_to_all.5.received), custom_call_target="tpu_custom_call" | custom-call | flops 1048576 | bytes 1048576 | tf_op jit(solution)/shard_map/pallas_call | solution.py:583
  (4 shorter events, 0.0 us)
Async XLA Ops:
  0.6 4.9 %copy-start.2 = (s32[4,16,256]{2,1,0:T(8,128)S(1)}, s32[4,16,256]{2,1,0:T(8,128)}, u32[]{:S(2)}) copy-start(s32[4,16,256]{2,1,0:T(8,128)} %walls.9) | copy-start | bytes 196612
  0.6 4.9 %copy-start = (f32[27,4,16,256]{3,2,1,0:T(8,128)S(1)}, f32[27,4,16,256]{3,2,1,0:T(8,128)}, u32[]{:S(2)}) copy-start(f32[27,4,16,256]{3,2,1,0:T(8,128)} %pops.7) | copy-start | bytes 5308420
  0.6 4.9 %copy-start.3 = (f32[4,16,256]{2,1,0:T(8,128)S(1)}, f32[4,16,256]{2,1,0:T(8,128)}, u32[]{:S(2)}) copy-start(f32[4,16,256]{2,1,0:T(8,128)} %omega.5) | copy-start | bytes 196612
  3.1 5.2 %collective-permute-start = (bf16[240,256]{1,0:T(8,128)(2,1)}, bf16[240,256]{1,0:T(8,128)(2,1)S(1)}, u32[]{:S(2)}, u32[]{:S(2)}) collective-permute-start(bf16[240,256]{1,0:T(8,128)(2,1)} %get-tuple-element.26), channel_id=1, source_target_pairs={{0,1},{1,2},{2,3},{3,0},{4,5},{5,6},{6,7},{7,4},{8,9},{9,10},{10,1... | collective-permute-start | bytes 368648 | tf_op jit(solution)/shard_map/ppermute | solution.py:511
  3.6 5.9 %collective-permute-start.1 = (bf16[240,256]{1,0:T(8,128)(2,1)}, bf16[240,256]{1,0:T(8,128)(2,1)S(1)}, u32[]{:S(2)}, u32[]{:S(2)}) collective-permute-start(bf16[240,256]{1,0:T(8,128)(2,1)} %get-tuple-element.27), channel_id=1, source_target_pairs={{1,0},{2,1},{3,2},{0,3},{5,4},{6,5},{7,6},{4,7},{9,8},{10,9},{11,1... | collective-permute-start | bytes 368648 | tf_op jit(solution)/shard_map/ppermute | solution.py:511
  10.2 8.2 %collective-permute-start.2 = (bf16[192,256]{1,0:T(8,128)(2,1)S(1)}, bf16[192,256]{1,0:T(8,128)(2,1)S(1)}, u32[]{:S(2)}, u32[]{:S(2)}) collective-permute-start(bf16[192,256]{1,0:T(8,128)(2,1)S(1)} %get-tuple-element.31), channel_id=1, source_target_pairs={{0,4},{4,8},{8,12},{12,16},{16,20},{20,24},{24,28},{28,0},{1,5},{5... | collective-permute-start | bytes 294920 | tf_op jit(solution)/shard_map/ppermute | solution.py:511
  11.8 7.7 %collective-permute-start.3 = (bf16[192,256]{1,0:T(8,128)(2,1)S(1)}, bf16[192,256]{1,0:T(8,128)(2,1)S(1)}, u32[]{:S(2)}, u32[]{:S(2)}) collective-permute-start(bf16[192,256]{1,0:T(8,128)(2,1)S(1)} %get-tuple-element.32), channel_id=1, source_target_pairs={{4,0},{8,4},{12,8},{16,12},{20,16},{24,20},{28,24},{0,28},{5,1},{9... | collective-permute-start | bytes 294920 | tf_op jit(solution)/shard_map/ppermute | solution.py:511
  19.5 6.6 %copy-start.4 = (s32[128,32]{0,1:T(8,128)S(1)}, s32[128,32]{0,1:T(8,128)}, u32[]{:S(2)}) copy-start(s32[128,32]{0,1:T(8,128)} %param.12) | copy-start | bytes 49156
  19.5 6.6 %copy-start.5 = (s32[1,1,16]{2,1,0:T(1,128)S(1)}, s32[1,1,16]{2,1,0:T(1,128)}, u32[]{:S(2)}) copy-start(s32[1,1,16]{2,1,0:T(1,128)} %sites.1) | copy-start | bytes 196
  19.5 6.6 %copy-start.6 = (s32[1,1,16]{2,1,0:T(1,128)S(1)}, s32[1,1,16]{2,1,0:T(1,128)}, u32[]{:S(2)}) copy-start(s32[1,1,16]{2,1,0:T(1,128)} %patches.1) | copy-start | bytes 196
  19.5 7.3 %copy-start.1 = (bf16[4096,512]{1,0:T(8,128)(2,1)S(1)}, bf16[4096,512]{1,0:T(8,128)(2,1)}, u32[]{:S(2)}) copy-start(bf16[4096,512]{1,0:T(8,128)(2,1)} %radiation.3) | copy-start | bytes 12582916
  20.6 8.5 %collective-permute-start.4 = (bf16[192,256]{1,0:T(8,128)(2,1)S(1)}, bf16[192,256]{1,0:T(8,128)(2,1)S(1)}, u32[]{:S(2)}, u32[]{:S(2)}) collective-permute-start(bf16[192,256]{1,0:T(8,128)(2,1)S(1)} %get-tuple-element.34), channel_id=1, source_target_pairs={{0,4},{4,8},{8,12},{12,16},{16,20},{20,24},{24,28},{28,0},{1,5},{5... | collective-permute-start | bytes 294920 | tf_op jit(solution)/shard_map/ppermute | solution.py:511
  21.0 8.1 %collective-permute-start.5 = (bf16[192,256]{1,0:T(8,128)(2,1)S(1)}, bf16[192,256]{1,0:T(8,128)(2,1)S(1)}, u32[]{:S(2)}, u32[]{:S(2)}) collective-permute-start(bf16[192,256]{1,0:T(8,128)(2,1)S(1)} %get-tuple-element.35), channel_id=1, source_target_pairs={{4,0},{8,4},{12,8},{16,12},{20,16},{24,20},{28,24},{0,28},{5,1},{9... | collective-permute-start | bytes 294920 | tf_op jit(solution)/shard_map/ppermute | solution.py:511

commit v2 on v1

--- a/solution.py
+++ b/solution.py
@@ -149,7 +149,13 @@
     return copies
 
 
-def rows_kernel(pops_in, omega_in, walls_in, up, down, pops, omega, walls, sems):
+def rows_order(side):
+    outward = 1 - 2 * side
+    both = [i for i in range(27) if STEP[i][1] == outward]
+    return both, [i for i in range(27) if STEP[i][1] != outward]
+
+
+def rows_kernel(pops_in, omega_in, walls_in, up, down, pops, omega, walls, packed, sems):
     planes, ny, nz = omega.shape
     row = lax.broadcasted_iota(jnp.int32, (SUB, nz), 0)
     chunk = 4
@@ -164,31 +170,47 @@
     def read(group, plane, first):
         part = pl.ds(first, SUB)
         if group < 27:
-            return pops[group, plane, part, :] - 1.0
+            return pops[group, plane, part, :]
         if group == 27:
             return 1.0 - omega[plane, part, :]
         return walls[plane, part, :].astype(F32)
 
-    def pack(group, first, at):
-        if group > 28:
-            return jnp.zeros((SUB, nz), F32)
-        tile = None
-        for plane in range(planes):
-            turn = (2 * plane - at) % SUB
-            piece = read(group, plane, first)
-            piece = pltpu.roll(piece, turn, 0) if turn else piece
-            tile = piece if tile is None else jnp.where(row // 2 == plane, piece, tile)
-        return tile
-
-    for pair in range(15):
-        if pair % 2 == 0 and pair < 14:
-            copies[pair // 2].wait()
-        if pair == 13:
-            for copy in cells:
-                copy.wait()
-        for out, first, at in ((up, ny - SUB, SUB - 2), (down, 0, 0)):
-            both = [pack(2 * pair + k, first, at) for k in range(2)]
-            out[pl.ds(16 * pair, 16), :] = jnp.concatenate(both, axis=0).astype(BF16)
+    def pack(group):
+        for side, first, at in ((0, ny - SUB, SUB - 2), (1, 0, 0)):
+            tile = None
+            for plane in range(planes):
+                turn = (2 * plane - at) % SUB
+                piece = read(group, plane, first)
+                piece = pltpu.roll(piece, turn, 0) if turn else piece
+                tile = piece if tile is None else jnp.where(row // 2 == plane, piece, tile)
+            packed[side, group, :, :] = tile
+
+    for copy in cells:
+        copy.wait()
+    pack(27)
+    pack(28)
+    for i in range(27):
+        if i % chunk == 0:
+            copies[i // chunk].wait()
+        pack(i)
+    for side, out in ((0, up), (1, down)):
+        for part in range(nz // LANES):
+            cols = pl.ds(LANES * part, LANES)
+            closed = packed[side, 28, :, cols] > 0.5
+            f = [packed[side, i, :, cols] * WEIGHT[i] for i in range(27)]
+            relaxed, _ = collide(f, packed[side, 27, :, cols])
+            for i in range(27):
+                packed[side, i, :, cols] = jnp.where(closed, SOLID, relaxed[i]) * (1.0 / WEIGHT[i]) - 1.0
+        both, edge = rows_order(side)
+        edge = edge + [27, 28]
+        tiles = [packed[side, i, :, :] for i in both]
+        for k in range(0, len(edge), 2):
+            one, two = (packed[side, i, :, :] for i in edge[k : k + 2])
+            at_edge = row % 2 == 1 - side
+            tiles.append(jnp.where(at_edge, one, pltpu.roll(two, SUB - 1 if side == 0 else 1, 0)))
+        tiles.append(jnp.zeros((SUB, nz), F32))
+        for k in range(0, len(tiles), 2):
+            out[pl.ds(SUB * k, 2 * SUB), :] = jnp.concatenate(tiles[k : k + 2], axis=0).astype(BF16)
 
 
 def first_main_kernel(pops, omega, walls, post):
@@ -208,55 +230,76 @@
     lax.fori_loop(0, planes, body, 0)
 
 
-def fold(tiles):
-    if len(tiles) == 1:
-        return tiles[0]
-    row = lax.broadcasted_iota(jnp.int32, tiles[0].shape, 0)
-    return jnp.where((row < 2) | (row > 5), tiles[0], pltpu.roll(tiles[1], 4, 0))
-
-
-def pack_x(main, halo, plane, first, out):
+def corner_rows(reach):
+    places = {}
+    for k in range(9):
+        sy, j = STEP[k][1], k % 3
+        if reach == 2:
+            rows = {1: ((6, 6), (7, 7)), 0: ((7, 3), (0, 4)), -1: ((0, 0), (1, 1))}[sy]
+            places[k] = [(ring, j, at) for ring, at in rows]
+        else:
+            places[k] = {1: [(7, 0, j)], 0: [], -1: [(0, 0, 3 + j)]}[sy]
+    return places
+
+
+def face_rows(ny, reach):
+    return 9 * ny + (4 if reach == 2 else 2) * SUB
+
+
+def pack_x(main, halo, plane, first, reach, out):
     ny, nz = main.shape[2:]
-    scaled = lambda ref, i: ref[i, plane, :, :] * (1.0 / WEIGHT[i]) - 1.0
+    row = lax.broadcasted_iota(jnp.int32, (SUB, nz), 0)
+    scaled = lambda ref, k: ref[first + k, plane, :, :] * (1.0 / WEIGHT[k]) - 1.0
     for k in range(9):
-        out[pl.ds(ny * k, ny), :] = scaled(main, first + k).astype(BF16)
-    tiles = [fold([scaled(halo, first + k + j) for j in range(2) if k + j < 9]) for k in range(0, 9, 2)]
-    tiles.append(jnp.zeros((SUB, nz), F32))
+        out[pl.ds(ny * k, ny), :] = scaled(main, k).astype(BF16)
+    tiles = [jnp.zeros((SUB, nz), F32) for _ in range((out.shape[0] - 9 * ny) // SUB)]
+    for k, places in corner_rows(reach).items():
+        for ring, tile, at in places:
+            turn = (at - ring) % SUB
+            value = scaled(halo, k)
+            value = pltpu.roll(value, turn, 0) if turn else value
+            tiles[tile] = jnp.where(row == at, value, tiles[tile])
     out[pl.ds(9 * ny, SUB * len(tiles)), :] = jnp.concatenate(tiles, axis=0).astype(BF16)
 
 
-def first_halo_kernel(before, after, main, halo, retain, solid, send_up, send_down, wide_before, wide_after):
+def odd_block():
+    return lax.rem(lax.axis_index("gx"), 2)
+
+
+def pack_faces(main, halo, last, reach, far, near):
+    odd = odd_block()
+    pack_x(main, halo, odd * last, odd * 18, reach, far)
+    pack_x(main, halo, (1 - odd) * last, (1 - odd) * 18, reach, near)
+
+
+def first_halo_kernel(before, after, main, halo, retain, solid, send_far, send_near, wide_before, wide_after):
     _, planes, _, nz = halo.shape
     row = lax.broadcasted_iota(jnp.int32, (SUB, nz), 0)
     wide_before[...] = before[...].astype(F32)
     wide_after[...] = after[...].astype(F32)
 
+    def received(side, group, plane):
+        both, edge = rows_order(side)
+        edge = edge + [27, 28]
+        turn = (SUB - 2, 0)[side] - 2 * plane
+        if group in both:
+            tile = both.index(group)
+        else:
+            k = edge.index(group)
+            tile = len(both) + k // 2
+            turn += (k % 2) * (1 - 2 * side)
+        value = (wide_before, wide_after)[side][pl.ds(SUB * tile, SUB), :]
+        return pltpu.roll(value, turn % SUB, 0) if turn % SUB else value
+
     def beside(group, plane):
-        low = wide_after[pl.ds(SUB * group, SUB), :]
-        high = wide_before[pl.ds(SUB * group, SUB), :]
-        turn_low, turn_high = (-2 * plane) % SUB, (SUB - 2 - 2 * plane) % SUB
-        low = pltpu.roll(low, turn_low, 0) if turn_low else low
-        high = pltpu.roll(high, turn_high, 0) if turn_high else high
-        return jnp.where(row < 4, low, high)
+        return jnp.where(row < 4, received(1, group, plane), received(0, group, plane))
 
     for plane in range(planes):
         retain[plane, :, :] = beside(27, plane)
         solid[plane, :, :] = beside(28, plane)
         for i in range(27):
             halo[i, plane, :, :] = (beside(i, plane) + 1.0) * WEIGHT[i]
-
-    def body(plane, carry):
-        for part in range(nz // LANES):
-            at = (plane, slice(None), pl.ds(LANES * part, LANES))
-            closed = solid[at] > 0.5
-            out, _ = collide([halo[(i, *at)] for i in range(27)], retain[at])
-            for i in range(27):
-                halo[(i, *at)] = jnp.where(closed, SOLID, out[i])
-        return carry
-
-    lax.fori_loop(0, planes, body, 0)
-    pack_x(main, halo, planes - 1, 18, send_up)
-    pack_x(main, halo, 0, 0, send_down)
+    pack_faces(main, halo, planes - 1, 2, send_far, send_near)
 
 
 def turned(value, i):
@@ -273,20 +316,27 @@
     return jnp.where(value > LIMIT, load(26 - i, plane), value)
 
 
-def widen(face, wide):
-    wide[...] = face[...].astype(F32)
-
-
-def loader(planes, ny, places, before=None, after=None):
+def widen(far, near, wide):
+    odd = odd_block()
+    wide[odd, :, :] = far[...].astype(F32)
+    wide[1 - odd, :, :] = near[...].astype(F32)
+
+
+def loader(planes, ny, places, wide=None):
     def load(i, plane):
         if 0 <= plane < planes:
             main, halo, at = places[plane]
             return jnp.concatenate([main[i, at, :, :], halo[i, at, :, :]], axis=0)
-        wide, k = (before, i - 18) if plane < 0 else (after, i)
-        halo = wide[pl.ds(9 * ny + SUB * (k // 2), SUB), :]
-        if k % 2:
-            halo = pltpu.roll(halo, 4, 0)
-        both = jnp.concatenate([wide[pl.ds(ny * k, ny), :], halo], axis=0)
+        side, k = (0, i - 18) if plane < 0 else (1, i)
+        reach = 2 if wide.shape[1] == face_rows(ny, 2) else 1
+        used = corner_rows(reach)[k]
+        if used:
+            ring, tile, at = used[0]
+            halo = wide[side, pl.ds(9 * ny + SUB * tile, SUB), :]
+            halo = pltpu.roll(halo, (ring - at) % SUB, 0) if ring != at else halo
+        else:
+            halo = jnp.zeros((SUB, wide.shape[2]), F32)
+        both = jnp.concatenate([wide[side, pl.ds(ny * k, ny), :], halo], axis=0)
         return (both + 1.0) * WEIGHT[i]
 
     return load
@@ -330,16 +380,14 @@
 
 
 def middle_outer_kernel(
-    main, halo, pops, omega, walls, retain, solid, before, after, _,
-    main2, halo2, macro, send_up, send_down, read, wide_before, wide_after,
+    main, halo, pops, omega, walls, retain, solid, far, near, _, __,
+    main2, halo2, macro, send_far, send_near, read, wide,
 ):
     planes, ny, _ = omega.shape
-    widen(before, wide_before)
-    widen(after, wide_after)
-    load = loader(planes, ny, [(main, halo, p) for p in range(planes)], wide_before, wide_after)
+    widen(far, near, wide)
+    load = loader(planes, ny, [(main, halo, p) for p in range(planes)], wide)
     middle((0, planes - 1), load, pops, omega, walls, retain, solid, main2, halo2, macro, read)
-    pack_x(main2, halo2, 1, 18, send_up)
-    pack_x(main2, halo2, 0, 0, send_down)
+    pack_faces(main2, halo2, 1, 1, send_far, send_near)
 
 
 def add_moments(sums, i, f):
@@ -362,13 +410,11 @@
             total = term if total is None else total + term
         parts.append(total)
     surface = jnp.concatenate(parts, axis=1).astype(BF16)
-    response = lax.dot_general(
-        surface, radiation[...], (((1,), (1,)), ((), ())), preferred_element_type=F32
-    )
+    response = jnp.dot(surface, radiation[...], preferred_element_type=F32)
     return response.astype(BF16)
 
 
-def slots_kernel(bins, counts, sites, patches, pick, level):
+def slots_kernel(bins, radiation, counts, sites, patches, pick, level, turned_radiation):
     halves, slots, lines = pick.shape
     slot = lax.broadcasted_iota(jnp.int32, (slots, lines), 0)
     line = lax.broadcasted_iota(jnp.int32, (slots, lines), 1)
@@ -380,21 +426,38 @@
         pick[h, :, :] = (wanted == line * halves + h).astype(BF16)
 
     n_patch = bins.shape[1]
-    slot = lax.broadcasted_iota(jnp.int32, (LANES, n_patch), 0)
-    named = lax.broadcasted_iota(jnp.int32, (LANES, n_patch), 1)
-    wanted = jnp.full((LANES, n_patch), -1, jnp.int32)
+    slot = lax.broadcasted_iota(jnp.int32, (slots, n_patch), 0)
+    named = lax.broadcasted_iota(jnp.int32, (slots, n_patch), 1)
+    wanted = jnp.full((slots, n_patch), -1, jnp.int32)
     for k in range(slots):
         wanted = jnp.where(slot == k, patches[0, 0, k], wanted)
     chosen = (wanted == named).astype(BF16)
     per_block = lax.dot_general(
-        bins[...].astype(F32).astype(BF16), chosen, (((1,), (1,)), ((), ())), preferred_element_type=F32
+        chosen, bins[...].astype(F32).astype(BF16), (((1,), (1,)), ((), ())), preferred_element_type=F32
     )
     devices, _, width = level.shape
-    first = lax.broadcasted_iota(jnp.int32, (SUB, width), 0) == 0
+    groups = slots // SUB
+    group = lax.broadcasted_iota(jnp.int32, (SUB, width), 1) // (width // groups)
+    tiles = {}
     for d in range(devices):
         blk = d * width // OBS_BLK
-        line = jnp.broadcast_to(per_block[blk : blk + 1, :width], (SUB, width))
-        level[d, :, :] = jnp.where(first, line, 0.0).astype(BF16)
+        if blk not in tiles:
+            tile = None
+            for g in range(groups):
+                column = per_block[SUB * g : SUB * (g + 1), blk : blk + 1]
+                column = jnp.broadcast_to(column, (SUB, width))
+                tile = column if tile is None else jnp.where(group == g, column, tile)
+            tiles[blk] = tile.astype(BF16)
+        level[d, :, :] = tiles[blk]
+
+    observers, terms = radiation.shape
+
+    def body(k, carry):
+        rows = pl.ds(pl.multiple_of(k * terms, terms), terms)
+        turned_radiation[:, rows] = radiation[rows, :].T
+        return carry
+
+    lax.fori_loop(0, observers // terms, body, 0)
 
 
 def last_early_kernel(
@@ -442,14 +505,13 @@
 
 
 def last_kernel(
-    before, after, walls, spare, part, inner, radiation, pick, early, level, started,
-    out, send, g_out, fields, wide_before, wide_after, sems,
+    far, near, walls, spare, part, inner, radiation, pick, early, level, started,
+    out, send, g_out, fields, wide, sems,
 ):
     planes, ny, _ = walls.shape
     last = planes - 1
-    widen(before, wide_before)
-    widen(after, wide_after)
-    load = loader(planes, ny, None, wide_before, wide_after)
+    widen(far, near, wide)
+    load = loader(planes, ny, None, wide)
     rows, copies = {}, []
     for edge, (plane, first) in enumerate(((0, 18), (last, 0))):
         own = walls[plane, :, :] == 1
@@ -480,21 +542,17 @@
 def bin_kernel(received, signal, hits):
     devices, rows, width = received.shape
     slots = (rows - SUB) // 2
-    lev = received[:, pl.ds(2 * slots, SUB), :].astype(F32)[:, 0, :].astype(BF16)
-    total = devices * slots
-    src = lax.broadcasted_iota(jnp.int32, (total, devices), 0) // slots
-    col = lax.broadcasted_iota(jnp.int32, (total, devices), 1)
-    spread = jnp.dot((src == col).astype(BF16), lev, preferred_element_type=F32)
-    slot = lax.broadcasted_iota(jnp.int32, (total, width), 0) % slots
-    lane = lax.broadcasted_iota(jnp.int32, (total, width), 1)
-    mine = jnp.where(slot == lane, spread, 0.0).astype(BF16)
-    level = jnp.dot(mine, jnp.ones((width, LEVELS), BF16), preferred_element_type=F32)
-    lane = lax.broadcasted_iota(jnp.int32, (total, LEVELS), 1).astype(F32)
-    for step in range(2):
-        hit = (level + float(step) == lane).astype(F32).astype(BF16)
-        hits[:, pl.ds(step * slots, slots), :] = hit.reshape(devices, slots, LEVELS)
-    left = received[:, pl.ds(0, 2 * slots), :].reshape(2 * total, width)
-    right = hits[...].reshape(2 * total, LEVELS)
+    groups = slots // SUB
+    lane = lax.broadcasted_iota(jnp.int32, (slots, LEVELS), 1).astype(F32)
+    for d in range(devices):
+        tile = received[d, pl.ds(2 * slots, SUB), :].astype(F32)
+        starts = [g * (width // groups) for g in range(groups)]
+        level = jnp.concatenate([jnp.broadcast_to(tile[:, k : k + 1], (SUB, LEVELS)) for k in starts], axis=0)
+        for step in range(2):
+            hit = (level == lane - float(step)).astype(F32).astype(BF16)
+            hits[d, pl.ds(step * slots, slots), :] = hit
+    left = received[:, pl.ds(0, 2 * slots), :].reshape(devices * 2 * slots, width)
+    right = hits[...].reshape(devices * 2 * slots, LEVELS)
     signal[...] = lax.dot_general(left, right, (((0,), (0,)), ((), ())), preferred_element_type=F32)
 
 
@@ -505,56 +563,68 @@
     devices = size_x * size_y
     width = radiation.shape[0] // devices
 
-    def exchange(up, down, axis, size):
-        right = [(i, (i + 1) % size) for i in range(size)]
+    def exchange(up, down):
+        right = [(i, (i + 1) % size_y) for i in range(size_y)]
         left = [(j, i) for i, j in right]
-        return lax.ppermute(up, axis, right), lax.ppermute(down, axis, left)
+        return lax.ppermute(up, "gy", right), lax.ppermute(down, "gy", left)
+
+    def swap(far, near):
+        far_pairs = [(i, (i - 1 + 2 * (i % 2)) % size_x) for i in range(size_x)]
+        near_pairs = [(i, i + 1 - 2 * (i % 2)) for i in range(size_x)]
+        return lax.ppermute(far, "gx", far_pairs), lax.ppermute(near, "gx", near_pairs)
 
     dma = pltpu.SemaphoreType.DMA
     block, cells = populations.shape, (planes, ny, nz)
-    beside = (30 * SUB, nz)
+    beside = (20 * SUB, nz)
     up, down = call(
         rows_kernel,
         [HBM] * 3,
         [(VMEM, beside, BF16)] * 2,
-        [pltpu.VMEM(block, F32), pltpu.VMEM(cells, F32), pltpu.VMEM(cells, walls.dtype), dma((9,))],
+        [
+            pltpu.VMEM(block, F32), pltpu.VMEM(cells, F32), pltpu.VMEM(cells, walls.dtype),
+            pltpu.VMEM((2, 29, SUB, nz), F32), dma((9,)),
+        ],
         cost=1 << 20,
         limit=64800000,
     )(populations, omega, walls)
-    before, after = exchange(up, down, "gy", size_y)
-    pick, level = call(
+    before, after = exchange(up, down)
+    pick, level, radiation = call(
         slots_kernel,
-        [VMEM] + [SMEM] * 3,
-        [(VMEM, (nz // LANES, slots, planes * ny), BF16), (VMEM, (devices, SUB, width), BF16)],
-        cost=1 << 18,
-    )(bins.T, counts, sample_site, sample_patch)
+        [VMEM] * 2 + [SMEM] * 3,
+        [
+            (VMEM, (nz // LANES, slots, planes * ny), BF16),
+            (VMEM, (devices, SUB, width), BF16),
+            (VMEM, radiation.shape[::-1], BF16),
+        ],
+        cost=1 << 22,
+    )(bins.T, radiation, counts, sample_site, sample_patch)
     (main,) = call(first_main_kernel, [VMEM] * 3, [(VMEM, block, F32)], cost=1 << 22)(populations, omega, walls)
 
     edge = (planes, SUB, nz)
-    face = (9 * ny + 6 * SUB, nz)
-    faces = [(VMEM, face, BF16)] * 2
-    halo, retain, solid, up, down = call(
+    face, last_face = ((face_rows(ny, reach), nz) for reach in (2, 1))
+    faces, last_faces = ([(VMEM, shape, BF16)] * 2 for shape in (face, last_face))
+    halo, retain, solid, far, near = call(
         first_halo_kernel,
         [VMEM] * 3,
         [(VMEM, (27, *edge), F32), (VMEM, edge, F32), (VMEM, edge, F32), *faces],
         [pltpu.VMEM(beside, F32)] * 2,
         cost=1 << 20,
     )(before, after, main)
-    before, after = exchange(up, down, "gx", size_x)
+    far, near = swap(far, near)
 
     def relaxed(n):
         return [(VMEM, (27, n, ny, nz), F32), (VMEM, (27, n, SUB, nz), F32), (VMEM, (4, n, ny, nz), F32)]
 
     read = pltpu.VMEM((27, ny + SUB, nz), F32)
-    wide = [pltpu.VMEM(face, F32)] * 2
+    wide, last_wide = (pltpu.VMEM((2, *shape), F32) for shape in (face, last_face))
     args = (main, halo, populations, omega, walls, retain, solid)
     main_in, halo_in, macro_in = call(
         middle_inner_kernel, [VMEM] * 7, relaxed(planes - 2), [read], cost=1 << 22
     )(*args)
-    main_out, halo_out, macro_out, up, down = call(
-        middle_outer_kernel, [VMEM] * 10, relaxed(2) + faces, [read, *wide], cost=1 << 22
-    )(*args, before, after, macro_in)
-    before, after = exchange(up, down, "gx", size_x)
+    main_out, halo_out, macro_out, far, near = call(
+        middle_outer_kernel, [VMEM] * 11, relaxed(2) + last_faces, [read, wide], cost=1 << 22
+    )(*args, far, near, macro_in, pick)
+    far, near = swap(far, near)
 
     fields = pltpu.VMEM((4, planes * ny, nz), BF16)
     inner = (4, planes - 2, ny, nz)
@@ -575,10 +645,10 @@
         last_kernel,
         [VMEM] * 10 + [HBM],
         [(HBM, block, F32), (VMEM, (devices, 2 * slots + SUB, width), BF16)],
-        [pltpu.VMEM((9, 2, ny, nz), F32), fields, *wide, dma((2,))],
+        [pltpu.VMEM((9, 2, ny, nz), F32), fields, last_wide, dma((2,))],
         aliases={10: 0},
         cost=1 << 22,
-    )(before, after, walls, spare, part, inner, radiation, pick, early, level, started)
+    )(far, near, walls, spare, part, inner, radiation, pick, early, level, started)
     received = lax.all_to_all(send, ("gx", "gy"), 0, 0, tiled=True)
     (signal,) = call(
         bin_kernel, [VMEM], [(VMEM, (width, LEVELS), F32)], [pltpu.VMEM((devices, 2 * slots, LEVELS), BF16)], cost=1 << 20

time: 48.1 us -> 46.2 us (0.960)
  starting transfers between devices: 12 us -> 9.7 us
  blocking collectives: 16.2 us -> 15.3 us
  waiting for transfers between devices: 6.32 us -> 7.21 us
  Pallas kernels: 11.9 us -> 12.4 us
    ppermute x6, starting transfers between devices: 12 us -> 9.7 us  [the longest x2 7.2 us: swap(): lax.ppermute(far, 'gx', far_pairs)]
    pallas_call x2, Pallas kernels: 1.82 us -> 3.55 us  [the longest x1 2.4 us: per_device(): call(slots_kernel, [VMEM] * 2 + [SMEM] * 3, [(VMEM, (nz // LANES, slots,...]
    all_to_all x1, blocking collectives: 16.2 us -> 15.3 us  [per_device(): received = lax.all_to_all(send, ('gx', 'gy'), 0, 0, tiled=True)]
    ppermute x6, waiting for transfers between devices: 6.32 us -> 7.21 us  [the longest x2 3.02 us: swap(): lax.ppermute(far, 'gx', far_pairs)]
    pallas_call x1, Pallas kernels: 0.7 us -> 0.21 us  [per_device(): call(first_halo_kernel, [VMEM] * 3, [(VMEM, (27, *edge), F32), (VMEM, edg...]
    pallas_call x1, Pallas kernels: 1.46 us -> 0.97 us  [per_device(): call(last_kernel, [VMEM] * 10 + [HBM], [(HBM, block, F32), (VMEM, (device...]
  transfers between devices with their start and end apart: 6 -> 6, of which waited for: 4 -> 5; matrix products, arithmetic and copies ran while one was open for 0% -> 0% of each run, Pallas kernels for 11% -> 14%
where the time goes in v2:
time: 46.2 us; the launch traced here: 46.1 us
  blocking collectives  15.3 us (33%)
  Pallas kernels  12.4 us (27%)
  starting transfers between devices  9.7 us (21%)
  waiting for transfers between devices  7.21 us (16%)
  between operations  1.44 us (3%)
    all_to_all x1, blocking collectives, per_device(): received = lax.all_to_all(send, ('gx', 'gy'), 0, 0, tiled=True)  15.3 us
    ppermute x2, starting transfers between devices, swap(): lax.ppermute(far, 'gx', far_pairs)  7.2 us
    ppermute x2, waiting for transfers between devices, swap(): lax.ppermute(far, 'gx', far_pairs)  3.02 us
    pallas_call x1, Pallas kernels, per_device(): call(rows_kernel, [HBM] * 3, [(VMEM, beside, BF16)] * 2, [pltpu.VMEM(bloc...  2.61 us
    ppermute x2, starting transfers between devices, exchange(): return (lax.ppermute(up, 'gy', right), lax.ppermute(down, 'gy', left))  2.49 us
    pallas_call x1, Pallas kernels, per_device(): call(slots_kernel, [VMEM] * 2 + [SMEM] * 3, [(VMEM, (nz // LANES, slots,...  2.4 us
    ppermute x2, waiting for transfers between devices, swap(): lax.ppermute(near, 'gx', near_pairs)  2.23 us
    ppermute x2, waiting for transfers between devices, exchange(): return (lax.ppermute(up, 'gy', right), lax.ppermute(down, 'gy', left))  1.96 us
  transfers between devices with their start and end apart: 6, of which 5 were waited for; matrix products, arithmetic and copies ran while one was open for 0% of the time, Pallas kernels for 14%

profile of v2, /device:TPU:0, one launch (start us, length us, event | category | flops | bytes accessed | tf_op | source)
XLA Modules:
  0.0 46.1 jit_solution(8524511215372265844)
XLA Ops:
  0.6 0.0 copy-start.2
  0.6 0.0 copy-start
  0.6 0.0 copy-start.3
  0.7 2.6 %shard_map.96 = (bf16[160,256]{1,0:T(8,128)(2,1)}, bf16[160,256]{1,0:T(8,128)(2,1)}) custom-call(f32[27,4,16,256]{3,2,1,0:T(8,128)} %pops.7, f32[4,16,256]{2,1,0:T(8,128)} %omega.5, s32[4,16,256]{2,1,0:T(8,128)} %walls.9), custom_call_target="tpu_custom_call" | custom-call | flops 1048576 | bytes 1048576 | tf_op jit(solution)/shard_map/pallas_call | solution.py:579
  3.3 0.5 %collective-permute-start = (bf16[160,256]{1,0:T(8,128)(2,1)}, bf16[160,256]{1,0:T(8,128)(2,1)S(1)}, u32[]{:S(2)}, u32[]{:S(2)}) collective-permute-start(bf16[160,256]{1,0:T(8,128)(2,1)} %get-tuple-element.27), channel_id=1, source_target_pairs={{0,1},{1,2},{2,3},{3,0},{4,5},{5,6},{6,7},{7,4},{8,9},{9,10},{10,1... | collective-permute-start | bytes 245768 | tf_op jit(solution)/shard_map/ppermute | solution.py:569
  3.8 2.0 %collective-permute-start.1 = (bf16[160,256]{1,0:T(8,128)(2,1)}, bf16[160,256]{1,0:T(8,128)(2,1)S(1)}, u32[]{:S(2)}, u32[]{:S(2)}) collective-permute-start(bf16[160,256]{1,0:T(8,128)(2,1)} %get-tuple-element.28), channel_id=1, source_target_pairs={{1,0},{2,1},{3,2},{0,3},{5,4},{6,5},{7,6},{4,7},{9,8},{10,9},{11,1... | collective-permute-start | bytes 245768 | tf_op jit(solution)/shard_map/ppermute | solution.py:569
  5.8 0.0 copy-done.2
  5.8 0.0 copy-done
  5.8 0.0 copy-done.3
  5.8 1.1 %shard_map.95.main = f32[27,4,16,256]{3,2,1,0:T(8,128)S(1)} custom-call(f32[27,4,16,256]{3,2,1,0:T(8,128)S(1)} %copy-done, f32[4,16,256]{2,1,0:T(8,128)S(1)} %copy-done.3, s32[4,16,256]{2,1,0:T(8,128)S(1)} %copy-done.2), custom_call_target="tpu_custom_call" | custom-call | flops 4194304 | bytes 4194304 | tf_op jit(solution)/shard_map/pallas_call | solution.py:601
  6.8 0.0 copy-start.4
  6.9 0.0 copy-start.5
  6.9 0.0 copy-start.6
  6.9 1.2 %collective-permute-done.before = bf16[160,256]{1,0:T(8,128)(2,1)S(1)} collective-permute-done((bf16[160,256]{1,0:T(8,128)(2,1)}, bf16[160,256]{1,0:T(8,128)(2,1)S(1)}, u32[]{:S(2)}, u32[]{:S(2)}) %collective-permute-start) | collective-permute-done | bytes 81952 | tf_op jit(solution)/shard_map/ppermute | solution.py:569
  8.0 0.8 %collective-permute-done.1.after = bf16[160,256]{1,0:T(8,128)(2,1)S(1)} collective-permute-done((bf16[160,256]{1,0:T(8,128)(2,1)}, bf16[160,256]{1,0:T(8,128)(2,1)S(1)}, u32[]{:S(2)}, u32[]{:S(2)}) %collective-permute-start.1) | collective-permute-done | bytes 81952 | tf_op jit(solution)/shard_map/ppermute | solution.py:569
  8.8 0.2 shard_map.97
  9.1 4.7 %collective-permute-start.2 = (bf16[176,256]{1,0:T(8,128)(2,1)S(1)}, bf16[176,256]{1,0:T(8,128)(2,1)S(1)}, u32[]{:S(2)}, u32[]{:S(2)}) collective-permute-start(bf16[176,256]{1,0:T(8,128)(2,1)S(1)} %get-tuple-element.32), channel_id=1, source_target_pairs={{0,28},{4,8},{8,4},{12,16},{16,12},{20,24},{24,20},{28,0},{1,29},{... | collective-permute-start | bytes 270344 | tf_op jit(solution)/shard_map/ppermute | solution.py:574
  13.7 0.0 collective-permute-start.3
  14.4 0.0 copy-done.1
  14.4 2.4 %shard_map.99 = (bf16[2,16,64]{2,1,0:T(8,128)(2,1)S(1)}, bf16[32,8,128]{2,1,0:T(8,128)(2,1)S(1)}, bf16[512,4096]{1,0:T(8,128)(2,1)S(1)}) custom-call(s32[32,128]{1,0:T(8,128)S(1)} %bitcast.1, bf16[4096,512]{1,0:T(8,128)(2,1)S(1)} %copy-done.1, s32[1,1]{1,0:T(1,128)S(6)} %copy.12.counts, s32[1,1,16]{2,1,0:T(1,128)S(1)} %copy-done.5, s32[1,1,16]{2,1,0:T(1,128)S(1)} %copy-done.6), custom_call_target="tpu_custom_call" | custom-call | flops 4194304 | bytes 4194304 | tf_op jit(solution)/shard_map/pallas_call | solution.py:591
  16.8 1.1 %shard_map.98 = (f32[27,2,16,256]{3,2,1,0:T(8,128)S(1)}, f32[27,2,8,256]{3,2,1,0:T(8,128)S(1)}, f32[4,2,16,256]{3,2,1,0:T(8,128)S(1)}) custom-call(f32[27,4,16,256]{3,2,1,0:T(8,128)S(1)} %shard_map.95.main, f32[27,4,8,256]{3,2,1,0:T(8,128)S(1)} %get-tuple-element.29.halo, f32[27,4,16,256]{3,2,1,0:T(8,128)S(1)} %copy-done, f32[4,16,256]{2,1,0:T(8,128)S(1)} %copy-done.3, ...), custom_call_target="tpu_custom_call" | custom-call | flops 4194304 | bytes 4194304 | tf_op jit(solution)/shard_map/pallas_call | solution.py:621
  17.9 0.0 collective-permute-done.2.far
  17.9 1.0 %collective-permute-done.3.near = bf16[176,256]{1,0:T(8,128)(2,1)S(1)} collective-permute-done((bf16[176,256]{1,0:T(8,128)(2,1)S(1)}, bf16[176,256]{1,0:T(8,128)(2,1)S(1)}, u32[]{:S(2)}, u32[]{:S(2)}) %collective-permute-start.3) | collective-permute-done | bytes 90144 | tf_op jit(solution)/shard_map/ppermute | solution.py:574
  18.9 1.1 %shard_map.100 = (f32[27,2,16,256]{3,2,1,0:T(8,128)S(1)}, f32[27,2,8,256]{3,2,1,0:T(8,128)S(1)}, f32[4,2,16,256]{3,2,1,0:T(8,128)S(1)}, bf16[160,256]{1,0:T(8,128)(2,1)S(1)}, bf16[160,256]{1,0:T(8,128)(2,1)S(1)}) custom-call(f32[27,4,16,256]{3,2,1,0:T(8,128)S(1)} %shard_map.95.main, f32[27,4,8,256]{3,2,1,0:T(8,128)S(1)} %get-tuple-element.29.halo, ...), custom_call_target="tpu_custom_call" | custom-call | flops 4194304 | bytes 4194304 | tf_op jit(solution)/shard_map/pallas_call | solution.py:624
  20.1 2.5 %collective-permute-start.4 = (bf16[160,256]{1,0:T(8,128)(2,1)S(1)}, bf16[160,256]{1,0:T(8,128)(2,1)S(1)}, u32[]{:S(2)}, u32[]{:S(2)}) collective-permute-start(bf16[160,256]{1,0:T(8,128)(2,1)S(1)} %get-tuple-element.36), channel_id=1, source_target_pairs={{0,28},{4,8},{8,4},{12,16},{16,12},{20,24},{24,20},{28,0},{1,29},{... | collective-permute-start | bytes 245768 | tf_op jit(solution)/shard_map/ppermute | solution.py:574
  22.6 0.0 collective-permute-start.5
  22.6 1.9 %shard_map.101 = (f32[27,4,16,256]{3,2,1,0:T(8,128)}, f32[2,9,16,256]{3,2,1,0:T(8,128)S(1)}, f32[4,2,16,256]{3,2,1,0:T(8,128)S(1)}, f32[4,2,16,256]{3,2,1,0:T(8,128)S(1)}, bf16[32,16,128]{2,1,0:T(8,128)(2,1)S(1)}) custom-call(f32[27,2,16,256]{3,2,1,0:T(8,128)S(1)} %get-tuple-element.38.main_in, f32[27,2,8,256]{3,2,1,0:T(8,128)S(1)} %get-tuple-element.39.halo_in, ...), custom_call_target="tpu_custom_call" | custom-call | flops 4194304 | bytes 4194304 | tf_op jit(solution)/shard_map/pallas_call | solution.py:631
  24.6 3.0 %collective-permute-done.4.far = bf16[160,256]{1,0:T(8,128)(2,1)S(1)} collective-permute-done((bf16[160,256]{1,0:T(8,128)(2,1)S(1)}, bf16[160,256]{1,0:T(8,128)(2,1)S(1)}, u32[]{:S(2)}, u32[]{:S(2)}) %collective-permute-start.4) | collective-permute-done | bytes 81952 | tf_op jit(solution)/shard_map/ppermute | solution.py:574
  27.6 1.2 %collective-permute-done.5.near = bf16[160,256]{1,0:T(8,128)(2,1)S(1)} collective-permute-done((bf16[160,256]{1,0:T(8,128)(2,1)S(1)}, bf16[160,256]{1,0:T(8,128)(2,1)S(1)}, u32[]{:S(2)}, u32[]{:S(2)}) %collective-permute-start.5) | collective-permute-done | bytes 81952 | tf_op jit(solution)/shard_map/ppermute | solution.py:574
  28.8 1.0 %shard_map.102 = (f32[27,4,16,256]{3,2,1,0:T(8,128)}, bf16[32,40,128]{2,1,0:T(8,128)(2,1)S(1)}) custom-call(bf16[160,256]{1,0:T(8,128)(2,1)S(1)} %collective-permute-done.4.far, bf16[160,256]{1,0:T(8,128)(2,1)S(1)} %collective-permute-done.5.near, s32[4,16,256]{2,1,0:T(8,128)S(1)} %copy-done.2, ...), custom_call_target="tpu_custom_call", output_to_operand_aliasing={{0}: (10, {})} | custom-call | flops 4194304 | bytes 4194304 | tf_op jit(solution)/shard_map/pallas_call | solution.py:644
  29.8 15.3 %all_to_all.5.received = bf16[32,40,128]{2,1,0:T(8,128)(2,1)S(1)} all-to-all(bf16[32,40,128]{2,1,0:T(8,128)(2,1)S(1)} %get-tuple-element.51), channel_id=1, replica_groups=mesh['gx'=8,'gy'=4] {'gx','gy'}, dimensions={0} | all-to-all | bytes 655360 | tf_op jit(solution)/shard_map/all_to_all | solution.py:652
  45.1 1.0 %shard_map.103 = f32[128,128]{1,0:T(8,128)} custom-call(bf16[32,40,128]{2,1,0:T(8,128)(2,1)S(1)} %all_to_all.5.received), custom_call_target="tpu_custom_call" | custom-call | flops 1048576 | bytes 1048576 | tf_op jit(solution)/shard_map/pallas_call | solution.py:653
  (4 shorter events, 0.0 us)
Async XLA Ops:
  0.6 5.1 %copy-start.2 = (s32[4,16,256]{2,1,0:T(8,128)S(1)}, s32[4,16,256]{2,1,0:T(8,128)}, u32[]{:S(2)}) copy-start(s32[4,16,256]{2,1,0:T(8,128)} %walls.9) | copy-start | bytes 196612
  0.6 5.1 %copy-start = (f32[27,4,16,256]{3,2,1,0:T(8,128)S(1)}, f32[27,4,16,256]{3,2,1,0:T(8,128)}, u32[]{:S(2)}) copy-start(f32[27,4,16,256]{3,2,1,0:T(8,128)} %pops.7) | copy-start | bytes 5308420
  0.6 5.1 %copy-start.3 = (f32[4,16,256]{2,1,0:T(8,128)S(1)}, f32[4,16,256]{2,1,0:T(8,128)}, u32[]{:S(2)}) copy-start(f32[4,16,256]{2,1,0:T(8,128)} %omega.5) | copy-start | bytes 196612
  3.3 4.8 %collective-permute-start = (bf16[160,256]{1,0:T(8,128)(2,1)}, bf16[160,256]{1,0:T(8,128)(2,1)S(1)}, u32[]{:S(2)}, u32[]{:S(2)}) collective-permute-start(bf16[160,256]{1,0:T(8,128)(2,1)} %get-tuple-element.27), channel_id=1, source_target_pairs={{0,1},{1,2},{2,3},{3,0},{4,5},{5,6},{6,7},{7,4},{8,9},{9,10},{10,1... | collective-permute-start | bytes 245768 | tf_op jit(solution)/shard_map/ppermute | solution.py:569
  3.8 5.1 %collective-permute-start.1 = (bf16[160,256]{1,0:T(8,128)(2,1)}, bf16[160,256]{1,0:T(8,128)(2,1)S(1)}, u32[]{:S(2)}, u32[]{:S(2)}) collective-permute-start(bf16[160,256]{1,0:T(8,128)(2,1)} %get-tuple-element.28), channel_id=1, source_target_pairs={{1,0},{2,1},{3,2},{0,3},{5,4},{6,5},{7,6},{4,7},{9,8},{10,9},{11,1... | collective-permute-start | bytes 245768 | tf_op jit(solution)/shard_map/ppermute | solution.py:569
  5.8 8.6 %copy-start.1 = (bf16[4096,512]{1,0:T(8,128)(2,1)S(1)}, bf16[4096,512]{1,0:T(8,128)(2,1)}, u32[]{:S(2)}) copy-start(bf16[4096,512]{1,0:T(8,128)(2,1)} %radiation.1) | copy-start | bytes 12582916
  6.8 7.6 %copy-start.4 = (s32[128,32]{0,1:T(8,128)S(1)}, s32[128,32]{0,1:T(8,128)}, u32[]{:S(2)}) copy-start(s32[128,32]{0,1:T(8,128)} %param.12) | copy-start | bytes 49156
  6.9 7.6 %copy-start.5 = (s32[1,1,16]{2,1,0:T(1,128)S(1)}, s32[1,1,16]{2,1,0:T(1,128)}, u32[]{:S(2)}) copy-start(s32[1,1,16]{2,1,0:T(1,128)} %sites.1) | copy-start | bytes 196
  6.9 7.6 %copy-start.6 = (s32[1,1,16]{2,1,0:T(1,128)S(1)}, s32[1,1,16]{2,1,0:T(1,128)}, u32[]{:S(2)}) copy-start(s32[1,1,16]{2,1,0:T(1,128)} %patches.1) | copy-start | bytes 196
  9.1 8.9 %collective-permute-start.2 = (bf16[176,256]{1,0:T(8,128)(2,1)S(1)}, bf16[176,256]{1,0:T(8,128)(2,1)S(1)}, u32[]{:S(2)}, u32[]{:S(2)}) collective-permute-start(bf16[176,256]{1,0:T(8,128)(2,1)S(1)} %get-tuple-element.32), channel_id=1, source_target_pairs={{0,28},{4,8},{8,4},{12,16},{16,12},{20,24},{24,20},{28,0},{1,29},{... | collective-permute-start | bytes 270344 | tf_op jit(solution)/shard_map/ppermute | solution.py:574
  13.7 5.2 %collective-permute-start.3 = (bf16[176,256]{1,0:T(8,128)(2,1)S(1)}, bf16[176,256]{1,0:T(8,128)(2,1)S(1)}, u32[]{:S(2)}, u32[]{:S(2)}) collective-permute-start(bf16[176,256]{1,0:T(8,128)(2,1)S(1)} %get-tuple-element.33), channel_id=1, source_target_pairs={{0,4},{4,0},{8,12},{12,8},{16,20},{20,16},{24,28},{28,24},{1,5},{5... | collective-permute-start | bytes 270344 | tf_op jit(solution)/shard_map/ppermute | solution.py:574
  20.1 7.5 %collective-permute-start.4 = (bf16[160,256]{1,0:T(8,128)(2,1)S(1)}, bf16[160,256]{1,0:T(8,128)(2,1)S(1)}, u32[]{:S(2)}, u32[]{:S(2)}) collective-permute-start(bf16[160,256]{1,0:T(8,128)(2,1)S(1)} %get-tuple-element.36), channel_id=1, source_target_pairs={{0,28},{4,8},{8,4},{12,16},{16,12},{20,24},{24,20},{28,0},{1,29},{... | collective-permute-start | bytes 245768 | tf_op jit(solution)/shard_map/ppermute | solution.py:574
  22.6 6.2 %collective-permute-start.5 = (bf16[160,256]{1,0:T(8,128)(2,1)S(1)}, bf16[160,256]{1,0:T(8,128)(2,1)S(1)}, u32[]{:S(2)}, u32[]{:S(2)}) collective-permute-start(bf16[160,256]{1,0:T(8,128)(2,1)S(1)} %get-tuple-element.37), channel_id=1, source_target_pairs={{0,4},{4,0},{8,12},{12,8},{16,20},{20,16},{24,28},{28,24},{1,5},{5... | collective-permute-start | bytes 245768 | tf_op jit(solution)/shard_map/ppermute | solution.py:574

commit v3 on v2

--- a/solution.py
+++ b/solution.py
@@ -143,6 +143,16 @@
     return out, (rho, jx, jy, jz)
 
 
+def odd_block(axis):
+    return lax.rem(lax.axis_index(axis), 2)
+
+
+def widen(far, near, wide, axis):
+    odd = odd_block(axis)
+    wide[odd, :, :] = far[...].astype(F32)
+    wide[1 - odd, :, :] = near[...].astype(F32)
+
+
 def start_all(copies):
     for copy in copies:
         copy.start()
@@ -155,7 +165,7 @@
     return both, [i for i in range(27) if STEP[i][1] != outward]
 
 
-def rows_kernel(pops_in, omega_in, walls_in, up, down, pops, omega, walls, packed, sems):
+def rows_kernel(pops_in, omega_in, walls_in, far, near, pops, omega, walls, packed, faces, sems):
     planes, ny, nz = omega.shape
     row = lax.broadcasted_iota(jnp.int32, (SUB, nz), 0)
     chunk = 4
@@ -193,7 +203,7 @@
         if i % chunk == 0:
             copies[i // chunk].wait()
         pack(i)
-    for side, out in ((0, up), (1, down)):
+    for side in range(2):
         for part in range(nz // LANES):
             cols = pl.ds(LANES * part, LANES)
             closed = packed[side, 28, :, cols] > 0.5
@@ -209,8 +219,11 @@
             at_edge = row % 2 == 1 - side
             tiles.append(jnp.where(at_edge, one, pltpu.roll(two, SUB - 1 if side == 0 else 1, 0)))
         tiles.append(jnp.zeros((SUB, nz), F32))
-        for k in range(0, len(tiles), 2):
-            out[pl.ds(SUB * k, 2 * SUB), :] = jnp.concatenate(tiles[k : k + 2], axis=0).astype(BF16)
+        for k, tile in enumerate(tiles):
+            faces[side, pl.ds(SUB * k, SUB), :] = tile
+    odd = odd_block("gy")
+    far[...] = faces[1 - odd, :, :].astype(BF16)
+    near[...] = faces[odd, :, :].astype(BF16)
 
 
 def first_main_kernel(pops, omega, walls, post):
@@ -262,21 +275,16 @@
     out[pl.ds(9 * ny, SUB * len(tiles)), :] = jnp.concatenate(tiles, axis=0).astype(BF16)
 
 
-def odd_block():
-    return lax.rem(lax.axis_index("gx"), 2)
-
-
 def pack_faces(main, halo, last, reach, far, near):
-    odd = odd_block()
+    odd = odd_block("gx")
     pack_x(main, halo, odd * last, odd * 18, reach, far)
     pack_x(main, halo, (1 - odd) * last, (1 - odd) * 18, reach, near)
 
 
-def first_halo_kernel(before, after, main, halo, retain, solid, send_far, send_near, wide_before, wide_after):
+def first_halo_kernel(far, near, main, halo, retain, solid, send_far, send_near, wide):
     _, planes, _, nz = halo.shape
     row = lax.broadcasted_iota(jnp.int32, (SUB, nz), 0)
-    wide_before[...] = before[...].astype(F32)
-    wide_after[...] = after[...].astype(F32)
+    widen(far, near, wide, "gy")
 
     def received(side, group, plane):
         both, edge = rows_order(side)
@@ -288,7 +296,7 @@
             k = edge.index(group)
             tile = len(both) + k // 2
             turn += (k % 2) * (1 - 2 * side)
-        value = (wide_before, wide_after)[side][pl.ds(SUB * tile, SUB), :]
+        value = wide[side, pl.ds(SUB * tile, SUB), :]
         return pltpu.roll(value, turn % SUB, 0) if turn % SUB else value
 
     def beside(group, plane):
@@ -314,12 +322,6 @@
 def pull(load, i, plane):
     value = turned(load(i, plane - STEP[i][0]), i)
     return jnp.where(value > LIMIT, load(26 - i, plane), value)
-
-
-def widen(far, near, wide):
-    odd = odd_block()
-    wide[odd, :, :] = far[...].astype(F32)
-    wide[1 - odd, :, :] = near[...].astype(F32)
 
 
 def loader(planes, ny, places, wide=None):
@@ -384,7 +386,7 @@
     main2, halo2, macro, send_far, send_near, read, wide,
 ):
     planes, ny, _ = omega.shape
-    widen(far, near, wide)
+    widen(far, near, wide, "gx")
     load = loader(planes, ny, [(main, halo, p) for p in range(planes)], wide)
     middle((0, planes - 1), load, pops, omega, walls, retain, solid, main2, halo2, macro, read)
     pack_faces(main2, halo2, 1, 1, send_far, send_near)
@@ -510,7 +512,7 @@
 ):
     planes, ny, _ = walls.shape
     last = planes - 1
-    widen(far, near, wide)
+    widen(far, near, wide, "gx")
     load = loader(planes, ny, None, wide)
     rows, copies = {}, []
     for edge, (plane, first) in enumerate(((0, 18), (last, 0))):
@@ -563,31 +565,26 @@
     devices = size_x * size_y
     width = radiation.shape[0] // devices
 
-    def exchange(up, down):
-        right = [(i, (i + 1) % size_y) for i in range(size_y)]
-        left = [(j, i) for i, j in right]
-        return lax.ppermute(up, "gy", right), lax.ppermute(down, "gy", left)
-
-    def swap(far, near):
-        far_pairs = [(i, (i - 1 + 2 * (i % 2)) % size_x) for i in range(size_x)]
-        near_pairs = [(i, i + 1 - 2 * (i % 2)) for i in range(size_x)]
-        return lax.ppermute(far, "gx", far_pairs), lax.ppermute(near, "gx", near_pairs)
+    def swap(far, near, axis, size):
+        far_pairs = [(i, (i - 1 + 2 * (i % 2)) % size) for i in range(size)]
+        near_pairs = [(i, i + 1 - 2 * (i % 2)) for i in range(size)]
+        return lax.ppermute(far, axis, far_pairs), lax.ppermute(near, axis, near_pairs)
 
     dma = pltpu.SemaphoreType.DMA
     block, cells = populations.shape, (planes, ny, nz)
     beside = (20 * SUB, nz)
-    up, down = call(
+    far, near = call(
         rows_kernel,
         [HBM] * 3,
         [(VMEM, beside, BF16)] * 2,
         [
             pltpu.VMEM(block, F32), pltpu.VMEM(cells, F32), pltpu.VMEM(cells, walls.dtype),
-            pltpu.VMEM((2, 29, SUB, nz), F32), dma((9,)),
+            pltpu.VMEM((2, 29, SUB, nz), F32), pltpu.VMEM((2, *beside), F32), dma((9,)),
         ],
         cost=1 << 20,
         limit=64800000,
     )(populations, omega, walls)
-    before, after = exchange(up, down)
+    far, near = swap(far, near, "gy", size_y)
     pick, level, radiation = call(
         slots_kernel,
         [VMEM] * 2 + [SMEM] * 3,
@@ -607,10 +604,10 @@
         first_halo_kernel,
         [VMEM] * 3,
         [(VMEM, (27, *edge), F32), (VMEM, edge, F32), (VMEM, edge, F32), *faces],
-        [pltpu.VMEM(beside, F32)] * 2,
+        [pltpu.VMEM((2, *beside), F32)],
         cost=1 << 20,
-    )(before, after, main)
-    far, near = swap(far, near)
+    )(far, near, main)
+    far, near = swap(far, near, "gx", size_x)
 
     def relaxed(n):
         return [(VMEM, (27, n, ny, nz), F32), (VMEM, (27, n, SUB, nz), F32), (VMEM, (4, n, ny, nz), F32)]
@@ -624,7 +621,7 @@
     main_out, halo_out, macro_out, far, near = call(
         middle_outer_kernel, [VMEM] * 11, relaxed(2) + last_faces, [read, wide], cost=1 << 22
     )(*args, far, near, macro_in, pick)
-    far, near = swap(far, near)
+    far, near = swap(far, near, "gx", size_x)
 
     fields = pltpu.VMEM((4, planes * ny, nz), BF16)
     inner = (4, planes - 2, ny, nz)

time: 46.2 us -> 45.9 us (level)
  waiting for transfers between devices: 7.21 us -> 5.37 us
  starting transfers between devices: 9.7 us -> 11.2 us
    ppermute x6, waiting for transfers between devices: 7.21 us -> 5.37 us  [the longest x3 4.13 us: swap(): lax.ppermute(far, axis, far_pairs)]
    ppermute x6, starting transfers between devices: 9.7 us -> 11.2 us  [the longest x3 10.5 us: swap(): lax.ppermute(far, axis, far_pairs)]
  transfers between devices with their start and end apart: 6 -> 6, of which waited for: 5 -> 4; matrix products, arithmetic and copies ran while one was open for 0% -> 0% of each run, Pallas kernels for 14% -> 14%
where the time goes in v3:
time: 45.9 us; the launch traced here: 45.8 us
  blocking collectives  15.3 us (33%)
  Pallas kernels  12.4 us (27%)
  starting transfers between devices  11.2 us (24%)
  waiting for transfers between devices  5.37 us (12%)
  between operations  1.44 us (3%)
    all_to_all x1, blocking collectives, per_device(): received = lax.all_to_all(send, ('gx', 'gy'), 0, 0, tiled=True)  15.3 us
    ppermute x3, starting transfers between devices, swap(): lax.ppermute(far, axis, far_pairs)  10.5 us
    ppermute x3, waiting for transfers between devices, swap(): lax.ppermute(far, axis, far_pairs)  4.13 us
    pallas_call x1, Pallas kernels, per_device(): call(rows_kernel, [HBM] * 3, [(VMEM, beside, BF16)] * 2, [pltpu.VMEM(bloc...  2.65 us
    pallas_call x1, Pallas kernels, per_device(): call(slots_kernel, [VMEM] * 2 + [SMEM] * 3, [(VMEM, (nz // LANES, slots,...  2.4 us
    pallas_call x1, Pallas kernels, per_device(): call(last_early_kernel, [VMEM] * 10, [(HBM, block, F32), (VMEM, (2, 9, ny...  1.94 us
    ppermute x3, waiting for transfers between devices, swap(): lax.ppermute(near, axis, near_pairs)  1.24 us
    pallas_call x1, Pallas kernels, per_device(): call(middle_outer_kernel, [VMEM] * 11, relaxed(2) + last_faces, [read, wi...  1.14 us
  transfers between devices with their start and end apart: 6, of which 4 were waited for; matrix products, arithmetic and copies ran while one was open for 0% of the time, Pallas kernels for 14%

profile of v3, /device:TPU:0, one launch (start us, length us, event | category | flops | bytes accessed | tf_op | source)
XLA Modules:
  0.0 45.8 jit_solution(16317128300886511133)
XLA Ops:
  0.6 0.0 copy-start.2
  0.6 0.0 copy-start
  0.6 0.0 copy-start.3
  0.7 2.7 %shard_map.96 = (bf16[160,256]{1,0:T(8,128)(2,1)}, bf16[160,256]{1,0:T(8,128)(2,1)}) custom-call(f32[27,4,16,256]{3,2,1,0:T(8,128)} %pops.7, f32[4,16,256]{2,1,0:T(8,128)} %omega.5, s32[4,16,256]{2,1,0:T(8,128)} %walls.9), custom_call_target="tpu_custom_call" | custom-call | flops 1048576 | bytes 1048576 | tf_op jit(solution)/shard_map/pallas_call | solution.py:576
  3.3 2.4 %collective-permute-start = (bf16[160,256]{1,0:T(8,128)(2,1)}, bf16[160,256]{1,0:T(8,128)(2,1)S(1)}, u32[]{:S(2)}, u32[]{:S(2)}) collective-permute-start(bf16[160,256]{1,0:T(8,128)(2,1)} %get-tuple-element.27), channel_id=1, source_target_pairs={{0,3},{1,2},{2,1},{3,0},{4,7},{5,6},{6,5},{7,4},{8,11},{9,10},{10,... | collective-permute-start | bytes 245768 | tf_op jit(solution)/shard_map/ppermute | solution.py:571
  5.8 0.7 %collective-permute-start.1 = (bf16[160,256]{1,0:T(8,128)(2,1)}, bf16[160,256]{1,0:T(8,128)(2,1)S(1)}, u32[]{:S(2)}, u32[]{:S(2)}) collective-permute-start(bf16[160,256]{1,0:T(8,128)(2,1)} %get-tuple-element.28), channel_id=1, source_target_pairs={{0,1},{1,0},{2,3},{3,2},{4,5},{5,4},{6,7},{7,6},{8,9},{9,8},{10,11... | collective-permute-start | bytes 245768 | tf_op jit(solution)/shard_map/ppermute | solution.py:571
  6.4 0.0 copy-done.2
  6.4 0.0 copy-done
  6.4 0.0 copy-done.3
  6.5 1.1 %shard_map.95.main = f32[27,4,16,256]{3,2,1,0:T(8,128)S(1)} custom-call(f32[27,4,16,256]{3,2,1,0:T(8,128)S(1)} %copy-done, f32[4,16,256]{2,1,0:T(8,128)S(1)} %copy-done.3, s32[4,16,256]{2,1,0:T(8,128)S(1)} %copy-done.2), custom_call_target="tpu_custom_call" | custom-call | flops 4194304 | bytes 4194304 | tf_op jit(solution)/shard_map/pallas_call | solution.py:598
  7.5 0.0 copy-start.4
  7.5 0.0 copy-start.5
  7.5 0.0 copy-start.6
  7.6 1.4 %collective-permute-done.far = bf16[160,256]{1,0:T(8,128)(2,1)S(1)} collective-permute-done((bf16[160,256]{1,0:T(8,128)(2,1)}, bf16[160,256]{1,0:T(8,128)(2,1)S(1)}, u32[]{:S(2)}, u32[]{:S(2)}) %collective-permute-start) | collective-permute-done | bytes 81952 | tf_op jit(solution)/shard_map/ppermute | solution.py:571
  8.9 0.0 collective-permute-done.1.near
  8.9 0.2 shard_map.97
  9.1 5.5 %collective-permute-start.2 = (bf16[176,256]{1,0:T(8,128)(2,1)S(1)}, bf16[176,256]{1,0:T(8,128)(2,1)S(1)}, u32[]{:S(2)}, u32[]{:S(2)}) collective-permute-start(bf16[176,256]{1,0:T(8,128)(2,1)S(1)} %get-tuple-element.32), channel_id=1, source_target_pairs={{0,28},{4,8},{8,4},{12,16},{16,12},{20,24},{24,20},{28,0},{1,29},{... | collective-permute-start | bytes 270344 | tf_op jit(solution)/shard_map/ppermute | solution.py:571
  14.6 0.0 collective-permute-start.3
  15.3 0.0 copy-done.1
  15.3 2.4 %shard_map.99 = (bf16[2,16,64]{2,1,0:T(8,128)(2,1)S(1)}, bf16[32,8,128]{2,1,0:T(8,128)(2,1)S(1)}, bf16[512,4096]{1,0:T(8,128)(2,1)S(1)}) custom-call(s32[32,128]{1,0:T(8,128)S(1)} %bitcast.1, bf16[4096,512]{1,0:T(8,128)(2,1)S(1)} %copy-done.1, s32[1,1]{1,0:T(1,128)S(6)} %copy.12.counts, s32[1,1,16]{2,1,0:T(1,128)S(1)} %copy-done.5, s32[1,1,16]{2,1,0:T(1,128)S(1)} %copy-done.6), custom_call_target="tpu_custom_call" | custom-call | flops 4194304 | bytes 4194304 | tf_op jit(solution)/shard_map/pallas_call | solution.py:588
  17.7 1.1 %shard_map.98 = (f32[27,2,16,256]{3,2,1,0:T(8,128)S(1)}, f32[27,2,8,256]{3,2,1,0:T(8,128)S(1)}, f32[4,2,16,256]{3,2,1,0:T(8,128)S(1)}) custom-call(f32[27,4,16,256]{3,2,1,0:T(8,128)S(1)} %shard_map.95.main, f32[27,4,8,256]{3,2,1,0:T(8,128)S(1)} %get-tuple-element.29.halo, f32[27,4,16,256]{3,2,1,0:T(8,128)S(1)} %copy-done, f32[4,16,256]{2,1,0:T(8,128)S(1)} %copy-done.3, ...), custom_call_target="tpu_custom_call" | custom-call | flops 4194304 | bytes 4194304 | tf_op jit(solution)/shard_map/pallas_call | solution.py:618
  18.8 0.0 collective-permute-done.2.far
  18.8 0.6 %collective-permute-done.3.near = bf16[176,256]{1,0:T(8,128)(2,1)S(1)} collective-permute-done((bf16[176,256]{1,0:T(8,128)(2,1)S(1)}, bf16[176,256]{1,0:T(8,128)(2,1)S(1)}, u32[]{:S(2)}, u32[]{:S(2)}) %collective-permute-start.3) | collective-permute-done | bytes 90144 | tf_op jit(solution)/shard_map/ppermute | solution.py:571
  19.4 1.1 %shard_map.100 = (f32[27,2,16,256]{3,2,1,0:T(8,128)S(1)}, f32[27,2,8,256]{3,2,1,0:T(8,128)S(1)}, f32[4,2,16,256]{3,2,1,0:T(8,128)S(1)}, bf16[160,256]{1,0:T(8,128)(2,1)S(1)}, bf16[160,256]{1,0:T(8,128)(2,1)S(1)}) custom-call(f32[27,4,16,256]{3,2,1,0:T(8,128)S(1)} %shard_map.95.main, f32[27,4,8,256]{3,2,1,0:T(8,128)S(1)} %get-tuple-element.29.halo, ...), custom_call_target="tpu_custom_call" | custom-call | flops 4194304 | bytes 4194304 | tf_op jit(solution)/shard_map/pallas_call | solution.py:621
  20.6 2.6 %collective-permute-start.4 = (bf16[160,256]{1,0:T(8,128)(2,1)S(1)}, bf16[160,256]{1,0:T(8,128)(2,1)S(1)}, u32[]{:S(2)}, u32[]{:S(2)}) collective-permute-start(bf16[160,256]{1,0:T(8,128)(2,1)S(1)} %get-tuple-element.36), channel_id=1, source_target_pairs={{0,28},{4,8},{8,4},{12,16},{16,12},{20,24},{24,20},{28,0},{1,29},{... | collective-permute-start | bytes 245768 | tf_op jit(solution)/shard_map/ppermute | solution.py:571
  23.2 0.0 collective-permute-start.5
  23.2 1.9 %shard_map.101 = (f32[27,4,16,256]{3,2,1,0:T(8,128)}, f32[2,9,16,256]{3,2,1,0:T(8,128)S(1)}, f32[4,2,16,256]{3,2,1,0:T(8,128)S(1)}, f32[4,2,16,256]{3,2,1,0:T(8,128)S(1)}, bf16[32,16,128]{2,1,0:T(8,128)(2,1)S(1)}) custom-call(f32[27,2,16,256]{3,2,1,0:T(8,128)S(1)} %get-tuple-element.38.main_in, f32[27,2,8,256]{3,2,1,0:T(8,128)S(1)} %get-tuple-element.39.halo_in, ...), custom_call_target="tpu_custom_call" | custom-call | flops 4194304 | bytes 4194304 | tf_op jit(solution)/shard_map/pallas_call | solution.py:628
  25.1 2.8 %collective-permute-done.4.far = bf16[160,256]{1,0:T(8,128)(2,1)S(1)} collective-permute-done((bf16[160,256]{1,0:T(8,128)(2,1)S(1)}, bf16[160,256]{1,0:T(8,128)(2,1)S(1)}, u32[]{:S(2)}, u32[]{:S(2)}) %collective-permute-start.4) | collective-permute-done | bytes 81952 | tf_op jit(solution)/shard_map/ppermute | solution.py:571
  27.9 0.6 %collective-permute-done.5.near = bf16[160,256]{1,0:T(8,128)(2,1)S(1)} collective-permute-done((bf16[160,256]{1,0:T(8,128)(2,1)S(1)}, bf16[160,256]{1,0:T(8,128)(2,1)S(1)}, u32[]{:S(2)}, u32[]{:S(2)}) %collective-permute-start.5) | collective-permute-done | bytes 81952 | tf_op jit(solution)/shard_map/ppermute | solution.py:571
  28.5 1.0 %shard_map.102 = (f32[27,4,16,256]{3,2,1,0:T(8,128)}, bf16[32,40,128]{2,1,0:T(8,128)(2,1)S(1)}) custom-call(bf16[160,256]{1,0:T(8,128)(2,1)S(1)} %collective-permute-done.4.far, bf16[160,256]{1,0:T(8,128)(2,1)S(1)} %collective-permute-done.5.near, s32[4,16,256]{2,1,0:T(8,128)S(1)} %copy-done.2, ...), custom_call_target="tpu_custom_call", output_to_operand_aliasing={{0}: (10, {})} | custom-call | flops 4194304 | bytes 4194304 | tf_op jit(solution)/shard_map/pallas_call | solution.py:641
  29.5 15.3 %all_to_all.5.received = bf16[32,40,128]{2,1,0:T(8,128)(2,1)S(1)} all-to-all(bf16[32,40,128]{2,1,0:T(8,128)(2,1)S(1)} %get-tuple-element.51), channel_id=1, replica_groups=mesh['gx'=8,'gy'=4] {'gx','gy'}, dimensions={0} | all-to-all | bytes 655360 | tf_op jit(solution)/shard_map/all_to_all | solution.py:649
  44.8 1.0 %shard_map.103 = f32[128,128]{1,0:T(8,128)} custom-call(bf16[32,40,128]{2,1,0:T(8,128)(2,1)S(1)} %all_to_all.5.received), custom_call_target="tpu_custom_call" | custom-call | flops 1048576 | bytes 1048576 | tf_op jit(solution)/shard_map/pallas_call | solution.py:650
  (4 shorter events, 0.0 us)
Async XLA Ops:
  0.6 5.8 %copy-start.2 = (s32[4,16,256]{2,1,0:T(8,128)S(1)}, s32[4,16,256]{2,1,0:T(8,128)}, u32[]{:S(2)}) copy-start(s32[4,16,256]{2,1,0:T(8,128)} %walls.9) | copy-start | bytes 196612
  0.6 5.8 %copy-start = (f32[27,4,16,256]{3,2,1,0:T(8,128)S(1)}, f32[27,4,16,256]{3,2,1,0:T(8,128)}, u32[]{:S(2)}) copy-start(f32[27,4,16,256]{3,2,1,0:T(8,128)} %pops.7) | copy-start | bytes 5308420
  0.6 5.8 %copy-start.3 = (f32[4,16,256]{2,1,0:T(8,128)S(1)}, f32[4,16,256]{2,1,0:T(8,128)}, u32[]{:S(2)}) copy-start(f32[4,16,256]{2,1,0:T(8,128)} %omega.5) | copy-start | bytes 196612
  3.3 5.6 %collective-permute-start = (bf16[160,256]{1,0:T(8,128)(2,1)}, bf16[160,256]{1,0:T(8,128)(2,1)S(1)}, u32[]{:S(2)}, u32[]{:S(2)}) collective-permute-start(bf16[160,256]{1,0:T(8,128)(2,1)} %get-tuple-element.27), channel_id=1, source_target_pairs={{0,3},{1,2},{2,1},{3,0},{4,7},{5,6},{6,5},{7,4},{8,11},{9,10},{10,... | collective-permute-start | bytes 245768 | tf_op jit(solution)/shard_map/ppermute | solution.py:571
  5.8 3.1 %collective-permute-start.1 = (bf16[160,256]{1,0:T(8,128)(2,1)}, bf16[160,256]{1,0:T(8,128)(2,1)S(1)}, u32[]{:S(2)}, u32[]{:S(2)}) collective-permute-start(bf16[160,256]{1,0:T(8,128)(2,1)} %get-tuple-element.28), channel_id=1, source_target_pairs={{0,1},{1,0},{2,3},{3,2},{4,5},{5,4},{6,7},{7,6},{8,9},{9,8},{10,11... | collective-permute-start | bytes 245768 | tf_op jit(solution)/shard_map/ppermute | solution.py:571
  6.4 8.8 %copy-start.1 = (bf16[4096,512]{1,0:T(8,128)(2,1)S(1)}, bf16[4096,512]{1,0:T(8,128)(2,1)}, u32[]{:S(2)}) copy-start(bf16[4096,512]{1,0:T(8,128)(2,1)} %radiation.1) | copy-start | bytes 12582916
  7.5 7.8 %copy-start.4 = (s32[128,32]{0,1:T(8,128)S(1)}, s32[128,32]{0,1:T(8,128)}, u32[]{:S(2)}) copy-start(s32[128,32]{0,1:T(8,128)} %param.12) | copy-start | bytes 49156
  7.5 7.7 %copy-start.5 = (s32[1,1,16]{2,1,0:T(1,128)S(1)}, s32[1,1,16]{2,1,0:T(1,128)}, u32[]{:S(2)}) copy-start(s32[1,1,16]{2,1,0:T(1,128)} %sites.1) | copy-start | bytes 196
  7.5 7.7 %copy-start.6 = (s32[1,1,16]{2,1,0:T(1,128)S(1)}, s32[1,1,16]{2,1,0:T(1,128)}, u32[]{:S(2)}) copy-start(s32[1,1,16]{2,1,0:T(1,128)} %patches.1) | copy-start | bytes 196
  9.1 9.6 %collective-permute-start.2 = (bf16[176,256]{1,0:T(8,128)(2,1)S(1)}, bf16[176,256]{1,0:T(8,128)(2,1)S(1)}, u32[]{:S(2)}, u32[]{:S(2)}) collective-permute-start(bf16[176,256]{1,0:T(8,128)(2,1)S(1)} %get-tuple-element.32), channel_id=1, source_target_pairs={{0,28},{4,8},{8,4},{12,16},{16,12},{20,24},{24,20},{28,0},{1,29},{... | collective-permute-start | bytes 270344 | tf_op jit(solution)/shard_map/ppermute | solution.py:571
  14.6 4.8 %collective-permute-start.3 = (bf16[176,256]{1,0:T(8,128)(2,1)S(1)}, bf16[176,256]{1,0:T(8,128)(2,1)S(1)}, u32[]{:S(2)}, u32[]{:S(2)}) collective-permute-start(bf16[176,256]{1,0:T(8,128)(2,1)S(1)} %get-tuple-element.33), channel_id=1, source_target_pairs={{0,4},{4,0},{8,12},{12,8},{16,20},{20,16},{24,28},{28,24},{1,5},{5... | collective-permute-start | bytes 270344 | tf_op jit(solution)/shard_map/ppermute | solution.py:571
  20.6 7.3 %collective-permute-start.4 = (bf16[160,256]{1,0:T(8,128)(2,1)S(1)}, bf16[160,256]{1,0:T(8,128)(2,1)S(1)}, u32[]{:S(2)}, u32[]{:S(2)}) collective-permute-start(bf16[160,256]{1,0:T(8,128)(2,1)S(1)} %get-tuple-element.36), channel_id=1, source_target_pairs={{0,28},{4,8},{8,4},{12,16},{16,12},{20,24},{24,20},{28,0},{1,29},{... | collective-permute-start | bytes 245768 | tf_op jit(solution)/shard_map/ppermute | solution.py:571
  23.2 5.3 %collective-permute-start.5 = (bf16[160,256]{1,0:T(8,128)(2,1)S(1)}, bf16[160,256]{1,0:T(8,128)(2,1)S(1)}, u32[]{:S(2)}, u32[]{:S(2)}) collective-permute-start(bf16[160,256]{1,0:T(8,128)(2,1)S(1)} %get-tuple-element.37), channel_id=1, source_target_pairs={{0,4},{4,0},{8,12},{12,8},{16,20},{20,16},{24,28},{28,24},{1,5},{5... | collective-permute-start | bytes 245768 | tf_op jit(solution)/shard_map/ppermute | solution.py:571

commit v4 on v3

--- a/solution.py
+++ b/solution.py
@@ -1,3 +1,5 @@
+import functools
+
 import jax
 import jax.numpy as jnp
 from jax import lax
@@ -153,6 +155,13 @@
     wide[1 - odd, :, :] = near[...].astype(F32)
 
 
+def merge_named(own, wide, *others):
+    named = own
+    for more in (wide[0, pl.ds(wide.shape[1] - SUB, SUB), :], wide[1, pl.ds(wide.shape[1] - SUB, SUB), :], *others):
+        named = jnp.maximum(named, more)
+    return named
+
+
 def start_all(copies):
     for copy in copies:
         copy.start()
@@ -165,7 +174,24 @@
     return both, [i for i in range(27) if STEP[i][1] != outward]
 
 
-def rows_kernel(pops_in, omega_in, walls_in, far, near, pops, omega, walls, packed, faces, sems):
+def named_tile(patches, place, nz):
+    slots = patches.shape[-1]
+    groups = slots // SUB
+    ids = jnp.broadcast_to(patches[0, :, :].astype(F32) + 1.0, (SUB, slots))
+    row = lax.broadcasted_iota(jnp.int32, (SUB, slots), 0)
+    slot = lax.broadcasted_iota(jnp.int32, (SUB, slots), 1)
+    lane = lax.broadcasted_iota(jnp.int32, (SUB, nz), 1)
+    tile = jnp.zeros((SUB, nz), F32)
+    for g in range(groups):
+        column = jnp.sum(jnp.where(slot == SUB * g + row, ids, 0.0), axis=1, keepdims=True)
+        tile = jnp.where(lane == place * groups + g, column, tile)
+    return tile
+
+
+def rows_kernel(
+    size_y, pops_in, omega_in, walls_in, patches_in, far, near, own,
+    pops, omega, walls, patches, packed, faces, sems,
+):
     planes, ny, nz = omega.shape
     row = lax.broadcasted_iota(jnp.int32, (SUB, nz), 0)
     chunk = 4
@@ -173,6 +199,7 @@
     cells = [
         pltpu.make_async_copy(omega_in, omega, sems.at[len(spans)]),
         pltpu.make_async_copy(walls_in, walls, sems.at[len(spans) + 1]),
+        pltpu.make_async_copy(patches_in, patches, sems.at[len(spans) + 2]),
     ]
     copies = [pltpu.make_async_copy(pops_in.at[span], pops.at[span], sems.at[k]) for k, span in enumerate(spans)]
     start_all(cells + copies)
@@ -199,6 +226,8 @@
         copy.wait()
     pack(27)
     pack(28)
+    named = named_tile(patches, lax.axis_index("gx") * size_y + lax.axis_index("gy"), nz)
+    own[...] = jnp.concatenate([named, jnp.zeros((SUB, nz), F32)], axis=0).astype(BF16)
     for i in range(27):
         if i % chunk == 0:
             copies[i // chunk].wait()
@@ -218,7 +247,7 @@
             one, two = (packed[side, i, :, :] for i in edge[k : k + 2])
             at_edge = row % 2 == 1 - side
             tiles.append(jnp.where(at_edge, one, pltpu.roll(two, SUB - 1 if side == 0 else 1, 0)))
-        tiles.append(jnp.zeros((SUB, nz), F32))
+        tiles.append(named)
         for k, tile in enumerate(tiles):
             faces[side, pl.ds(SUB * k, SUB), :] = tile
     odd = odd_block("gy")
@@ -259,7 +288,7 @@
     return 9 * ny + (4 if reach == 2 else 2) * SUB
 
 
-def pack_x(main, halo, plane, first, reach, out):
+def pack_x(main, halo, plane, first, reach, named, out):
     ny, nz = main.shape[2:]
     row = lax.broadcasted_iota(jnp.int32, (SUB, nz), 0)
     scaled = lambda ref, k: ref[first + k, plane, :, :] * (1.0 / WEIGHT[k]) - 1.0
@@ -272,16 +301,17 @@
             value = scaled(halo, k)
             value = pltpu.roll(value, turn, 0) if turn else value
             tiles[tile] = jnp.where(row == at, value, tiles[tile])
+    tiles[-1] = named
     out[pl.ds(9 * ny, SUB * len(tiles)), :] = jnp.concatenate(tiles, axis=0).astype(BF16)
 
 
-def pack_faces(main, halo, last, reach, far, near):
+def pack_faces(main, halo, last, reach, named, far, near):
     odd = odd_block("gx")
-    pack_x(main, halo, odd * last, odd * 18, reach, far)
-    pack_x(main, halo, (1 - odd) * last, (1 - odd) * 18, reach, near)
-
-
-def first_halo_kernel(far, near, main, halo, retain, solid, send_far, send_near, wide):
+    pack_x(main, halo, odd * last, odd * 18, reach, named, far)
+    pack_x(main, halo, (1 - odd) * last, (1 - odd) * 18, reach, named, near)
+
+
+def first_halo_kernel(far, near, main, own, across, halo, retain, solid, named, send_far, send_near, wide):
     _, planes, _, nz = halo.shape
     row = lax.broadcasted_iota(jnp.int32, (SUB, nz), 0)
     widen(far, near, wide, "gy")
@@ -307,7 +337,8 @@
         solid[plane, :, :] = beside(28, plane)
         for i in range(27):
             halo[i, plane, :, :] = (beside(i, plane) + 1.0) * WEIGHT[i]
-    pack_faces(main, halo, planes - 1, 2, send_far, send_near)
+    named[...] = merge_named(own[...].astype(F32)[:SUB], wide, across[...].astype(F32)[:SUB])
+    pack_faces(main, halo, planes - 1, 2, named[...], send_far, send_near)
 
 
 def turned(value, i):
@@ -382,14 +413,16 @@
 
 
 def middle_outer_kernel(
-    main, halo, pops, omega, walls, retain, solid, far, near, _, __,
-    main2, halo2, macro, send_far, send_near, read, wide,
+    main, halo, pops, omega, walls, retain, solid, far, near, own, _, __,
+    main2, halo2, macro, named, send_far, send_near, read, wide,
 ):
     planes, ny, _ = omega.shape
     widen(far, near, wide, "gx")
     load = loader(planes, ny, [(main, halo, p) for p in range(planes)], wide)
     middle((0, planes - 1), load, pops, omega, walls, retain, solid, main2, halo2, macro, read)
-    pack_faces(main2, halo2, 1, 1, send_far, send_near)
+    more = merge_named(own[...], wide)
+    named[...] = jnp.concatenate([more, jnp.zeros(more.shape, F32)], axis=0).astype(BF16)
+    pack_faces(main2, halo2, 1, 1, more, send_far, send_near)
 
 
 def add_moments(sums, i, f):
@@ -416,7 +449,7 @@
     return response.astype(BF16)
 
 
-def slots_kernel(bins, radiation, counts, sites, patches, pick, level, turned_radiation):
+def slots_kernel(size_y, bins, radiation, counts, sites, patches, pick, level, own_bins, turned_radiation):
     halves, slots, lines = pick.shape
     slot = lax.broadcasted_iota(jnp.int32, (slots, lines), 0)
     line = lax.broadcasted_iota(jnp.int32, (slots, lines), 1)
@@ -451,6 +484,10 @@
                 tile = column if tile is None else jnp.where(group == g, column, tile)
             tiles[blk] = tile.astype(BF16)
         level[d, :, :] = tiles[blk]
+
+    place = lax.axis_index("gx") * size_y + lax.axis_index("gy")
+    mine = bins[pl.ds(lax.div(place * width, OBS_BLK), 1), :].astype(F32)
+    own_bins[...] = jnp.broadcast_to(mine, own_bins.shape).astype(BF16)
 
     observers, terms = radiation.shape
 
@@ -507,8 +544,8 @@
 
 
 def last_kernel(
-    far, near, walls, spare, part, inner, radiation, pick, early, level, started,
-    out, send, g_out, fields, wide, sems,
+    far, near, walls, spare, part, inner, radiation, pick, early, level, own, across, started,
+    out, send, named, g_out, fields, wide, sems,
 ):
     planes, ny, _ = walls.shape
     last = planes - 1
@@ -536,9 +573,31 @@
     for d in range(devices):
         send[d, pl.ds(0, slots), :] = early[d, :, :]
         send[d, pl.ds(slots, slots), :] = response[:, d * width : (d + 1) * width]
-        send[d, pl.ds(2 * slots, SUB), :] = level[d, :, :]
+        if send.shape[1] > 2 * slots:
+            send[d, pl.ds(2 * slots, SUB), :] = level[d, :, :]
+    named[...] = merge_named(own[...].astype(F32)[:SUB], wide, across[...].astype(F32)[:SUB])
     for copy in copies:
         copy.wait()
+
+
+def bin_named_kernel(received, named, own_bins, signal, hits, known):
+    devices, rows, width = received.shape
+    slots = rows // 2
+    groups = slots // SUB
+    patch = lax.broadcasted_iota(jnp.int32, (slots, known.shape[-1]), 1).astype(F32) + 1.0
+    for d in range(devices):
+        columns = [named[:, groups * d + g : groups * d + g + 1] for g in range(groups)]
+        ids = jnp.concatenate([jnp.broadcast_to(c, (SUB, patch.shape[1])) for c in columns], axis=0)
+        known[d, :, :] = (ids == patch).astype(F32).astype(BF16)
+    flat = known[...].reshape(devices * slots, patch.shape[1])
+    level = lax.dot_general(flat, own_bins[...], (((1,), (1,)), ((), ())), preferred_element_type=F32)
+    lane = lax.broadcasted_iota(jnp.int32, level.shape, 1).astype(F32)
+    for step in range(2):
+        hit = (level == lane - float(step)).astype(F32).astype(BF16)
+        hits[:, pl.ds(step * slots, slots), :] = hit.reshape(devices, slots, LEVELS)
+    left = received[...].reshape(devices * rows, width)
+    right = hits[...].reshape(devices * rows, LEVELS)
+    signal[...] = lax.dot_general(left, right, (((0,), (0,)), ((), ())), preferred_element_type=F32)
 
 
 def bin_kernel(received, signal, hits):
@@ -573,24 +632,27 @@
     dma = pltpu.SemaphoreType.DMA
     block, cells = populations.shape, (planes, ny, nz)
     beside = (20 * SUB, nz)
-    far, near = call(
-        rows_kernel,
-        [HBM] * 3,
-        [(VMEM, beside, BF16)] * 2,
+    far, near, own = call(
+        functools.partial(rows_kernel, size_y),
+        [HBM] * 4,
+        [(VMEM, beside, BF16)] * 2 + [(VMEM, (2 * SUB, nz), BF16)],
         [
             pltpu.VMEM(block, F32), pltpu.VMEM(cells, F32), pltpu.VMEM(cells, walls.dtype),
-            pltpu.VMEM((2, 29, SUB, nz), F32), pltpu.VMEM((2, *beside), F32), dma((9,)),
+            pltpu.VMEM(sample_patch.shape, sample_patch.dtype),
+            pltpu.VMEM((2, 29, SUB, nz), F32), pltpu.VMEM((2, *beside), F32), dma((10,)),
         ],
         cost=1 << 20,
         limit=64800000,
-    )(populations, omega, walls)
+    )(populations, omega, walls, sample_patch)
     far, near = swap(far, near, "gy", size_y)
-    pick, level, radiation = call(
-        slots_kernel,
+    across = lax.ppermute(own, "gy", [(i, (i + size_y // 2) % size_y) for i in range(size_y)])
+    pick, level, own_bins, radiation = call(
+        functools.partial(slots_kernel, size_y),
         [VMEM] * 2 + [SMEM] * 3,
         [
             (VMEM, (nz // LANES, slots, planes * ny), BF16),
             (VMEM, (devices, SUB, width), BF16),
+            (VMEM, (LEVELS, bins.shape[0]), BF16),
             (VMEM, radiation.shape[::-1], BF16),
         ],
         cost=1 << 22,
@@ -600,13 +662,13 @@
     edge = (planes, SUB, nz)
     face, last_face = ((face_rows(ny, reach), nz) for reach in (2, 1))
     faces, last_faces = ([(VMEM, shape, BF16)] * 2 for shape in (face, last_face))
-    halo, retain, solid, far, near = call(
+    halo, retain, solid, named, far, near = call(
         first_halo_kernel,
-        [VMEM] * 3,
-        [(VMEM, (27, *edge), F32), (VMEM, edge, F32), (VMEM, edge, F32), *faces],
+        [VMEM] * 5,
+        [(VMEM, (27, *edge), F32), (VMEM, edge, F32), (VMEM, edge, F32), (VMEM, (SUB, nz), F32), *faces],
         [pltpu.VMEM((2, *beside), F32)],
         cost=1 << 20,
-    )(far, near, main)
+    )(far, near, main, own, across)
     far, near = swap(far, near, "gx", size_x)
 
     def relaxed(n):
@@ -618,10 +680,11 @@
     main_in, halo_in, macro_in = call(
         middle_inner_kernel, [VMEM] * 7, relaxed(planes - 2), [read], cost=1 << 22
     )(*args)
-    main_out, halo_out, macro_out, far, near = call(
-        middle_outer_kernel, [VMEM] * 11, relaxed(2) + last_faces, [read, wide], cost=1 << 22
-    )(*args, far, near, macro_in, pick)
+    main_out, halo_out, macro_out, named, far, near = call(
+        middle_outer_kernel, [VMEM] * 12, relaxed(2) + [(VMEM, (2 * SUB, nz), BF16), *last_faces], [read, wide], cost=1 << 22
+    )(*args, far, near, named, macro_in, pick)
     far, near = swap(far, near, "gx", size_x)
+    across = lax.ppermute(named, "gx", [(i, (i + size_x // 2) % size_x) for i in range(size_x)])
 
     fields = pltpu.VMEM((4, planes * ny, nz), BF16)
     inner = (4, planes - 2, ny, nz)
@@ -638,18 +701,24 @@
         [pltpu.VMEM(block, F32), fields, dma((planes,))],
         cost=1 << 22,
     )(main_in, halo_in, main_out, halo_out, populations, walls, macro_in, macro_out, radiation, pick)
-    advanced, send = call(
+    ride = (size_x, size_y) == (8, 4)
+    sent = 2 * slots if ride else 2 * slots + SUB
+    advanced, send, named = call(
         last_kernel,
-        [VMEM] * 10 + [HBM],
-        [(HBM, block, F32), (VMEM, (devices, 2 * slots + SUB, width), BF16)],
+        [VMEM] * 12 + [HBM],
+        [(HBM, block, F32), (VMEM, (devices, sent, width), BF16), (VMEM, (SUB, nz), F32)],
         [pltpu.VMEM((9, 2, ny, nz), F32), fields, last_wide, dma((2,))],
-        aliases={10: 0},
+        aliases={12: 0},
         cost=1 << 22,
-    )(far, near, walls, spare, part, inner, radiation, pick, early, level, started)
+    )(far, near, walls, spare, part, inner, radiation, pick, early, level, named, across, started)
     received = lax.all_to_all(send, ("gx", "gy"), 0, 0, tiled=True)
-    (signal,) = call(
-        bin_kernel, [VMEM], [(VMEM, (width, LEVELS), F32)], [pltpu.VMEM((devices, 2 * slots, LEVELS), BF16)], cost=1 << 20
-    )(received)
+    hits = pltpu.VMEM((devices, 2 * slots, LEVELS), BF16)
+    result = [(VMEM, (width, LEVELS), F32)]
+    if ride:
+        known = pltpu.VMEM((devices, slots, bins.shape[0]), BF16)
+        (signal,) = call(bin_named_kernel, [VMEM] * 3, result, [hits, known], cost=1 << 20)(received, named, own_bins)
+    else:
+        (signal,) = call(bin_kernel, [VMEM], result, [hits], cost=1 << 20)(received)
     return advanced, signal
 
 

time: 45.9 us -> 44.9 us (0.978)
  blocking collectives: 15.3 us -> 13.7 us
    ppermute x0 -> x2, waiting for transfers between devices: none -> 4.58 us  [the longest x1 2.7 us: per_device(): lax.ppermute(own, 'gy', [(i, (i + size_y // 2) % size_y) for i in range(s...]
    ppermute x3, waiting for transfers between devices: 4.13 us -> 0.06 us  [swap(): lax.ppermute(far, axis, far_pairs)]
    all_to_all x1, blocking collectives: 15.3 us -> 13.7 us  [per_device(): received = lax.all_to_all(send, ('gx', 'gy'), 0, 0, tiled=True)]
    ppermute x0 -> x2, starting transfers between devices: none -> 0.78 us  [the longest x1 0.73 us: per_device(): lax.ppermute(named, 'gx', [(i, (i + size_x // 2) % size_x) for i in range...]
    ppermute x3, starting transfers between devices: 10.5 us -> 9.77 us  [swap(): lax.ppermute(far, axis, far_pairs)]
  transfers between devices with their start and end apart: 6 -> 8, of which waited for: 4 -> 5; matrix products, arithmetic and copies ran while one was open for 0% -> 0% of each run, Pallas kernels for 14% -> 14%
where the time goes in v4:
time: 44.9 us; the launch traced here: 44.8 us
  blocking collectives  13.7 us (31%)
  Pallas kernels  12.6 us (28%)
  starting transfers between devices  11.2 us (25%)
  waiting for transfers between devices  5.76 us (13%)
  between operations  1.45 us (3%)
    all_to_all x1, blocking collectives, per_device(): received = lax.all_to_all(send, ('gx', 'gy'), 0, 0, tiled=True)  13.7 us
    ppermute x3, starting transfers between devices, swap(): lax.ppermute(far, axis, far_pairs)  9.77 us
    ppermute x1, waiting for transfers between devices, per_device(): lax.ppermute(own, 'gy', [(i, (i + size_y // 2) % size_y) for i in range(s...  2.7 us
    pallas_call x1, Pallas kernels, per_device(): call(functools.partial(rows_kernel, size_y), [HBM] * 4, [(VMEM, beside, B...  2.69 us
    pallas_call x1, Pallas kernels, per_device(): call(functools.partial(slots_kernel, size_y), [VMEM] * 2 + [SMEM] * 3, [(...  2.4 us
    pallas_call x1, Pallas kernels, per_device(): call(last_early_kernel, [VMEM] * 10, [(HBM, block, F32), (VMEM, (2, 9, ny...  1.93 us
    ppermute x1, waiting for transfers between devices, per_device(): lax.ppermute(named, 'gx', [(i, (i + size_x // 2) % size_x) for i in range...  1.88 us
    pallas_call x1, Pallas kernels, per_device(): call(middle_outer_kernel, [VMEM] * 12, relaxed(2) + [(VMEM, (2 * SUB, nz)...  1.15 us
  transfers between devices with their start and end apart: 8, of which 5 were waited for; matrix products, arithmetic and copies ran while one was open for 0% of the time, Pallas kernels for 14%

profile of v4, /device:TPU:0, one launch (start us, length us, event | category | flops | bytes accessed | tf_op | source)
XLA Modules:
  0.0 44.8 jit_solution(1571971141645201331)
XLA Ops:
  0.6 0.0 copy-start.2
  0.6 0.0 copy-start
  0.7 2.7 %shard_map.96 = (bf16[160,256]{1,0:T(8,128)(2,1)}, bf16[160,256]{1,0:T(8,128)(2,1)}, bf16[16,256]{1,0:T(8,128)(2,1)}) custom-call(f32[27,4,16,256]{3,2,1,0:T(8,128)} %pops.7, f32[4,16,256]{2,1,0:T(8,128)} %omega.5, s32[4,16,256]{2,1,0:T(8,128)} %walls.9, s32[1,1,16]{2,1,0:T(1,128)} %patches.1), custom_call_target="tpu_custom_call" | custom-call | flops 1048576 | bytes 1048576 | tf_op jit(solution)/shard_map/pallas_call | solution.py:635
  3.4 2.4 %collective-permute-start = (bf16[160,256]{1,0:T(8,128)(2,1)}, bf16[160,256]{1,0:T(8,128)(2,1)S(1)}, u32[]{:S(2)}, u32[]{:S(2)}) collective-permute-start(bf16[160,256]{1,0:T(8,128)(2,1)} %get-tuple-element.32), channel_id=1, source_target_pairs={{0,3},{1,2},{2,1},{3,0},{4,7},{5,6},{6,5},{7,4},{8,11},{9,10},{10,... | collective-permute-start | bytes 245768 | tf_op jit(solution)/shard_map/ppermute | solution.py:630
  5.8 0.7 %collective-permute-start.1 = (bf16[160,256]{1,0:T(8,128)(2,1)}, bf16[160,256]{1,0:T(8,128)(2,1)S(1)}, u32[]{:S(2)}, u32[]{:S(2)}) collective-permute-start(bf16[160,256]{1,0:T(8,128)(2,1)} %get-tuple-element.33), channel_id=1, source_target_pairs={{0,1},{1,0},{2,3},{3,2},{4,5},{5,4},{6,7},{7,6},{8,9},{9,8},{10,11... | collective-permute-start | bytes 245768 | tf_op jit(solution)/shard_map/ppermute | solution.py:630
  6.5 0.1 collective-permute-start.2
  6.5 1.1 %shard_map.95.main = f32[27,4,16,256]{3,2,1,0:T(8,128)S(1)} custom-call(f32[27,4,16,256]{3,2,1,0:T(8,128)S(1)} %copy-done, f32[4,16,256]{2,1,0:T(8,128)S(1)} %copy-done.3, s32[4,16,256]{2,1,0:T(8,128)S(1)} %copy-done.2), custom_call_target="tpu_custom_call" | custom-call | flops 4194304 | bytes 4194304 | tf_op jit(solution)/shard_map/pallas_call | solution.py:660
  7.6 0.0 copy-start.4
  7.6 0.0 copy-start.6
  7.6 0.0 copy-start.7
  7.6 2.7 %collective-permute-done.2.across = bf16[16,256]{1,0:T(8,128)(2,1)S(1)} collective-permute-done((bf16[16,256]{1,0:T(8,128)(2,1)}, bf16[16,256]{1,0:T(8,128)(2,1)S(1)}, u32[]{:S(2)}, u32[]{:S(2)}) %collective-permute-start.2) | collective-permute-done | bytes 8224 | tf_op jit(solution)/shard_map/ppermute | solution.py:648
  10.3 0.0 collective-permute-done.far
  10.3 0.0 collective-permute-done.1.near
  10.3 0.0 copy-done.5
  10.3 0.2 shard_map.97
  10.6 4.6 %collective-permute-start.3 = (bf16[176,256]{1,0:T(8,128)(2,1)S(1)}, bf16[176,256]{1,0:T(8,128)(2,1)S(1)}, u32[]{:S(2)}, u32[]{:S(2)}) collective-permute-start(bf16[176,256]{1,0:T(8,128)(2,1)S(1)} %get-tuple-element.38), channel_id=1, source_target_pairs={{0,28},{4,8},{8,4},{12,16},{16,12},{20,24},{24,20},{28,0},{1,29},{... | collective-permute-start | bytes 270344 | tf_op jit(solution)/shard_map/ppermute | solution.py:630
  15.2 0.0 collective-permute-start.4
  15.9 2.4 %shard_map.99 = (bf16[2,16,64]{2,1,0:T(8,128)(2,1)S(1)}, bf16[32,8,128]{2,1,0:T(8,128)(2,1)S(1)}, bf16[128,128]{1,0:T(8,128)(2,1)S(1)}, bf16[512,4096]{1,0:T(8,128)(2,1)S(1)}) custom-call(s32[32,128]{1,0:T(8,128)S(1)} %bitcast.1, bf16[4096,512]{1,0:T(8,128)(2,1)S(1)} %copy-done.1, s32[1,1]{1,0:T(1,128)S(6)} %copy.12.counts, s32[1,1,16]{2,1,0:T(1,128)S(1)} %copy-done.7, ...), custom_call_target="tpu_custom_call" | custom-call | flops 4194304 | bytes 4194304 | tf_op jit(solution)/shard_map/pallas_call | solution.py:649
  18.3 1.1 %shard_map.98 = (f32[27,2,16,256]{3,2,1,0:T(8,128)S(1)}, f32[27,2,8,256]{3,2,1,0:T(8,128)S(1)}, f32[4,2,16,256]{3,2,1,0:T(8,128)S(1)}) custom-call(f32[27,4,16,256]{3,2,1,0:T(8,128)S(1)} %shard_map.95.main, f32[27,4,8,256]{3,2,1,0:T(8,128)S(1)} %get-tuple-element.35.halo, f32[27,4,16,256]{3,2,1,0:T(8,128)S(1)} %copy-done, f32[4,16,256]{2,1,0:T(8,128)S(1)} %copy-done.3, ...), custom_call_target="tpu_custom_call" | custom-call | flops 4194304 | bytes 4194304 | tf_op jit(solution)/shard_map/pallas_call | solution.py:680
  19.4 0.0 collective-permute-done.3.far
  19.4 0.4 collective-permute-done.4.near
  19.8 1.1 %shard_map.100 = (f32[27,2,16,256]{3,2,1,0:T(8,128)S(1)}, f32[27,2,8,256]{3,2,1,0:T(8,128)S(1)}, f32[4,2,16,256]{3,2,1,0:T(8,128)S(1)}, bf16[16,256]{1,0:T(8,128...) custom-call(f32[27,4,16,256]{3,2,1,0:T(8,128)S(1)} %shard_map.95.main, ...), custom_call_target="tpu_custom_call" | custom-call | flops 4194304 | bytes 4194304 | tf_op jit(solution)/shard_map/pallas_call | solution.py:683
  21.0 2.7 %collective-permute-start.5 = (bf16[160,256]{1,0:T(8,128)(2,1)S(1)}, bf16[160,256]{1,0:T(8,128)(2,1)S(1)}, u32[]{:S(2)}, u32[]{:S(2)}) collective-permute-start(bf16[160,256]{1,0:T(8,128)(2,1)S(1)} %get-tuple-element.43), channel_id=1, source_target_pairs={{0,28},{4,8},{8,4},{12,16},{16,12},{20,24},{24,20},{28,0},{1,29},{... | collective-permute-start | bytes 245768 | tf_op jit(solution)/shard_map/ppermute | solution.py:630
  23.7 0.0 collective-permute-start.6
  23.7 0.7 %collective-permute-start.7 = (bf16[16,256]{1,0:T(8,128)(2,1)S(1)}, bf16[16,256]{1,0:T(8,128)(2,1)S(1)}, u32[]{:S(2)}, u32[]{:S(2)}) collective-permute-start(bf16[16,256]{1,0:T(8,128)(2,1)S(1)} %get-tuple-element.56.own), channel_id=1, source_target_pairs={{0,16},{4,20},{8,24},{12,28},{16,0},{20,4},{24,8},{28,12},{1,17},{... | collective-permute-start | bytes 24584 | tf_op jit(solution)/shard_map/ppermute | solution.py:687
  24.4 1.9 %shard_map.101 = (f32[27,4,16,256]{3,2,1,0:T(8,128)}, f32[2,9,16,256]{3,2,1,0:T(8,128)S(1)}, f32[4,2,16,256]{3,2,1,0:T(8,128)S(1)}, f32[4,2,16,256]{3,2,1,0:T(8,128)S(1)}, bf16[32,16,128]{2,1,0:T(8,128)(2,1)S(1)}) custom-call(f32[27,2,16,256]{3,2,1,0:T(8,128)S(1)} %get-tuple-element.45.main_in, f32[27,2,8,256]{3,2,1,0:T(8,128)S(1)} %get-tuple-element.46.halo_in, ...), custom_call_target="tpu_custom_call" | custom-call | flops 4194304 | bytes 4194304 | tf_op jit(solution)/shard_map/pallas_call | solution.py:691
  26.3 1.9 %collective-permute-done.7.across = bf16[16,256]{1,0:T(8,128)(2,1)S(1)} collective-permute-done((bf16[16,256]{1,0:T(8,128)(2,1)S(1)}, bf16[16,256]{1,0:T(8,128)(2,1)S(1)}, u32[]{:S(2)}, u32[]{:S(2)}) %collective-permute-start.7) | collective-permute-done | bytes 8224 | tf_op jit(solution)/shard_map/ppermute | solution.py:687
  28.2 0.1 collective-permute-done.5.far
  28.3 0.7 %collective-permute-done.6.near = bf16[160,256]{1,0:T(8,128)(2,1)S(1)} collective-permute-done((bf16[160,256]{1,0:T(8,128)(2,1)S(1)}, bf16[160,256]{1,0:T(8,128)(2,1)S(1)}, u32[]{:S(2)}, u32[]{:S(2)}) %collective-permute-start.6) | collective-permute-done | bytes 81952 | tf_op jit(solution)/shard_map/ppermute | solution.py:630
  29.0 1.0 %shard_map.102 = (f32[27,4,16,256]{3,2,1,0:T(8,128)}, bf16[32,32,128]{2,1,0:T(8,128)(2,1)S(1)}, f32[8,256]{1,0:T(8,128)S(1)}) custom-call(bf16[160,256]{1,0:T(8,128)(2,1)S(1)} %collective-permute-done.5.far, bf16[160,256]{1,0:T(8,128)(2,1)S(1)} %collective-permute-done.6.near, s32[4,16,256]{2,1,0:T(8,128)S(1)} %copy-done.2, ...), custom_call_target="tpu_custom_call", output_to_operand_aliasing={{0}: (12, {})} | custom-call | flops 4194304 | bytes 4194304 | tf_op jit(solution)/shard_map/pallas_call | solution.py:706
  30.0 13.7 %all_to_all.5.received = bf16[32,32,128]{2,1,0:T(8,128)(2,1)S(1)} all-to-all(bf16[32,32,128]{2,1,0:T(8,128)(2,1)S(1)} %get-tuple-element.59), channel_id=1, replica_groups=mesh['gx'=8,'gy'=4] {'gx','gy'}, dimensions={0} | all-to-all | bytes 524288 | tf_op jit(solution)/shard_map/all_to_all | solution.py:714
  43.6 1.1 %shard_map.103 = f32[128,128]{1,0:T(8,128)} custom-call(bf16[32,32,128]{2,1,0:T(8,128)(2,1)S(1)} %all_to_all.5.received, f32[8,256]{1,0:T(8,128)S(1)} %get-tuple-element.60.named, bf16[128,128]{1,0:T(8,128)(2,1)S(1)} %get-tuple-element.61.own_bins), custom_call_target="tpu_custom_call" | custom-call | flops 1048576 | bytes 1048576 | tf_op jit(solution)/shard_map/pallas_call | solution.py:719
  (10 shorter events, 0.0 us)
Async XLA Ops:
  0.6 5.9 %copy-start.2 = (s32[4,16,256]{2,1,0:T(8,128)S(1)}, s32[4,16,256]{2,1,0:T(8,128)}, u32[]{:S(2)}) copy-start(s32[4,16,256]{2,1,0:T(8,128)} %walls.9) | copy-start | bytes 196612
  0.6 5.9 %copy-start = (f32[27,4,16,256]{3,2,1,0:T(8,128)S(1)}, f32[27,4,16,256]{3,2,1,0:T(8,128)}, u32[]{:S(2)}) copy-start(f32[27,4,16,256]{3,2,1,0:T(8,128)} %pops.7) | copy-start | bytes 5308420
  0.6 5.9 %copy-start.3 = (f32[4,16,256]{2,1,0:T(8,128)S(1)}, f32[4,16,256]{2,1,0:T(8,128)}, u32[]{:S(2)}) copy-start(f32[4,16,256]{2,1,0:T(8,128)} %omega.5) | copy-start | bytes 196612
  3.4 7.0 %collective-permute-start = (bf16[160,256]{1,0:T(8,128)(2,1)}, bf16[160,256]{1,0:T(8,128)(2,1)S(1)}, u32[]{:S(2)}, u32[]{:S(2)}) collective-permute-start(bf16[160,256]{1,0:T(8,128)(2,1)} %get-tuple-element.32), channel_id=1, source_target_pairs={{0,3},{1,2},{2,1},{3,0},{4,7},{5,6},{6,5},{7,4},{8,11},{9,10},{10,... | collective-permute-start | bytes 245768 | tf_op jit(solution)/shard_map/ppermute | solution.py:630
  5.8 4.5 %collective-permute-start.1 = (bf16[160,256]{1,0:T(8,128)(2,1)}, bf16[160,256]{1,0:T(8,128)(2,1)S(1)}, u32[]{:S(2)}, u32[]{:S(2)}) collective-permute-start(bf16[160,256]{1,0:T(8,128)(2,1)} %get-tuple-element.33), channel_id=1, source_target_pairs={{0,1},{1,0},{2,3},{3,2},{4,5},{5,4},{6,7},{7,6},{8,9},{9,8},{10,11... | collective-permute-start | bytes 245768 | tf_op jit(solution)/shard_map/ppermute | solution.py:630
  6.5 3.9 %copy-start.5 = (bf16[16,256]{1,0:T(8,128)(2,1)S(1)}, bf16[16,256]{1,0:T(8,128)(2,1)}, u32[]{:S(2)}) copy-start(bf16[16,256]{1,0:T(8,128)(2,1)} %get-tuple-element.34.own) | copy-start | bytes 24580
  6.5 3.9 %collective-permute-start.2 = (bf16[16,256]{1,0:T(8,128)(2,1)}, bf16[16,256]{1,0:T(8,128)(2,1)S(1)}, u32[]{:S(2)}, u32[]{:S(2)}) collective-permute-start(bf16[16,256]{1,0:T(8,128)(2,1)} %get-tuple-element.34.own), channel_id=1, source_target_pairs={{0,2},{1,3},{2,0},{3,1},{4,6},{5,7},{6,4},{7,5},{8,10},{9,11},{10,... | collective-permute-start | bytes 24584 | tf_op jit(solution)/shard_map/ppermute | solution.py:648
  6.5 9.3 %copy-start.1 = (bf16[4096,512]{1,0:T(8,128)(2,1)S(1)}, bf16[4096,512]{1,0:T(8,128)(2,1)}, u32[]{:S(2)}) copy-start(bf16[4096,512]{1,0:T(8,128)(2,1)} %radiation.1) | copy-start | bytes 12582916
  7.6 8.3 %copy-start.4 = (s32[128,32]{0,1:T(8,128)S(1)}, s32[128,32]{0,1:T(8,128)}, u32[]{:S(2)}) copy-start(s32[128,32]{0,1:T(8,128)} %param.12) | copy-start | bytes 49156
  7.6 8.3 %copy-start.6 = (s32[1,1,16]{2,1,0:T(1,128)S(1)}, s32[1,1,16]{2,1,0:T(1,128)}, u32[]{:S(2)}) copy-start(s32[1,1,16]{2,1,0:T(1,128)} %patches.1) | copy-start | bytes 196
  7.6 8.3 %copy-start.7 = (s32[1,1,16]{2,1,0:T(1,128)S(1)}, s32[1,1,16]{2,1,0:T(1,128)}, u32[]{:S(2)}) copy-start(s32[1,1,16]{2,1,0:T(1,128)} %sites.1) | copy-start | bytes 196
  10.6 8.8 %collective-permute-start.3 = (bf16[176,256]{1,0:T(8,128)(2,1)S(1)}, bf16[176,256]{1,0:T(8,128)(2,1)S(1)}, u32[]{:S(2)}, u32[]{:S(2)}) collective-permute-start(bf16[176,256]{1,0:T(8,128)(2,1)S(1)} %get-tuple-element.38), channel_id=1, source_target_pairs={{0,28},{4,8},{8,4},{12,16},{16,12},{20,24},{24,20},{28,0},{1,29},{... | collective-permute-start | bytes 270344 | tf_op jit(solution)/shard_map/ppermute | solution.py:630
  15.2 4.6 %collective-permute-start.4 = (bf16[176,256]{1,0:T(8,128)(2,1)S(1)}, bf16[176,256]{1,0:T(8,128)(2,1)S(1)}, u32[]{:S(2)}, u32[]{:S(2)}) collective-permute-start(bf16[176,256]{1,0:T(8,128)(2,1)S(1)} %get-tuple-element.39), channel_id=1, source_target_pairs={{0,4},{4,0},{8,12},{12,8},{16,20},{20,16},{24,28},{28,24},{1,5},{5... | collective-permute-start | bytes 270344 | tf_op jit(solution)/shard_map/ppermute | solution.py:630
  21.0 7.3 %collective-permute-start.5 = (bf16[160,256]{1,0:T(8,128)(2,1)S(1)}, bf16[160,256]{1,0:T(8,128)(2,1)S(1)}, u32[]{:S(2)}, u32[]{:S(2)}) collective-permute-start(bf16[160,256]{1,0:T(8,128)(2,1)S(1)} %get-tuple-element.43), channel_id=1, source_target_pairs={{0,28},{4,8},{8,4},{12,16},{16,12},{20,24},{24,20},{28,0},{1,29},{... | collective-permute-start | bytes 245768 | tf_op jit(solution)/shard_map/ppermute | solution.py:630
  23.7 5.3 %collective-permute-start.6 = (bf16[160,256]{1,0:T(8,128)(2,1)S(1)}, bf16[160,256]{1,0:T(8,128)(2,1)S(1)}, u32[]{:S(2)}, u32[]{:S(2)}) collective-permute-start(bf16[160,256]{1,0:T(8,128)(2,1)S(1)} %get-tuple-element.44), channel_id=1, source_target_pairs={{0,4},{4,0},{8,12},{12,8},{16,20},{20,16},{24,28},{28,24},{1,5},{5... | collective-permute-start | bytes 245768 | tf_op jit(solution)/shard_map/ppermute | solution.py:630
  23.7 4.5 %collective-permute-start.7 = (bf16[16,256]{1,0:T(8,128)(2,1)S(1)}, bf16[16,256]{1,0:T(8,128)(2,1)S(1)}, u32[]{:S(2)}, u32[]{:S(2)}) collective-permute-start(bf16[16,256]{1,0:T(8,128)(2,1)S(1)} %get-tuple-element.56.own), channel_id=1, source_target_pairs={{0,16},{4,20},{8,24},{12,28},{16,0},{20,4},{24,8},{28,12},{1,17},{... | collective-permute-start | bytes 24584 | tf_op jit(solution)/shard_map/ppermute | solution.py:687

commit v5 on v4

--- a/solution.py
+++ b/solution.py
@@ -197,11 +197,15 @@
     chunk = 4
     spans = [pl.ds(i, min(chunk, 27 - i)) for i in range(0, 27, chunk)]
     cells = [
-        pltpu.make_async_copy(omega_in, omega, sems.at[len(spans)]),
-        pltpu.make_async_copy(walls_in, walls, sems.at[len(spans) + 1]),
-        pltpu.make_async_copy(patches_in, patches, sems.at[len(spans) + 2]),
+        pltpu.make_async_copy(omega_in, omega, sems.at[0, len(spans)]),
+        pltpu.make_async_copy(walls_in, walls, sems.at[1, len(spans)]),
+        pltpu.make_async_copy(patches_in, patches, sems.at[0, len(spans) + 1]),
     ]
-    copies = [pltpu.make_async_copy(pops_in.at[span], pops.at[span], sems.at[k]) for k, span in enumerate(spans)]
+    copies = [
+        pltpu.make_async_copy(pops_in.at[span, :, rows, :], pops.at[span, :, rows, :], sems.at[side, k])
+        for k, span in enumerate(spans)
+        for side, rows in enumerate((pl.ds(0, 2), pl.ds(ny - 2, 2)))
+    ]
     start_all(cells + copies)
 
     def read(group, plane, first):
@@ -230,7 +234,8 @@
     own[...] = jnp.concatenate([named, jnp.zeros((SUB, nz), F32)], axis=0).astype(BF16)
     for i in range(27):
         if i % chunk == 0:
-            copies[i // chunk].wait()
+            for copy in copies[i // chunk * 2 : i // chunk * 2 + 2]:
+                copy.wait()
         pack(i)
     for side in range(2):
         for part in range(nz // LANES):
@@ -375,51 +380,90 @@
     return load
 
 
-def middle(mine, load, pops, omega, walls, retain, solid, main2, halo2, macro, read):
+def collide_rows(at, t, f, closed, keep, main2, macro):
+    rows, cols = t
+    out, sums = collide(f, keep)
+    for i in range(27):
+        main2[i, at, rows, cols] = jnp.where(closed, SOLID, out[i])
+    macro[0, at, rows, cols] = sums[0] - 1.0
+    for m in range(1, 4):
+        macro[m, at, rows, cols] = sums[m]
+
+
+def middle_inner_kernel(main, halo, pops, omega, walls, retain, solid, main2, halo2, macro, ready, read):
     planes, ny, nz = omega.shape
-    for at, plane in enumerate(mine):
+    last = planes - 1
+    load = loader(planes, ny, [(main, halo, p) for p in range(planes)])
+    for plane in (*range(1, last), 0, last):
+        inside = 0 < plane < last
         own = walls[plane, :, :] == 1
         for i in range(27):
-            value = pull(load, i, plane)
-            read[i, pl.ds(0, ny), :] = jnp.where(own, pops[i, plane, :, :] * WEIGHT[i], value[:ny])
-            read[i, pl.ds(ny, SUB), :] = value[ny:]
-        for t in range(ny // SUB + 1):
-            for part in range(nz // LANES):
-                rows, cols = pl.ds(SUB * t, SUB), pl.ds(LANES * part, LANES)
-                inner = SUB * t < ny
-                if inner:
-                    closed = walls[plane, rows, cols] == 1
-                    keep = 1.0 - omega[plane, rows, cols]
+            value = pull(load, i, plane) if 0 <= plane - STEP[i][0] <= last else load(26 - i, plane)
+            value = [jnp.where(own, pops[i, plane, :, :] * WEIGHT[i], value[:ny]), value[ny:]]
+            for rows, part in zip((pl.ds(0, ny), pl.ds(ny, SUB)), value):
+                if inside:
+                    read[i, rows, :] = part
                 else:
-                    closed = solid[plane, :, cols] > 0.5
-                    keep = retain[plane, :, cols]
-                out, sums = collide([read[i, rows, cols] for i in range(27)], keep)
-                for i in range(27):
-                    value = jnp.where(closed, SOLID, out[i])
-                    if inner:
-                        main2[i, at, rows, cols] = value
-                    else:
-                        halo2[i, at, :, cols] = value
-                if inner:
-                    macro[0, at, rows, cols] = sums[0] - 1.0
-                    for m in range(1, 4):
-                        macro[m, at, rows, cols] = sums[m]
-
-
-def middle_inner_kernel(main, halo, pops, omega, walls, retain, solid, main2, halo2, macro, read):
-    planes, ny, _ = omega.shape
-    load = loader(planes, ny, [(main, halo, p) for p in range(planes)])
-    middle(range(1, planes - 1), load, pops, omega, walls, retain, solid, main2, halo2, macro, read)
+                    ready[i, int(plane > 0), rows, :] = part
+        if not inside:
+            continue
+        at = plane - 1
+        for part in range(nz // LANES):
+            cols = pl.ds(LANES * part, LANES)
+            for t in range(ny // SUB):
+                rows = pl.ds(SUB * t, SUB)
+                f = [read[i, rows, cols] for i in range(27)]
+                closed = walls[plane, rows, cols] == 1
+                collide_rows(at, (rows, cols), f, closed, 1.0 - omega[plane, rows, cols], main2, macro)
+            out, _ = collide([read[i, pl.ds(ny, SUB), cols] for i in range(27)], retain[plane, :, cols])
+            closed = solid[plane, :, cols] > 0.5
+            for i in range(27):
+                halo2[i, at, :, cols] = jnp.where(closed, SOLID, out[i])
 
 
 def middle_outer_kernel(
-    main, halo, pops, omega, walls, retain, solid, far, near, own, _, __,
+    ready, omega, walls, retain, solid, far, near, own, _,
     main2, halo2, macro, named, send_far, send_near, read, wide,
 ):
-    planes, ny, _ = omega.shape
+    planes, ny, nz = omega.shape
+    last = planes - 1
     widen(far, near, wide, "gx")
-    load = loader(planes, ny, [(main, halo, p) for p in range(planes)], wide)
-    middle((0, planes - 1), load, pops, omega, walls, retain, solid, main2, halo2, macro, read)
+    load = loader(planes, ny, None, wide)
+    sides = ((0, 18), (last, 0))
+    for at, (plane, first) in enumerate(sides):
+        solid_cell = walls[plane, :, :] == 1
+        for k in range(9):
+            value = turned(load(first + k, plane - STEP[first + k][0]), first + k)
+            spare = ready[first + k, at, :, :]
+            shut = value > LIMIT
+            read[k, at, pl.ds(0, ny), :] = jnp.where(solid_cell | shut[:ny], spare[:ny], value[:ny])
+            read[k, at, pl.ds(ny, SUB), :] = jnp.where(shut[ny:], spare[ny:], value[ny:])
+
+    def streamed(at, rows, cols):
+        first = sides[at][1]
+        return [
+            read[i - first, at, rows, cols] if 0 <= i - first < 9 else ready[i, at, rows, cols] for i in range(27)
+        ]
+
+    row = lax.broadcasted_iota(jnp.int32, (SUB, LANES), 0)
+    edge = (row == 0) | (row == SUB - 1)
+    merge = lambda pair: jnp.where(edge, pair[0], pltpu.roll(pair[1], SUB // 2, 0))
+    for part in range(nz // LANES):
+        cols = pl.ds(LANES * part, LANES)
+        for at, (plane, _) in enumerate(sides):
+            for t in range(ny // SUB):
+                rows = pl.ds(SUB * t, SUB)
+                closed = walls[plane, rows, cols] == 1
+                keep = 1.0 - omega[plane, rows, cols]
+                collide_rows(at, (rows, cols), streamed(at, rows, cols), closed, keep, main2, macro)
+        both = [streamed(at, pl.ds(ny, SUB), cols) for at in range(2)]
+        keep = merge([retain[plane, :, cols] for plane, _ in sides])
+        closed = merge([solid[plane, :, cols] for plane, _ in sides]) > 0.5
+        out, _ = collide([merge(pair) for pair in zip(*both)], keep)
+        for i in range(27):
+            value = jnp.where(closed, SOLID, out[i])
+            halo2[i, 0, :, cols] = value
+            halo2[i, 1, :, cols] = pltpu.roll(value, SUB // 2, 0)
     more = merge_named(own[...], wide)
     named[...] = jnp.concatenate([more, jnp.zeros(more.shape, F32)], axis=0).astype(BF16)
     pack_faces(main2, halo2, 1, 1, more, send_far, send_near)
@@ -639,7 +683,7 @@
         [
             pltpu.VMEM(block, F32), pltpu.VMEM(cells, F32), pltpu.VMEM(cells, walls.dtype),
             pltpu.VMEM(sample_patch.shape, sample_patch.dtype),
-            pltpu.VMEM((2, 29, SUB, nz), F32), pltpu.VMEM((2, *beside), F32), dma((10,)),
+            pltpu.VMEM((2, 29, SUB, nz), F32), pltpu.VMEM((2, *beside), F32), dma((2, 9)),
         ],
         cost=1 << 20,
         limit=64800000,
@@ -676,13 +720,20 @@
 
     read = pltpu.VMEM((27, ny + SUB, nz), F32)
     wide, last_wide = (pltpu.VMEM((2, *shape), F32) for shape in (face, last_face))
-    args = (main, halo, populations, omega, walls, retain, solid)
-    main_in, halo_in, macro_in = call(
-        middle_inner_kernel, [VMEM] * 7, relaxed(planes - 2), [read], cost=1 << 22
-    )(*args)
+    main_in, halo_in, macro_in, ready = call(
+        middle_inner_kernel,
+        [VMEM] * 7,
+        relaxed(planes - 2) + [(VMEM, (27, 2, ny + SUB, nz), F32)],
+        [read],
+        cost=1 << 22,
+    )(main, halo, populations, omega, walls, retain, solid)
     main_out, halo_out, macro_out, named, far, near = call(
-        middle_outer_kernel, [VMEM] * 12, relaxed(2) + [(VMEM, (2 * SUB, nz), BF16), *last_faces], [read, wide], cost=1 << 22
-    )(*args, far, near, named, macro_in, pick)
+        middle_outer_kernel,
+        [VMEM] * 9,
+        relaxed(2) + [(VMEM, (2 * SUB, nz), BF16), *last_faces],
+        [pltpu.VMEM((9, 2, ny + SUB, nz), F32), wide],
+        cost=1 << 22,
+    )(ready, omega, walls, retain, solid, far, near, named, pick)
     far, near = swap(far, near, "gx", size_x)
     across = lax.ppermute(named, "gx", [(i, (i + size_x // 2) % size_x) for i in range(size_x)])
 

time: 44.9 us -> 44.3 us (0.987)
  transfers between devices with their start and end apart: 8 -> 8, of which waited for: 5 -> 5; matrix products, arithmetic and copies ran while one was open for 0% -> 0% of each run, Pallas kernels for 14% -> 15%
where the time goes in v5:
time: 44.3 us; the launch traced here: 44.1 us
  blocking collectives  13.7 us (31%)
  Pallas kernels  12.3 us (28%)
  starting transfers between devices  11.2 us (25%)
  waiting for transfers between devices  5.51 us (12%)
  between operations  1.45 us (3%)
    all_to_all x1, blocking collectives, per_device(): received = lax.all_to_all(send, ('gx', 'gy'), 0, 0, tiled=True)  13.7 us
    ppermute x3, starting transfers between devices, swap(): lax.ppermute(far, axis, far_pairs)  9.77 us
    ppermute x1, waiting for transfers between devices, per_device(): lax.ppermute(own, 'gy', [(i, (i + size_y // 2) % size_y) for i in range(s...  2.7 us
    pallas_call x1, Pallas kernels, per_device(): call(functools.partial(slots_kernel, size_y), [VMEM] * 2 + [SMEM] * 3, [(...  2.4 us
    pallas_call x1, Pallas kernels, per_device(): call(functools.partial(rows_kernel, size_y), [HBM] * 4, [(VMEM, beside, B...  2.36 us
    pallas_call x1, Pallas kernels, per_device(): call(last_early_kernel, [VMEM] * 10, [(HBM, block, F32), (VMEM, (2, 9, ny...  1.93 us
    ppermute x1, waiting for transfers between devices, per_device(): lax.ppermute(named, 'gx', [(i, (i + size_x // 2) % size_x) for i in range...  1.88 us
    pallas_call x1, Pallas kernels, per_device(): call(middle_inner_kernel, [VMEM] * 7, relaxed(planes - 2) + [(VMEM, (27,...  1.31 us
  transfers between devices with their start and end apart: 8, of which 5 were waited for; matrix products, arithmetic and copies ran while one was open for 0% of the time, Pallas kernels for 15%

profile of v5, /device:TPU:0, one launch (start us, length us, event | category | flops | bytes accessed | tf_op | source)
XLA Modules:
  0.0 44.1 jit_solution(11723656779497587979)
XLA Ops:
  0.6 0.0 copy-start.2
  0.6 0.0 copy-start
  0.7 2.4 %shard_map.96 = (bf16[160,256]{1,0:T(8,128)(2,1)}, bf16[160,256]{1,0:T(8,128)(2,1)}, bf16[16,256]{1,0:T(8,128)(2,1)}) custom-call(f32[27,4,16,256]{3,2,1,0:T(8,128)} %pops.5, f32[4,16,256]{2,1,0:T(8,128)} %omega.5, s32[4,16,256]{2,1,0:T(8,128)} %walls.9, s32[1,1,16]{2,1,0:T(1,128)} %patches.1), custom_call_target="tpu_custom_call" | custom-call | flops 1048576 | bytes 1048576 | tf_op jit(solution)/shard_map/pallas_call | solution.py:679
  3.0 2.4 %collective-permute-start = (bf16[160,256]{1,0:T(8,128)(2,1)}, bf16[160,256]{1,0:T(8,128)(2,1)S(1)}, u32[]{:S(2)}, u32[]{:S(2)}) collective-permute-start(bf16[160,256]{1,0:T(8,128)(2,1)} %get-tuple-element.33), channel_id=1, source_target_pairs={{0,3},{1,2},{2,1},{3,0},{4,7},{5,6},{6,5},{7,4},{8,11},{9,10},{10,... | collective-permute-start | bytes 245768 | tf_op jit(solution)/shard_map/ppermute | solution.py:674
  5.5 0.7 %collective-permute-start.1 = (bf16[160,256]{1,0:T(8,128)(2,1)}, bf16[160,256]{1,0:T(8,128)(2,1)S(1)}, u32[]{:S(2)}, u32[]{:S(2)}) collective-permute-start(bf16[160,256]{1,0:T(8,128)(2,1)} %get-tuple-element.34), channel_id=1, source_target_pairs={{0,1},{1,0},{2,3},{3,2},{4,5},{5,4},{6,7},{7,6},{8,9},{9,8},{10,11... | collective-permute-start | bytes 245768 | tf_op jit(solution)/shard_map/ppermute | solution.py:674
  6.2 0.1 collective-permute-start.2
  6.2 0.0 copy-done
  6.2 1.1 %shard_map.95.main = f32[27,4,16,256]{3,2,1,0:T(8,128)S(1)} custom-call(f32[27,4,16,256]{3,2,1,0:T(8,128)S(1)} %copy-done, f32[4,16,256]{2,1,0:T(8,128)S(1)} %copy-done.3, s32[4,16,256]{2,1,0:T(8,128)S(1)} %copy-done.2), custom_call_target="tpu_custom_call" | custom-call | flops 4194304 | bytes 4194304 | tf_op jit(solution)/shard_map/pallas_call | solution.py:704
  7.3 0.0 copy-start.4
  7.3 0.0 copy-start.6
  7.3 0.0 copy-start.7
  7.3 2.7 %collective-permute-done.2.across = bf16[16,256]{1,0:T(8,128)(2,1)S(1)} collective-permute-done((bf16[16,256]{1,0:T(8,128)(2,1)}, bf16[16,256]{1,0:T(8,128)(2,1)S(1)}, u32[]{:S(2)}, u32[]{:S(2)}) %collective-permute-start.2) | collective-permute-done | bytes 8224 | tf_op jit(solution)/shard_map/ppermute | solution.py:692
  10.0 0.0 collective-permute-done.far
  10.0 0.0 collective-permute-done.1.near
  10.0 0.2 shard_map.97
  10.3 4.6 %collective-permute-start.3 = (bf16[176,256]{1,0:T(8,128)(2,1)S(1)}, bf16[176,256]{1,0:T(8,128)(2,1)S(1)}, u32[]{:S(2)}, u32[]{:S(2)}) collective-permute-start(bf16[176,256]{1,0:T(8,128)(2,1)S(1)} %get-tuple-element.40), channel_id=1, source_target_pairs={{0,28},{4,8},{8,4},{12,16},{16,12},{20,24},{24,20},{28,0},{1,29},{... | collective-permute-start | bytes 270344 | tf_op jit(solution)/shard_map/ppermute | solution.py:674
  14.9 0.0 collective-permute-start.4
  15.6 2.4 %shard_map.99 = (bf16[2,16,64]{2,1,0:T(8,128)(2,1)S(1)}, bf16[32,8,128]{2,1,0:T(8,128)(2,1)S(1)}, bf16[128,128]{1,0:T(8,128)(2,1)S(1)}, bf16[512,4096]{1,0:T(8,128)(2,1)S(1)}) custom-call(s32[32,128]{1,0:T(8,128)S(1)} %bitcast.1, bf16[4096,512]{1,0:T(8,128)(2,1)S(1)} %copy-done.1, s32[1,1]{1,0:T(1,128)S(6)} %copy.12.counts, s32[1,1,16]{2,1,0:T(1,128)S(1)} %copy-done.7, ...), custom_call_target="tpu_custom_call" | custom-call | flops 4194304 | bytes 4194304 | tf_op jit(solution)/shard_map/pallas_call | solution.py:693
  18.0 1.3 %shard_map.98 = (f32[27,2,16,256]{3,2,1,0:T(8,128)S(1)}, f32[27,2,8,256]{3,2,1,0:T(8,128)S(1)}, f32[4,2,16,256]{3,2,1,0:T(8,128)S(1)}, f32[27,2,24,256]{3,2,1,0:T(8,128)S(1)}) custom-call(f32[27,4,16,256]{3,2,1,0:T(8,128)S(1)} %shard_map.95.main, f32[27,4,8,256]{3,2,1,0:T(8,128)S(1)} %get-tuple-element.36.halo, f32[27,4,16,256]{3,2,1,0:T(8,128)S(1)} %copy-done, ...), custom_call_target="tpu_custom_call" | custom-call | flops 4194304 | bytes 4194304 | tf_op jit(solution)/shard_map/pallas_call | solution.py:723
  19.3 0.0 collective-permute-done.3.far
  19.3 0.2 collective-permute-done.4.near
  19.5 0.8 %shard_map.100 = (f32[27,2,16,256]{3,2,1,0:T(8,128)S(1)}, f32[27,2,8,256]{3,2,1,0:T(8,128)S(1)}, f32[4,2,16,256]{3,2,1,0:T(8,128)S(1)}, bf16[16,256]{1,0:T(8,128...) custom-call(f32[27,2,24,256]{3,2,1,0:T(8,128)S(1)} %get-tuple-element.39.ready, ...), custom_call_target="tpu_custom_call" | custom-call | flops 4194304 | bytes 4194304 | tf_op jit(solution)/shard_map/pallas_call | solution.py:730
  20.3 2.7 %collective-permute-start.5 = (bf16[160,256]{1,0:T(8,128)(2,1)S(1)}, bf16[160,256]{1,0:T(8,128)(2,1)S(1)}, u32[]{:S(2)}, u32[]{:S(2)}) collective-permute-start(bf16[160,256]{1,0:T(8,128)(2,1)S(1)} %get-tuple-element.44), channel_id=1, source_target_pairs={{0,28},{4,8},{8,4},{12,16},{16,12},{20,24},{24,20},{28,0},{1,29},{... | collective-permute-start | bytes 245768 | tf_op jit(solution)/shard_map/ppermute | solution.py:674
  23.0 0.0 collective-permute-start.6
  23.0 0.7 %collective-permute-start.7 = (bf16[16,256]{1,0:T(8,128)(2,1)S(1)}, bf16[16,256]{1,0:T(8,128)(2,1)S(1)}, u32[]{:S(2)}, u32[]{:S(2)}) collective-permute-start(bf16[16,256]{1,0:T(8,128)(2,1)S(1)} %get-tuple-element.58.own), channel_id=1, source_target_pairs={{0,16},{4,20},{8,24},{12,28},{16,0},{20,4},{24,8},{28,12},{1,17},{... | collective-permute-start | bytes 24584 | tf_op jit(solution)/shard_map/ppermute | solution.py:738
  23.8 1.9 %shard_map.101 = (f32[27,4,16,256]{3,2,1,0:T(8,128)}, f32[2,9,16,256]{3,2,1,0:T(8,128)S(1)}, f32[4,2,16,256]{3,2,1,0:T(8,128)S(1)}, f32[4,2,16,256]{3,2,1,0:T(8,128)S(1)}, bf16[32,16,128]{2,1,0:T(8,128)(2,1)S(1)}) custom-call(f32[27,2,16,256]{3,2,1,0:T(8,128)S(1)} %get-tuple-element.46.main_in, f32[27,2,8,256]{3,2,1,0:T(8,128)S(1)} %get-tuple-element.47.halo_in, ...), custom_call_target="tpu_custom_call" | custom-call | flops 4194304 | bytes 4194304 | tf_op jit(solution)/shard_map/pallas_call | solution.py:742
  25.7 1.9 %collective-permute-done.7.across = bf16[16,256]{1,0:T(8,128)(2,1)S(1)} collective-permute-done((bf16[16,256]{1,0:T(8,128)(2,1)S(1)}, bf16[16,256]{1,0:T(8,128)(2,1)S(1)}, u32[]{:S(2)}, u32[]{:S(2)}) %collective-permute-start.7) | collective-permute-done | bytes 8224 | tf_op jit(solution)/shard_map/ppermute | solution.py:738
  27.6 0.1 collective-permute-done.5.far
  27.6 0.7 %collective-permute-done.6.near = bf16[160,256]{1,0:T(8,128)(2,1)S(1)} collective-permute-done((bf16[160,256]{1,0:T(8,128)(2,1)S(1)}, bf16[160,256]{1,0:T(8,128)(2,1)S(1)}, u32[]{:S(2)}, u32[]{:S(2)}) %collective-permute-start.6) | collective-permute-done | bytes 81952 | tf_op jit(solution)/shard_map/ppermute | solution.py:674
  28.4 1.0 %shard_map.102 = (f32[27,4,16,256]{3,2,1,0:T(8,128)}, bf16[32,32,128]{2,1,0:T(8,128)(2,1)S(1)}, f32[8,256]{1,0:T(8,128)S(1)}) custom-call(bf16[160,256]{1,0:T(8,128)(2,1)S(1)} %collective-permute-done.5.far, bf16[160,256]{1,0:T(8,128)(2,1)S(1)} %collective-permute-done.6.near, s32[4,16,256]{2,1,0:T(8,128)S(1)} %copy-done.2, ...), custom_call_target="tpu_custom_call", output_to_operand_aliasing={{0}: (12, {})} | custom-call | flops 4194304 | bytes 4194304 | tf_op jit(solution)/shard_map/pallas_call | solution.py:757
  29.3 13.7 %all_to_all.5.received = bf16[32,32,128]{2,1,0:T(8,128)(2,1)S(1)} all-to-all(bf16[32,32,128]{2,1,0:T(8,128)(2,1)S(1)} %get-tuple-element.61), channel_id=1, replica_groups=mesh['gx'=8,'gy'=4] {'gx','gy'}, dimensions={0} | all-to-all | bytes 524288 | tf_op jit(solution)/shard_map/all_to_all | solution.py:765
  43.0 1.1 %shard_map.103 = f32[128,128]{1,0:T(8,128)} custom-call(bf16[32,32,128]{2,1,0:T(8,128)(2,1)S(1)} %all_to_all.5.received, f32[8,256]{1,0:T(8,128)S(1)} %get-tuple-element.62.named, bf16[128,128]{1,0:T(8,128)(2,1)S(1)} %get-tuple-element.63.own_bins), custom_call_target="tpu_custom_call" | custom-call | flops 1048576 | bytes 1048576 | tf_op jit(solution)/shard_map/pallas_call | solution.py:770
  (10 shorter events, 0.0 us)
Async XLA Ops:
  0.6 5.6 %copy-start.2 = (s32[4,16,256]{2,1,0:T(8,128)S(1)}, s32[4,16,256]{2,1,0:T(8,128)}, u32[]{:S(2)}) copy-start(s32[4,16,256]{2,1,0:T(8,128)} %walls.9) | copy-start | bytes 196612
  0.6 5.6 %copy-start = (f32[27,4,16,256]{3,2,1,0:T(8,128)S(1)}, f32[27,4,16,256]{3,2,1,0:T(8,128)}, u32[]{:S(2)}) copy-start(f32[27,4,16,256]{3,2,1,0:T(8,128)} %pops.5) | copy-start | bytes 5308420
  0.6 5.6 %copy-start.3 = (f32[4,16,256]{2,1,0:T(8,128)S(1)}, f32[4,16,256]{2,1,0:T(8,128)}, u32[]{:S(2)}) copy-start(f32[4,16,256]{2,1,0:T(8,128)} %omega.5) | copy-start | bytes 196612
  3.0 7.0 %collective-permute-start = (bf16[160,256]{1,0:T(8,128)(2,1)}, bf16[160,256]{1,0:T(8,128)(2,1)S(1)}, u32[]{:S(2)}, u32[]{:S(2)}) collective-permute-start(bf16[160,256]{1,0:T(8,128)(2,1)} %get-tuple-element.33), channel_id=1, source_target_pairs={{0,3},{1,2},{2,1},{3,0},{4,7},{5,6},{6,5},{7,4},{8,11},{9,10},{10,... | collective-permute-start | bytes 245768 | tf_op jit(solution)/shard_map/ppermute | solution.py:674
  5.5 4.5 %collective-permute-start.1 = (bf16[160,256]{1,0:T(8,128)(2,1)}, bf16[160,256]{1,0:T(8,128)(2,1)S(1)}, u32[]{:S(2)}, u32[]{:S(2)}) collective-permute-start(bf16[160,256]{1,0:T(8,128)(2,1)} %get-tuple-element.34), channel_id=1, source_target_pairs={{0,1},{1,0},{2,3},{3,2},{4,5},{5,4},{6,7},{7,6},{8,9},{9,8},{10,11... | collective-permute-start | bytes 245768 | tf_op jit(solution)/shard_map/ppermute | solution.py:674
  6.1 3.9 %copy-start.5 = (bf16[16,256]{1,0:T(8,128)(2,1)S(1)}, bf16[16,256]{1,0:T(8,128)(2,1)}, u32[]{:S(2)}) copy-start(bf16[16,256]{1,0:T(8,128)(2,1)} %get-tuple-element.35.own) | copy-start | bytes 24580
  6.2 3.9 %collective-permute-start.2 = (bf16[16,256]{1,0:T(8,128)(2,1)}, bf16[16,256]{1,0:T(8,128)(2,1)S(1)}, u32[]{:S(2)}, u32[]{:S(2)}) collective-permute-start(bf16[16,256]{1,0:T(8,128)(2,1)} %get-tuple-element.35.own), channel_id=1, source_target_pairs={{0,2},{1,3},{2,0},{3,1},{4,6},{5,7},{6,4},{7,5},{8,10},{9,11},{10,... | collective-permute-start | bytes 24584 | tf_op jit(solution)/shard_map/ppermute | solution.py:692
  6.2 9.3 %copy-start.1 = (bf16[4096,512]{1,0:T(8,128)(2,1)S(1)}, bf16[4096,512]{1,0:T(8,128)(2,1)}, u32[]{:S(2)}) copy-start(bf16[4096,512]{1,0:T(8,128)(2,1)} %radiation.1) | copy-start | bytes 12582916
  7.3 8.3 %copy-start.4 = (s32[128,32]{0,1:T(8,128)S(1)}, s32[128,32]{0,1:T(8,128)}, u32[]{:S(2)}) copy-start(s32[128,32]{0,1:T(8,128)} %param.12) | copy-start | bytes 49156
  7.3 8.3 %copy-start.6 = (s32[1,1,16]{2,1,0:T(1,128)S(1)}, s32[1,1,16]{2,1,0:T(1,128)}, u32[]{:S(2)}) copy-start(s32[1,1,16]{2,1,0:T(1,128)} %patches.1) | copy-start | bytes 196
  7.3 8.3 %copy-start.7 = (s32[1,1,16]{2,1,0:T(1,128)S(1)}, s32[1,1,16]{2,1,0:T(1,128)}, u32[]{:S(2)}) copy-start(s32[1,1,16]{2,1,0:T(1,128)} %sites.1) | copy-start | bytes 196
  10.3 9.1 %collective-permute-start.3 = (bf16[176,256]{1,0:T(8,128)(2,1)S(1)}, bf16[176,256]{1,0:T(8,128)(2,1)S(1)}, u32[]{:S(2)}, u32[]{:S(2)}) collective-permute-start(bf16[176,256]{1,0:T(8,128)(2,1)S(1)} %get-tuple-element.40), channel_id=1, source_target_pairs={{0,28},{4,8},{8,4},{12,16},{16,12},{20,24},{24,20},{28,0},{1,29},{... | collective-permute-start | bytes 270344 | tf_op jit(solution)/shard_map/ppermute | solution.py:674
  14.9 4.6 %collective-permute-start.4 = (bf16[176,256]{1,0:T(8,128)(2,1)S(1)}, bf16[176,256]{1,0:T(8,128)(2,1)S(1)}, u32[]{:S(2)}, u32[]{:S(2)}) collective-permute-start(bf16[176,256]{1,0:T(8,128)(2,1)S(1)} %get-tuple-element.41), channel_id=1, source_target_pairs={{0,4},{4,0},{8,12},{12,8},{16,20},{20,16},{24,28},{28,24},{1,5},{5... | collective-permute-start | bytes 270344 | tf_op jit(solution)/shard_map/ppermute | solution.py:674
  20.3 7.3 %collective-permute-start.5 = (bf16[160,256]{1,0:T(8,128)(2,1)S(1)}, bf16[160,256]{1,0:T(8,128)(2,1)S(1)}, u32[]{:S(2)}, u32[]{:S(2)}) collective-permute-start(bf16[160,256]{1,0:T(8,128)(2,1)S(1)} %get-tuple-element.44), channel_id=1, source_target_pairs={{0,28},{4,8},{8,4},{12,16},{16,12},{20,24},{24,20},{28,0},{1,29},{... | collective-permute-start | bytes 245768 | tf_op jit(solution)/shard_map/ppermute | solution.py:674
  23.0 5.3 %collective-permute-start.6 = (bf16[160,256]{1,0:T(8,128)(2,1)S(1)}, bf16[160,256]{1,0:T(8,128)(2,1)S(1)}, u32[]{:S(2)}, u32[]{:S(2)}) collective-permute-start(bf16[160,256]{1,0:T(8,128)(2,1)S(1)} %get-tuple-element.45), channel_id=1, source_target_pairs={{0,4},{4,0},{8,12},{12,8},{16,20},{20,16},{24,28},{28,24},{1,5},{5... | collective-permute-start | bytes 245768 | tf_op jit(solution)/shard_map/ppermute | solution.py:674
  23.0 4.5 %collective-permute-start.7 = (bf16[16,256]{1,0:T(8,128)(2,1)S(1)}, bf16[16,256]{1,0:T(8,128)(2,1)S(1)}, u32[]{:S(2)}, u32[]{:S(2)}) collective-permute-start(bf16[16,256]{1,0:T(8,128)(2,1)S(1)} %get-tuple-element.58.own), channel_id=1, source_target_pairs={{0,16},{4,20},{8,24},{12,28},{16,0},{20,4},{24,8},{28,12},{1,17},{... | collective-permute-start | bytes 24584 | tf_op jit(solution)/shard_map/ppermute | solution.py:738

commit v6 on v5

--- a/solution.py
+++ b/solution.py
@@ -316,7 +316,7 @@
     pack_x(main, halo, (1 - odd) * last, (1 - odd) * 18, reach, named, near)
 
 
-def first_halo_kernel(far, near, main, own, across, halo, retain, solid, named, send_far, send_near, wide):
+def first_halo_kernel(near, far, main, own, across, halo, retain, solid, named, send_far, send_near, wide):
     _, planes, _, nz = halo.shape
     row = lax.broadcasted_iota(jnp.int32, (SUB, nz), 0)
     widen(far, near, wide, "gy")
@@ -493,28 +493,9 @@
     return response.astype(BF16)
 
 
-def slots_kernel(size_y, bins, radiation, counts, sites, patches, pick, level, own_bins, turned_radiation):
-    halves, slots, lines = pick.shape
-    slot = lax.broadcasted_iota(jnp.int32, (slots, lines), 0)
-    line = lax.broadcasted_iota(jnp.int32, (slots, lines), 1)
-    wanted = jnp.full((slots, lines), -1, jnp.int32)
-    for k in range(slots):
-        site = jnp.where(k < counts[0, 0], sites[0, 0, k], -halves)
-        wanted = jnp.where(slot == k, site, wanted)
-    for h in range(halves):
-        pick[h, :, :] = (wanted == line * halves + h).astype(BF16)
-
-    n_patch = bins.shape[1]
-    slot = lax.broadcasted_iota(jnp.int32, (slots, n_patch), 0)
-    named = lax.broadcasted_iota(jnp.int32, (slots, n_patch), 1)
-    wanted = jnp.full((slots, n_patch), -1, jnp.int32)
-    for k in range(slots):
-        wanted = jnp.where(slot == k, patches[0, 0, k], wanted)
-    chosen = (wanted == named).astype(BF16)
-    per_block = lax.dot_general(
-        chosen, bins[...].astype(F32).astype(BF16), (((1,), (1,)), ((), ())), preferred_element_type=F32
-    )
+def fill_levels(per_block, level):
     devices, _, width = level.shape
+    slots = per_block.shape[0]
     groups = slots // SUB
     group = lax.broadcasted_iota(jnp.int32, (SUB, width), 1) // (width // groups)
     tiles = {}
@@ -529,6 +510,31 @@
             tiles[blk] = tile.astype(BF16)
         level[d, :, :] = tiles[blk]
 
+
+def slots_kernel(size_y, ride, bins, radiation, counts, sites, patches, pick, level, own_bins, turned_radiation):
+    halves, slots, lines = pick.shape
+    slot = lax.broadcasted_iota(jnp.int32, (slots, lines), 0)
+    line = lax.broadcasted_iota(jnp.int32, (slots, lines), 1)
+    wanted = jnp.full((slots, lines), -1, jnp.int32)
+    for k in range(slots):
+        wanted = jnp.where(slot == k, sites[0, 0, k], wanted)
+    wanted = jnp.where(slot < jnp.broadcast_to(counts[...], slot.shape), wanted, -halves)
+    for h in range(halves):
+        pick[h, :, :] = (wanted == line * halves + h).astype(BF16)
+
+    n_patch = bins.shape[1]
+    slot = lax.broadcasted_iota(jnp.int32, (slots, n_patch), 0)
+    named = lax.broadcasted_iota(jnp.int32, (slots, n_patch), 1)
+    wanted = jnp.full((slots, n_patch), -1, jnp.int32)
+    for k in range(slots):
+        wanted = jnp.where(slot == k, patches[0, 0, k], wanted)
+    chosen = (wanted == named).astype(BF16)
+    per_block = lax.dot_general(
+        chosen, bins[...].astype(F32).astype(BF16), (((1,), (1,)), ((), ())), preferred_element_type=F32
+    )
+    devices, _, width = level.shape
+    if not ride:
+        fill_levels(per_block, level)
     place = lax.axis_index("gx") * size_y + lax.axis_index("gy")
     mine = bins[pl.ds(lax.div(place * width, OBS_BLK), 1), :].astype(F32)
     own_bins[...] = jnp.broadcast_to(mine, own_bins.shape).astype(BF16)
@@ -667,6 +673,7 @@
     size_x, size_y = lax.axis_size("gx"), lax.axis_size("gy")
     devices = size_x * size_y
     width = radiation.shape[0] // devices
+    ride = (size_x, size_y) == (8, 4)
 
     def swap(far, near, axis, size):
         far_pairs = [(i, (i - 1 + 2 * (i % 2)) % size) for i in range(size)]
@@ -691,8 +698,8 @@
     far, near = swap(far, near, "gy", size_y)
     across = lax.ppermute(own, "gy", [(i, (i + size_y // 2) % size_y) for i in range(size_y)])
     pick, level, own_bins, radiation = call(
-        functools.partial(slots_kernel, size_y),
-        [VMEM] * 2 + [SMEM] * 3,
+        functools.partial(slots_kernel, size_y, ride),
+        [VMEM] * 3 + [SMEM] * 2,
         [
             (VMEM, (nz // LANES, slots, planes * ny), BF16),
             (VMEM, (devices, SUB, width), BF16),
@@ -712,7 +719,7 @@
         [(VMEM, (27, *edge), F32), (VMEM, edge, F32), (VMEM, edge, F32), (VMEM, (SUB, nz), F32), *faces],
         [pltpu.VMEM((2, *beside), F32)],
         cost=1 << 20,
-    )(far, near, main, own, across)
+    )(near, far, main, own, across)
     far, near = swap(far, near, "gx", size_x)
 
     def relaxed(n):
@@ -752,7 +759,6 @@
         [pltpu.VMEM(block, F32), fields, dma((planes,))],
         cost=1 << 22,
     )(main_in, halo_in, main_out, halo_out, populations, walls, macro_in, macro_out, radiation, pick)
-    ride = (size_x, size_y) == (8, 4)
     sent = 2 * slots if ride else 2 * slots + SUB
     advanced, send, named = call(
         last_kernel,

time: 44.3 us -> 44.2 us (level)
  transfers between devices with their start and end apart: 8 -> 8, of which waited for: 5 -> 4; matrix products, arithmetic and copies ran while one was open for 0% -> 0% of each run, Pallas kernels for 15% -> 15%
where the time goes in v6:
time: 44.2 us; the launch traced here: 44 us
  blocking collectives  13.5 us (31%)
  Pallas kernels  12.1 us (27%)
  starting transfers between devices  11.1 us (25%)
  waiting for transfers between devices  5.81 us (13%)
  between operations  1.45 us (3%)
    all_to_all x1, blocking collectives, per_device(): received = lax.all_to_all(send, ('gx', 'gy'), 0, 0, tiled=True)  13.5 us
    ppermute x3, starting transfers between devices, swap(): lax.ppermute(far, axis, far_pairs)  9.94 us
    ppermute x1, waiting for transfers between devices, per_device(): lax.ppermute(own, 'gy', [(i, (i + size_y // 2) % size_y) for i in range(s...  2.7 us
    pallas_call x1, Pallas kernels, per_device(): call(functools.partial(rows_kernel, size_y), [HBM] * 4, [(VMEM, beside, B...  2.36 us
    pallas_call x1, Pallas kernels, per_device(): call(functools.partial(slots_kernel, size_y, ride), [VMEM] * 3 + [SMEM] *...  2.21 us
    ppermute x1, waiting for transfers between devices, per_device(): lax.ppermute(named, 'gx', [(i, (i + size_x // 2) % size_x) for i in range...  2.03 us
    pallas_call x1, Pallas kernels, per_device(): call(last_early_kernel, [VMEM] * 10, [(HBM, block, F32), (VMEM, (2, 9, ny...  1.93 us
    pallas_call x1, Pallas kernels, per_device(): call(middle_inner_kernel, [VMEM] * 7, relaxed(planes - 2) + [(VMEM, (27,...  1.31 us
  transfers between devices with their start and end apart: 8, of which 4 were waited for; matrix products, arithmetic and copies ran while one was open for 0% of the time, Pallas kernels for 15%

profile of v6, /device:TPU:0, one launch (start us, length us, event | category | flops | bytes accessed | tf_op | source)
XLA Modules:
  0.0 44.0 jit_solution(7514001655572830540)
XLA Ops:
  0.7 2.4 %shard_map.96 = (bf16[160,256]{1,0:T(8,128)(2,1)}, bf16[160,256]{1,0:T(8,128)(2,1)}, bf16[16,256]{1,0:T(8,128)(2,1)}) custom-call(f32[27,4,16,256]{3,2,1,0:T(8,128)} %pops.5, f32[4,16,256]{2,1,0:T(8,128)} %omega.5, s32[4,16,256]{2,1,0:T(8,128)} %walls.9, s32[1,1,16]{2,1,0:T(1,128)} %patches.1), custom_call_target="tpu_custom_call" | custom-call | flops 1048576 | bytes 1048576 | tf_op jit(solution)/shard_map/pallas_call | solution.py:686
  3.0 0.5 %collective-permute-start = (bf16[160,256]{1,0:T(8,128)(2,1)}, bf16[160,256]{1,0:T(8,128)(2,1)S(1)}, u32[]{:S(2)}, u32[]{:S(2)}) collective-permute-start(bf16[160,256]{1,0:T(8,128)(2,1)} %get-tuple-element.33), channel_id=1, source_target_pairs={{0,1},{1,0},{2,3},{3,2},{4,5},{5,4},{6,7},{7,6},{8,9},{9,8},{10,11... | collective-permute-start | bytes 245768 | tf_op jit(solution)/shard_map/ppermute | solution.py:681
  3.5 2.6 %collective-permute-start.1 = (bf16[160,256]{1,0:T(8,128)(2,1)}, bf16[160,256]{1,0:T(8,128)(2,1)S(1)}, u32[]{:S(2)}, u32[]{:S(2)}) collective-permute-start(bf16[160,256]{1,0:T(8,128)(2,1)} %get-tuple-element.34), channel_id=1, source_target_pairs={{0,3},{1,2},{2,1},{3,0},{4,7},{5,6},{6,5},{7,4},{8,11},{9,10},{10,... | collective-permute-start | bytes 245768 | tf_op jit(solution)/shard_map/ppermute | solution.py:681
  6.2 0.1 collective-permute-start.2
  6.2 0.0 copy-done.2
  6.2 0.0 copy-done.3
  6.2 1.1 %shard_map.95.main = f32[27,4,16,256]{3,2,1,0:T(8,128)S(1)} custom-call(f32[27,4,16,256]{3,2,1,0:T(8,128)S(1)} %copy-done, f32[4,16,256]{2,1,0:T(8,128)S(1)} %copy-done.3, s32[4,16,256]{2,1,0:T(8,128)S(1)} %copy-done.2), custom_call_target="tpu_custom_call" | custom-call | flops 4194304 | bytes 4194304 | tf_op jit(solution)/shard_map/pallas_call | solution.py:711
  7.3 0.0 copy-start.4
  7.3 0.0 copy-start.6
  7.3 0.0 copy-start.7
  7.3 2.7 %collective-permute-done.2.across = bf16[16,256]{1,0:T(8,128)(2,1)S(1)} collective-permute-done((bf16[16,256]{1,0:T(8,128)(2,1)}, bf16[16,256]{1,0:T(8,128)(2,1)S(1)}, u32[]{:S(2)}, u32[]{:S(2)}) %collective-permute-start.2) | collective-permute-done | bytes 8224 | tf_op jit(solution)/shard_map/ppermute | solution.py:699
  10.0 0.0 collective-permute-done.near
  10.0 0.0 collective-permute-done.1.far
  10.0 0.0 copy-done.5
  10.0 0.2 shard_map.97
  10.3 4.6 %collective-permute-start.3 = (bf16[176,256]{1,0:T(8,128)(2,1)S(1)}, bf16[176,256]{1,0:T(8,128)(2,1)S(1)}, u32[]{:S(2)}, u32[]{:S(2)}) collective-permute-start(bf16[176,256]{1,0:T(8,128)(2,1)S(1)} %get-tuple-element.40), channel_id=1, source_target_pairs={{0,28},{4,8},{8,4},{12,16},{16,12},{20,24},{24,20},{28,0},{1,29},{... | collective-permute-start | bytes 270344 | tf_op jit(solution)/shard_map/ppermute | solution.py:681
  14.9 0.0 collective-permute-start.4
  15.6 2.2 %shard_map.99 = (bf16[2,16,64]{2,1,0:T(8,128)(2,1)S(1)}, bf16[32,8,128]{2,1,0:T(8,128)(2,1)S(1)}, bf16[128,128]{1,0:T(8,128)(2,1)S(1)}, bf16[512,4096]{1,0:T(8,128)(2,1)S(1)}) custom-call(s32[32,128]{1,0:T(8,128)S(1)} %bitcast.1, bf16[4096,512]{1,0:T(8,128)(2,1)S(1)} %copy-done.1, s32[1,1]{1,0:T(1,128)S(6)} %copy.12.counts, s32[1,1,16]{2,1,0:T(1,128)S(1)} %copy-done.7, ...), custom_call_target="tpu_custom_call" | custom-call | flops 4194304 | bytes 4194304 | tf_op jit(solution)/shard_map/pallas_call | solution.py:700
  17.8 1.3 %shard_map.98 = (f32[27,2,16,256]{3,2,1,0:T(8,128)S(1)}, f32[27,2,8,256]{3,2,1,0:T(8,128)S(1)}, f32[4,2,16,256]{3,2,1,0:T(8,128)S(1)}, f32[27,2,24,256]{3,2,1,0:T(8,128)S(1)}) custom-call(f32[27,4,16,256]{3,2,1,0:T(8,128)S(1)} %shard_map.95.main, f32[27,4,8,256]{3,2,1,0:T(8,128)S(1)} %get-tuple-element.36.halo, f32[27,4,16,256]{3,2,1,0:T(8,128)S(1)} %copy-done, ...), custom_call_target="tpu_custom_call" | custom-call | flops 4194304 | bytes 4194304 | tf_op jit(solution)/shard_map/pallas_call | solution.py:730
  19.1 0.0 collective-permute-done.3.far
  19.1 0.4 collective-permute-done.4.near
  19.5 0.8 %shard_map.100 = (f32[27,2,16,256]{3,2,1,0:T(8,128)S(1)}, f32[27,2,8,256]{3,2,1,0:T(8,128)S(1)}, f32[4,2,16,256]{3,2,1,0:T(8,128)S(1)}, bf16[16,256]{1,0:T(8,128...) custom-call(f32[27,2,24,256]{3,2,1,0:T(8,128)S(1)} %get-tuple-element.39.ready, ...), custom_call_target="tpu_custom_call" | custom-call | flops 4194304 | bytes 4194304 | tf_op jit(solution)/shard_map/pallas_call | solution.py:737
  20.4 2.7 %collective-permute-start.5 = (bf16[160,256]{1,0:T(8,128)(2,1)S(1)}, bf16[160,256]{1,0:T(8,128)(2,1)S(1)}, u32[]{:S(2)}, u32[]{:S(2)}) collective-permute-start(bf16[160,256]{1,0:T(8,128)(2,1)S(1)} %get-tuple-element.44), channel_id=1, source_target_pairs={{0,28},{4,8},{8,4},{12,16},{16,12},{20,24},{24,20},{28,0},{1,29},{... | collective-permute-start | bytes 245768 | tf_op jit(solution)/shard_map/ppermute | solution.py:681
  23.1 0.0 collective-permute-start.6
  23.1 0.6 %collective-permute-start.7 = (bf16[16,256]{1,0:T(8,128)(2,1)S(1)}, bf16[16,256]{1,0:T(8,128)(2,1)S(1)}, u32[]{:S(2)}, u32[]{:S(2)}) collective-permute-start(bf16[16,256]{1,0:T(8,128)(2,1)S(1)} %get-tuple-element.58.own), channel_id=1, source_target_pairs={{0,16},{4,20},{8,24},{12,28},{16,0},{20,4},{24,8},{28,12},{1,17},{... | collective-permute-start | bytes 24584 | tf_op jit(solution)/shard_map/ppermute | solution.py:745
  23.7 1.9 %shard_map.101 = (f32[27,4,16,256]{3,2,1,0:T(8,128)}, f32[2,9,16,256]{3,2,1,0:T(8,128)S(1)}, f32[4,2,16,256]{3,2,1,0:T(8,128)S(1)}, f32[4,2,16,256]{3,2,1,0:T(8,128)S(1)}, bf16[32,16,128]{2,1,0:T(8,128)(2,1)S(1)}) custom-call(f32[27,2,16,256]{3,2,1,0:T(8,128)S(1)} %get-tuple-element.46.main_in, f32[27,2,8,256]{3,2,1,0:T(8,128)S(1)} %get-tuple-element.47.halo_in, ...), custom_call_target="tpu_custom_call" | custom-call | flops 4194304 | bytes 4194304 | tf_op jit(solution)/shard_map/pallas_call | solution.py:749
  25.6 2.0 %collective-permute-done.7.across = bf16[16,256]{1,0:T(8,128)(2,1)S(1)} collective-permute-done((bf16[16,256]{1,0:T(8,128)(2,1)S(1)}, bf16[16,256]{1,0:T(8,128)(2,1)S(1)}, u32[]{:S(2)}, u32[]{:S(2)}) %collective-permute-start.7) | collective-permute-done | bytes 8224 | tf_op jit(solution)/shard_map/ppermute | solution.py:745
  27.7 0.0 collective-permute-done.5.far
  27.7 0.7 %collective-permute-done.6.near = bf16[160,256]{1,0:T(8,128)(2,1)S(1)} collective-permute-done((bf16[160,256]{1,0:T(8,128)(2,1)S(1)}, bf16[160,256]{1,0:T(8,128)(2,1)S(1)}, u32[]{:S(2)}, u32[]{:S(2)}) %collective-permute-start.6) | collective-permute-done | bytes 81952 | tf_op jit(solution)/shard_map/ppermute | solution.py:681
  28.4 1.0 %shard_map.102 = (f32[27,4,16,256]{3,2,1,0:T(8,128)}, bf16[32,32,128]{2,1,0:T(8,128)(2,1)S(1)}, f32[8,256]{1,0:T(8,128)S(1)}) custom-call(bf16[160,256]{1,0:T(8,128)(2,1)S(1)} %collective-permute-done.5.far, bf16[160,256]{1,0:T(8,128)(2,1)S(1)} %collective-permute-done.6.near, s32[4,16,256]{2,1,0:T(8,128)S(1)} %copy-done.2, ...), custom_call_target="tpu_custom_call", output_to_operand_aliasing={{0}: (12, {})} | custom-call | flops 4194304 | bytes 4194304 | tf_op jit(solution)/shard_map/pallas_call | solution.py:763
  29.4 13.5 %all_to_all.5.received = bf16[32,32,128]{2,1,0:T(8,128)(2,1)S(1)} all-to-all(bf16[32,32,128]{2,1,0:T(8,128)(2,1)S(1)} %get-tuple-element.61), channel_id=1, replica_groups=mesh['gx'=8,'gy'=4] {'gx','gy'}, dimensions={0} | all-to-all | bytes 524288 | tf_op jit(solution)/shard_map/all_to_all | solution.py:771
  42.9 1.1 %shard_map.103 = f32[128,128]{1,0:T(8,128)} custom-call(bf16[32,32,128]{2,1,0:T(8,128)(2,1)S(1)} %all_to_all.5.received, f32[8,256]{1,0:T(8,128)S(1)} %get-tuple-element.62.named, bf16[128,128]{1,0:T(8,128)(2,1)S(1)} %get-tuple-element.63.own_bins), custom_call_target="tpu_custom_call" | custom-call | flops 1048576 | bytes 1048576 | tf_op jit(solution)/shard_map/pallas_call | solution.py:776
  (10 shorter events, 0.0 us)
Async XLA Ops:
  0.6 5.6 %copy-start.2 = (s32[4,16,256]{2,1,0:T(8,128)S(1)}, s32[4,16,256]{2,1,0:T(8,128)}, u32[]{:S(2)}) copy-start(s32[4,16,256]{2,1,0:T(8,128)} %walls.9) | copy-start | bytes 196612
  0.6 5.6 %copy-start = (f32[27,4,16,256]{3,2,1,0:T(8,128)S(1)}, f32[27,4,16,256]{3,2,1,0:T(8,128)}, u32[]{:S(2)}) copy-start(f32[27,4,16,256]{3,2,1,0:T(8,128)} %pops.5) | copy-start | bytes 5308420
  0.6 5.6 %copy-start.3 = (f32[4,16,256]{2,1,0:T(8,128)S(1)}, f32[4,16,256]{2,1,0:T(8,128)}, u32[]{:S(2)}) copy-start(f32[4,16,256]{2,1,0:T(8,128)} %omega.5) | copy-start | bytes 196612
  3.0 7.0 %collective-permute-start = (bf16[160,256]{1,0:T(8,128)(2,1)}, bf16[160,256]{1,0:T(8,128)(2,1)S(1)}, u32[]{:S(2)}, u32[]{:S(2)}) collective-permute-start(bf16[160,256]{1,0:T(8,128)(2,1)} %get-tuple-element.33), channel_id=1, source_target_pairs={{0,1},{1,0},{2,3},{3,2},{4,5},{5,4},{6,7},{7,6},{8,9},{9,8},{10,11... | collective-permute-start | bytes 245768 | tf_op jit(solution)/shard_map/ppermute | solution.py:681
  3.5 6.5 %collective-permute-start.1 = (bf16[160,256]{1,0:T(8,128)(2,1)}, bf16[160,256]{1,0:T(8,128)(2,1)S(1)}, u32[]{:S(2)}, u32[]{:S(2)}) collective-permute-start(bf16[160,256]{1,0:T(8,128)(2,1)} %get-tuple-element.34), channel_id=1, source_target_pairs={{0,3},{1,2},{2,1},{3,0},{4,7},{5,6},{6,5},{7,4},{8,11},{9,10},{10,... | collective-permute-start | bytes 245768 | tf_op jit(solution)/shard_map/ppermute | solution.py:681
  6.2 3.9 %copy-start.5 = (bf16[16,256]{1,0:T(8,128)(2,1)S(1)}, bf16[16,256]{1,0:T(8,128)(2,1)}, u32[]{:S(2)}) copy-start(bf16[16,256]{1,0:T(8,128)(2,1)} %get-tuple-element.35.own) | copy-start | bytes 24580
  6.2 3.9 %collective-permute-start.2 = (bf16[16,256]{1,0:T(8,128)(2,1)}, bf16[16,256]{1,0:T(8,128)(2,1)S(1)}, u32[]{:S(2)}, u32[]{:S(2)}) collective-permute-start(bf16[16,256]{1,0:T(8,128)(2,1)} %get-tuple-element.35.own), channel_id=1, source_target_pairs={{0,2},{1,3},{2,0},{3,1},{4,6},{5,7},{6,4},{7,5},{8,10},{9,11},{10,... | collective-permute-start | bytes 24584 | tf_op jit(solution)/shard_map/ppermute | solution.py:699
  6.2 9.3 %copy-start.1 = (bf16[4096,512]{1,0:T(8,128)(2,1)S(1)}, bf16[4096,512]{1,0:T(8,128)(2,1)}, u32[]{:S(2)}) copy-start(bf16[4096,512]{1,0:T(8,128)(2,1)} %radiation.1) | copy-start | bytes 12582916
  7.3 8.3 %copy-start.4 = (s32[128,32]{0,1:T(8,128)S(1)}, s32[128,32]{0,1:T(8,128)}, u32[]{:S(2)}) copy-start(s32[128,32]{0,1:T(8,128)} %param.12) | copy-start | bytes 49156
  7.3 8.3 %copy-start.6 = (s32[1,1,16]{2,1,0:T(1,128)S(1)}, s32[1,1,16]{2,1,0:T(1,128)}, u32[]{:S(2)}) copy-start(s32[1,1,16]{2,1,0:T(1,128)} %patches.1) | copy-start | bytes 196
  7.3 8.3 %copy-start.7 = (s32[1,1,16]{2,1,0:T(1,128)S(1)}, s32[1,1,16]{2,1,0:T(1,128)}, u32[]{:S(2)}) copy-start(s32[1,1,16]{2,1,0:T(1,128)} %sites.1) | copy-start | bytes 196
  10.3 8.9 %collective-permute-start.3 = (bf16[176,256]{1,0:T(8,128)(2,1)S(1)}, bf16[176,256]{1,0:T(8,128)(2,1)S(1)}, u32[]{:S(2)}, u32[]{:S(2)}) collective-permute-start(bf16[176,256]{1,0:T(8,128)(2,1)S(1)} %get-tuple-element.40), channel_id=1, source_target_pairs={{0,28},{4,8},{8,4},{12,16},{16,12},{20,24},{24,20},{28,0},{1,29},{... | collective-permute-start | bytes 270344 | tf_op jit(solution)/shard_map/ppermute | solution.py:681
  14.9 4.6 %collective-permute-start.4 = (bf16[176,256]{1,0:T(8,128)(2,1)S(1)}, bf16[176,256]{1,0:T(8,128)(2,1)S(1)}, u32[]{:S(2)}, u32[]{:S(2)}) collective-permute-start(bf16[176,256]{1,0:T(8,128)(2,1)S(1)} %get-tuple-element.41), channel_id=1, source_target_pairs={{0,4},{4,0},{8,12},{12,8},{16,20},{20,16},{24,28},{28,24},{1,5},{5... | collective-permute-start | bytes 270344 | tf_op jit(solution)/shard_map/ppermute | solution.py:681
  20.4 7.3 %collective-permute-start.5 = (bf16[160,256]{1,0:T(8,128)(2,1)S(1)}, bf16[160,256]{1,0:T(8,128)(2,1)S(1)}, u32[]{:S(2)}, u32[]{:S(2)}) collective-permute-start(bf16[160,256]{1,0:T(8,128)(2,1)S(1)} %get-tuple-element.44), channel_id=1, source_target_pairs={{0,28},{4,8},{8,4},{12,16},{16,12},{20,24},{24,20},{28,0},{1,29},{... | collective-permute-start | bytes 245768 | tf_op jit(solution)/shard_map/ppermute | solution.py:681
  23.1 5.3 %collective-permute-start.6 = (bf16[160,256]{1,0:T(8,128)(2,1)S(1)}, bf16[160,256]{1,0:T(8,128)(2,1)S(1)}, u32[]{:S(2)}, u32[]{:S(2)}) collective-permute-start(bf16[160,256]{1,0:T(8,128)(2,1)S(1)} %get-tuple-element.45), channel_id=1, source_target_pairs={{0,4},{4,0},{8,12},{12,8},{16,20},{20,16},{24,28},{28,24},{1,5},{5... | collective-permute-start | bytes 245768 | tf_op jit(solution)/shard_map/ppermute | solution.py:681
  23.1 4.6 %collective-permute-start.7 = (bf16[16,256]{1,0:T(8,128)(2,1)S(1)}, bf16[16,256]{1,0:T(8,128)(2,1)S(1)}, u32[]{:S(2)}, u32[]{:S(2)}) collective-permute-start(bf16[16,256]{1,0:T(8,128)(2,1)S(1)} %get-tuple-element.58.own), channel_id=1, source_target_pairs={{0,16},{4,20},{8,24},{12,28},{16,0},{20,4},{24,8},{28,12},{1,17},{... | collective-permute-start | bytes 24584 | tf_op jit(solution)/shard_map/ppermute | solution.py:745

commit v7 on v6

--- a/solution.py
+++ b/solution.py
@@ -422,7 +422,7 @@
 
 
 def middle_outer_kernel(
-    ready, omega, walls, retain, solid, far, near, own, _,
+    ready, omega, walls, retain, solid, near, far, own, _,
     main2, halo2, macro, named, send_far, send_near, read, wide,
 ):
     planes, ny, nz = omega.shape
@@ -740,7 +740,7 @@
         relaxed(2) + [(VMEM, (2 * SUB, nz), BF16), *last_faces],
         [pltpu.VMEM((9, 2, ny + SUB, nz), F32), wide],
         cost=1 << 22,
-    )(ready, omega, walls, retain, solid, far, near, named, pick)
+    )(ready, omega, walls, retain, solid, near, far, named, pick)
     far, near = swap(far, near, "gx", size_x)
     across = lax.ppermute(named, "gx", [(i, (i + size_x // 2) % size_x) for i in range(size_x)])
 

time: 44.2 us -> 44.4 us (level)
  starting transfers between devices: 11.1 us -> 11.6 us
    ppermute x3, starting transfers between devices: 0.52 us -> 2.11 us  [swap(): lax.ppermute(near, axis, near_pairs)]
    ppermute x3, starting transfers between devices: 9.94 us -> 9.2 us  [swap(): lax.ppermute(far, axis, far_pairs)]
    ppermute x3, waiting for transfers between devices: 1.07 us -> 0.49 us  [swap(): lax.ppermute(near, axis, near_pairs)]
  transfers between devices with their start and end apart: 8 -> 8, of which waited for: 4 -> 3; matrix products, arithmetic and copies ran while one was open for 0% -> 0% of each run, Pallas kernels for 15% -> 15%
where the time goes in v7:
time: 44.4 us; the launch traced here: 44.2 us
  blocking collectives  13.5 us (30%)
  Pallas kernels  12.1 us (27%)
  starting transfers between devices  11.6 us (26%)
  waiting for transfers between devices  5.54 us (12%)
  between operations  1.45 us (3%)
    all_to_all x1, blocking collectives, per_device(): received = lax.all_to_all(send, ('gx', 'gy'), 0, 0, tiled=True)  13.5 us
    ppermute x3, starting transfers between devices, swap(): lax.ppermute(far, axis, far_pairs)  9.2 us
    ppermute x1, waiting for transfers between devices, per_device(): lax.ppermute(own, 'gy', [(i, (i + size_y // 2) % size_y) for i in range(s...  2.7 us
    pallas_call x1, Pallas kernels, per_device(): call(functools.partial(rows_kernel, size_y), [HBM] * 4, [(VMEM, beside, B...  2.36 us
    ppermute x1, waiting for transfers between devices, per_device(): lax.ppermute(named, 'gx', [(i, (i + size_x // 2) % size_x) for i in range...  2.34 us
    pallas_call x1, Pallas kernels, per_device(): call(functools.partial(slots_kernel, size_y, ride), [VMEM] * 3 + [SMEM] *...  2.21 us
    ppermute x3, starting transfers between devices, swap(): lax.ppermute(near, axis, near_pairs)  2.11 us
    pallas_call x1, Pallas kernels, per_device(): call(last_early_kernel, [VMEM] * 10, [(HBM, block, F32), (VMEM, (2, 9, ny...  1.93 us
  transfers between devices with their start and end apart: 8, of which 3 were waited for; matrix products, arithmetic and copies ran while one was open for 0% of the time, Pallas kernels for 15%

profile of v7, /device:TPU:0, one launch (start us, length us, event | category | flops | bytes accessed | tf_op | source)
XLA Modules:
  0.0 44.2 jit_solution(13839689171358910380)
XLA Ops:
  0.7 2.4 %shard_map.96 = (bf16[160,256]{1,0:T(8,128)(2,1)}, bf16[160,256]{1,0:T(8,128)(2,1)}, bf16[16,256]{1,0:T(8,128)(2,1)}) custom-call(f32[27,4,16,256]{3,2,1,0:T(8,128)} %pops.5, f32[4,16,256]{2,1,0:T(8,128)} %omega.5, s32[4,16,256]{2,1,0:T(8,128)} %walls.9, s32[1,1,16]{2,1,0:T(1,128)} %patches.1), custom_call_target="tpu_custom_call" | custom-call | flops 1048576 | bytes 1048576 | tf_op jit(solution)/shard_map/pallas_call | solution.py:686
  3.0 0.5 %collective-permute-start = (bf16[160,256]{1,0:T(8,128)(2,1)}, bf16[160,256]{1,0:T(8,128)(2,1)S(1)}, u32[]{:S(2)}, u32[]{:S(2)}) collective-permute-start(bf16[160,256]{1,0:T(8,128)(2,1)} %get-tuple-element.33), channel_id=1, source_target_pairs={{0,1},{1,0},{2,3},{3,2},{4,5},{5,4},{6,7},{7,6},{8,9},{9,8},{10,11... | collective-permute-start | bytes 245768 | tf_op jit(solution)/shard_map/ppermute | solution.py:681
  3.5 2.6 %collective-permute-start.1 = (bf16[160,256]{1,0:T(8,128)(2,1)}, bf16[160,256]{1,0:T(8,128)(2,1)S(1)}, u32[]{:S(2)}, u32[]{:S(2)}) collective-permute-start(bf16[160,256]{1,0:T(8,128)(2,1)} %get-tuple-element.34), channel_id=1, source_target_pairs={{0,3},{1,2},{2,1},{3,0},{4,7},{5,6},{6,5},{7,4},{8,11},{9,10},{10,... | collective-permute-start | bytes 245768 | tf_op jit(solution)/shard_map/ppermute | solution.py:681
  6.2 0.1 collective-permute-start.2
  6.2 0.0 copy-done.2
  6.2 0.0 copy-done.3
  6.2 1.1 %shard_map.95.main = f32[27,4,16,256]{3,2,1,0:T(8,128)S(1)} custom-call(f32[27,4,16,256]{3,2,1,0:T(8,128)S(1)} %copy-done, f32[4,16,256]{2,1,0:T(8,128)S(1)} %copy-done.3, s32[4,16,256]{2,1,0:T(8,128)S(1)} %copy-done.2), custom_call_target="tpu_custom_call" | custom-call | flops 4194304 | bytes 4194304 | tf_op jit(solution)/shard_map/pallas_call | solution.py:711
  7.3 0.0 copy-start.4
  7.3 0.0 copy-start.6
  7.3 0.0 copy-start.7
  7.3 2.7 %collective-permute-done.2.across = bf16[16,256]{1,0:T(8,128)(2,1)S(1)} collective-permute-done((bf16[16,256]{1,0:T(8,128)(2,1)}, bf16[16,256]{1,0:T(8,128)(2,1)S(1)}, u32[]{:S(2)}, u32[]{:S(2)}) %collective-permute-start.2) | collective-permute-done | bytes 8224 | tf_op jit(solution)/shard_map/ppermute | solution.py:699
  10.0 0.0 collective-permute-done.near
  10.0 0.0 collective-permute-done.1.far
  10.0 0.0 copy-done.5
  10.0 0.2 shard_map.97
  10.3 1.6 %collective-permute-start.3 = (bf16[176,256]{1,0:T(8,128)(2,1)S(1)}, bf16[176,256]{1,0:T(8,128)(2,1)S(1)}, u32[]{:S(2)}, u32[]{:S(2)}) collective-permute-start(bf16[176,256]{1,0:T(8,128)(2,1)S(1)} %get-tuple-element.40), channel_id=1, source_target_pairs={{0,4},{4,0},{8,12},{12,8},{16,20},{20,16},{24,28},{28,24},{1,5},{5... | collective-permute-start | bytes 270344 | tf_op jit(solution)/shard_map/ppermute | solution.py:681
  11.9 3.5 %collective-permute-start.4 = (bf16[176,256]{1,0:T(8,128)(2,1)S(1)}, bf16[176,256]{1,0:T(8,128)(2,1)S(1)}, u32[]{:S(2)}, u32[]{:S(2)}) collective-permute-start(bf16[176,256]{1,0:T(8,128)(2,1)S(1)} %get-tuple-element.41), channel_id=1, source_target_pairs={{0,28},{4,8},{8,4},{12,16},{16,12},{20,24},{24,20},{28,0},{1,29},{... | collective-permute-start | bytes 270344 | tf_op jit(solution)/shard_map/ppermute | solution.py:681
  16.1 2.2 %shard_map.99 = (bf16[2,16,64]{2,1,0:T(8,128)(2,1)S(1)}, bf16[32,8,128]{2,1,0:T(8,128)(2,1)S(1)}, bf16[128,128]{1,0:T(8,128)(2,1)S(1)}, bf16[512,4096]{1,0:T(8,128)(2,1)S(1)}) custom-call(s32[32,128]{1,0:T(8,128)S(1)} %bitcast.1, bf16[4096,512]{1,0:T(8,128)(2,1)S(1)} %copy-done.1, s32[1,1]{1,0:T(1,128)S(6)} %copy.12.counts, s32[1,1,16]{2,1,0:T(1,128)S(1)} %copy-done.7, ...), custom_call_target="tpu_custom_call" | custom-call | flops 4194304 | bytes 4194304 | tf_op jit(solution)/shard_map/pallas_call | solution.py:700
  18.3 1.3 %shard_map.98 = (f32[27,2,16,256]{3,2,1,0:T(8,128)S(1)}, f32[27,2,8,256]{3,2,1,0:T(8,128)S(1)}, f32[4,2,16,256]{3,2,1,0:T(8,128)S(1)}, f32[27,2,24,256]{3,2,1,0:T(8,128)S(1)}) custom-call(f32[27,4,16,256]{3,2,1,0:T(8,128)S(1)} %shard_map.95.main, f32[27,4,8,256]{3,2,1,0:T(8,128)S(1)} %get-tuple-element.36.halo, f32[27,4,16,256]{3,2,1,0:T(8,128)S(1)} %copy-done, ...), custom_call_target="tpu_custom_call" | custom-call | flops 4194304 | bytes 4194304 | tf_op jit(solution)/shard_map/pallas_call | solution.py:730
  19.6 0.0 collective-permute-done.3.near
  19.7 0.0 collective-permute-done.4.far
  19.7 0.9 %shard_map.100 = (f32[27,2,16,256]{3,2,1,0:T(8,128)S(1)}, f32[27,2,8,256]{3,2,1,0:T(8,128)S(1)}, f32[4,2,16,256]{3,2,1,0:T(8,128)S(1)}, bf16[16,256]{1,0:T(8,128...) custom-call(f32[27,2,24,256]{3,2,1,0:T(8,128)S(1)} %get-tuple-element.39.ready, ...), custom_call_target="tpu_custom_call" | custom-call | flops 4194304 | bytes 4194304 | tf_op jit(solution)/shard_map/pallas_call | solution.py:737
  20.5 3.0 %collective-permute-start.5 = (bf16[160,256]{1,0:T(8,128)(2,1)S(1)}, bf16[160,256]{1,0:T(8,128)(2,1)S(1)}, u32[]{:S(2)}, u32[]{:S(2)}) collective-permute-start(bf16[160,256]{1,0:T(8,128)(2,1)S(1)} %get-tuple-element.44), channel_id=1, source_target_pairs={{0,28},{4,8},{8,4},{12,16},{16,12},{20,24},{24,20},{28,0},{1,29},{... | collective-permute-start | bytes 245768 | tf_op jit(solution)/shard_map/ppermute | solution.py:681
  23.6 0.0 collective-permute-start.6
  23.6 0.3 collective-permute-start.7
  23.8 1.9 %shard_map.101 = (f32[27,4,16,256]{3,2,1,0:T(8,128)}, f32[2,9,16,256]{3,2,1,0:T(8,128)S(1)}, f32[4,2,16,256]{3,2,1,0:T(8,128)S(1)}, f32[4,2,16,256]{3,2,1,0:T(8,128)S(1)}, bf16[32,16,128]{2,1,0:T(8,128)(2,1)S(1)}) custom-call(f32[27,2,16,256]{3,2,1,0:T(8,128)S(1)} %get-tuple-element.46.main_in, f32[27,2,8,256]{3,2,1,0:T(8,128)S(1)} %get-tuple-element.47.halo_in, ...), custom_call_target="tpu_custom_call" | custom-call | flops 4194304 | bytes 4194304 | tf_op jit(solution)/shard_map/pallas_call | solution.py:749
  25.8 2.3 %collective-permute-done.7.across = bf16[16,256]{1,0:T(8,128)(2,1)S(1)} collective-permute-done((bf16[16,256]{1,0:T(8,128)(2,1)S(1)}, bf16[16,256]{1,0:T(8,128)(2,1)S(1)}, u32[]{:S(2)}, u32[]{:S(2)}) %collective-permute-start.7) | collective-permute-done | bytes 8224 | tf_op jit(solution)/shard_map/ppermute | solution.py:745
  28.1 0.0 collective-permute-done.5.far
  28.1 0.5 %collective-permute-done.6.near = bf16[160,256]{1,0:T(8,128)(2,1)S(1)} collective-permute-done((bf16[160,256]{1,0:T(8,128)(2,1)S(1)}, bf16[160,256]{1,0:T(8,128)(2,1)S(1)}, u32[]{:S(2)}, u32[]{:S(2)}) %collective-permute-start.6) | collective-permute-done | bytes 81952 | tf_op jit(solution)/shard_map/ppermute | solution.py:681
  28.6 1.0 %shard_map.102 = (f32[27,4,16,256]{3,2,1,0:T(8,128)}, bf16[32,32,128]{2,1,0:T(8,128)(2,1)S(1)}, f32[8,256]{1,0:T(8,128)S(1)}) custom-call(bf16[160,256]{1,0:T(8,128)(2,1)S(1)} %collective-permute-done.5.far, bf16[160,256]{1,0:T(8,128)(2,1)S(1)} %collective-permute-done.6.near, s32[4,16,256]{2,1,0:T(8,128)S(1)} %copy-done.2, ...), custom_call_target="tpu_custom_call", output_to_operand_aliasing={{0}: (12, {})} | custom-call | flops 4194304 | bytes 4194304 | tf_op jit(solution)/shard_map/pallas_call | solution.py:763
  29.6 13.5 %all_to_all.5.received = bf16[32,32,128]{2,1,0:T(8,128)(2,1)S(1)} all-to-all(bf16[32,32,128]{2,1,0:T(8,128)(2,1)S(1)} %get-tuple-element.61), channel_id=1, replica_groups=mesh['gx'=8,'gy'=4] {'gx','gy'}, dimensions={0} | all-to-all | bytes 524288 | tf_op jit(solution)/shard_map/all_to_all | solution.py:771
  43.1 1.1 %shard_map.103 = f32[128,128]{1,0:T(8,128)} custom-call(bf16[32,32,128]{2,1,0:T(8,128)(2,1)S(1)} %all_to_all.5.received, f32[8,256]{1,0:T(8,128)S(1)} %get-tuple-element.62.named, bf16[128,128]{1,0:T(8,128)(2,1)S(1)} %get-tuple-element.63.own_bins), custom_call_target="tpu_custom_call" | custom-call | flops 1048576 | bytes 1048576 | tf_op jit(solution)/shard_map/pallas_call | solution.py:776
  (10 shorter events, 0.0 us)
Async XLA Ops:
  0.6 5.6 %copy-start.2 = (s32[4,16,256]{2,1,0:T(8,128)S(1)}, s32[4,16,256]{2,1,0:T(8,128)}, u32[]{:S(2)}) copy-start(s32[4,16,256]{2,1,0:T(8,128)} %walls.9) | copy-start | bytes 196612
  0.6 5.6 %copy-start = (f32[27,4,16,256]{3,2,1,0:T(8,128)S(1)}, f32[27,4,16,256]{3,2,1,0:T(8,128)}, u32[]{:S(2)}) copy-start(f32[27,4,16,256]{3,2,1,0:T(8,128)} %pops.5) | copy-start | bytes 5308420
  0.6 5.6 %copy-start.3 = (f32[4,16,256]{2,1,0:T(8,128)S(1)}, f32[4,16,256]{2,1,0:T(8,128)}, u32[]{:S(2)}) copy-start(f32[4,16,256]{2,1,0:T(8,128)} %omega.5) | copy-start | bytes 196612
  3.0 7.0 %collective-permute-start = (bf16[160,256]{1,0:T(8,128)(2,1)}, bf16[160,256]{1,0:T(8,128)(2,1)S(1)}, u32[]{:S(2)}, u32[]{:S(2)}) collective-permute-start(bf16[160,256]{1,0:T(8,128)(2,1)} %get-tuple-element.33), channel_id=1, source_target_pairs={{0,1},{1,0},{2,3},{3,2},{4,5},{5,4},{6,7},{7,6},{8,9},{9,8},{10,11... | collective-permute-start | bytes 245768 | tf_op jit(solution)/shard_map/ppermute | solution.py:681
  3.5 6.5 %collective-permute-start.1 = (bf16[160,256]{1,0:T(8,128)(2,1)}, bf16[160,256]{1,0:T(8,128)(2,1)S(1)}, u32[]{:S(2)}, u32[]{:S(2)}) collective-permute-start(bf16[160,256]{1,0:T(8,128)(2,1)} %get-tuple-element.34), channel_id=1, source_target_pairs={{0,3},{1,2},{2,1},{3,0},{4,7},{5,6},{6,5},{7,4},{8,11},{9,10},{10,... | collective-permute-start | bytes 245768 | tf_op jit(solution)/shard_map/ppermute | solution.py:681
  6.2 3.9 %copy-start.5 = (bf16[16,256]{1,0:T(8,128)(2,1)S(1)}, bf16[16,256]{1,0:T(8,128)(2,1)}, u32[]{:S(2)}) copy-start(bf16[16,256]{1,0:T(8,128)(2,1)} %get-tuple-element.35.own) | copy-start | bytes 24580
  6.2 3.9 %collective-permute-start.2 = (bf16[16,256]{1,0:T(8,128)(2,1)}, bf16[16,256]{1,0:T(8,128)(2,1)S(1)}, u32[]{:S(2)}, u32[]{:S(2)}) collective-permute-start(bf16[16,256]{1,0:T(8,128)(2,1)} %get-tuple-element.35.own), channel_id=1, source_target_pairs={{0,2},{1,3},{2,0},{3,1},{4,6},{5,7},{6,4},{7,5},{8,10},{9,11},{10,... | collective-permute-start | bytes 24584 | tf_op jit(solution)/shard_map/ppermute | solution.py:699
  6.2 9.8 %copy-start.1 = (bf16[4096,512]{1,0:T(8,128)(2,1)S(1)}, bf16[4096,512]{1,0:T(8,128)(2,1)}, u32[]{:S(2)}) copy-start(bf16[4096,512]{1,0:T(8,128)(2,1)} %radiation.1) | copy-start | bytes 12582916
  7.3 8.8 %copy-start.4 = (s32[128,32]{0,1:T(8,128)S(1)}, s32[128,32]{0,1:T(8,128)}, u32[]{:S(2)}) copy-start(s32[128,32]{0,1:T(8,128)} %param.12) | copy-start | bytes 49156
  7.3 8.8 %copy-start.6 = (s32[1,1,16]{2,1,0:T(1,128)S(1)}, s32[1,1,16]{2,1,0:T(1,128)}, u32[]{:S(2)}) copy-start(s32[1,1,16]{2,1,0:T(1,128)} %patches.1) | copy-start | bytes 196
  7.3 8.8 %copy-start.7 = (s32[1,1,16]{2,1,0:T(1,128)S(1)}, s32[1,1,16]{2,1,0:T(1,128)}, u32[]{:S(2)}) copy-start(s32[1,1,16]{2,1,0:T(1,128)} %sites.1) | copy-start | bytes 196
  10.3 9.4 %collective-permute-start.3 = (bf16[176,256]{1,0:T(8,128)(2,1)S(1)}, bf16[176,256]{1,0:T(8,128)(2,1)S(1)}, u32[]{:S(2)}, u32[]{:S(2)}) collective-permute-start(bf16[176,256]{1,0:T(8,128)(2,1)S(1)} %get-tuple-element.40), channel_id=1, source_target_pairs={{0,4},{4,0},{8,12},{12,8},{16,20},{20,16},{24,28},{28,24},{1,5},{5... | collective-permute-start | bytes 270344 | tf_op jit(solution)/shard_map/ppermute | solution.py:681
  11.9 7.8 %collective-permute-start.4 = (bf16[176,256]{1,0:T(8,128)(2,1)S(1)}, bf16[176,256]{1,0:T(8,128)(2,1)S(1)}, u32[]{:S(2)}, u32[]{:S(2)}) collective-permute-start(bf16[176,256]{1,0:T(8,128)(2,1)S(1)} %get-tuple-element.41), channel_id=1, source_target_pairs={{0,28},{4,8},{8,4},{12,16},{16,12},{20,24},{24,20},{28,0},{1,29},{... | collective-permute-start | bytes 270344 | tf_op jit(solution)/shard_map/ppermute | solution.py:681
  20.5 7.6 %collective-permute-start.5 = (bf16[160,256]{1,0:T(8,128)(2,1)S(1)}, bf16[160,256]{1,0:T(8,128)(2,1)S(1)}, u32[]{:S(2)}, u32[]{:S(2)}) collective-permute-start(bf16[160,256]{1,0:T(8,128)(2,1)S(1)} %get-tuple-element.44), channel_id=1, source_target_pairs={{0,28},{4,8},{8,4},{12,16},{16,12},{20,24},{24,20},{28,0},{1,29},{... | collective-permute-start | bytes 245768 | tf_op jit(solution)/shard_map/ppermute | solution.py:681
  23.6 5.0 %collective-permute-start.6 = (bf16[160,256]{1,0:T(8,128)(2,1)S(1)}, bf16[160,256]{1,0:T(8,128)(2,1)S(1)}, u32[]{:S(2)}, u32[]{:S(2)}) collective-permute-start(bf16[160,256]{1,0:T(8,128)(2,1)S(1)} %get-tuple-element.45), channel_id=1, source_target_pairs={{0,4},{4,0},{8,12},{12,8},{16,20},{20,16},{24,28},{28,24},{1,5},{5... | collective-permute-start | bytes 245768 | tf_op jit(solution)/shard_map/ppermute | solution.py:681
  23.6 4.5 %collective-permute-start.7 = (bf16[16,256]{1,0:T(8,128)(2,1)S(1)}, bf16[16,256]{1,0:T(8,128)(2,1)S(1)}, u32[]{:S(2)}, u32[]{:S(2)}) collective-permute-start(bf16[16,256]{1,0:T(8,128)(2,1)S(1)} %get-tuple-element.58.own), channel_id=1, source_target_pairs={{0,16},{4,20},{8,24},{12,28},{16,0},{20,4},{24,8},{28,12},{1,17},{... | collective-permute-start | bytes 24584 | tf_op jit(solution)/shard_map/ppermute | solution.py:745
